TPU v7x, 32 devices: a whole 2x2x4 slice. The times are simulated.
32 devices in a mesh: dp: 4 (over z), fsdp: 8 (over y, x, core).
Axes of the slice: x: 2, y: 2, z: 4, core: 2. Of those that a mesh axis runs over, the one named last changes fastest.
Arguments:
- inputs: bfloat16 [128, 256, 512], P(('dp', 'fsdp')), may hold values from -6 to 6
- memory: bfloat16 [128, 512, 512], P(('dp', 'fsdp'))
- cotangent: bfloat16 [128, 256, 512], P(('dp', 'fsdp')), may hold values from -6 to 6
- lengths: int32 [128], P(('dp', 'fsdp')), may hold values from 32 to 256
- mem_lengths: int32 [128], P(('dp', 'fsdp')), may hold values from 64 to 512
- attn_weights: float32 [8, 512, 512], P(None, ('dp', 'fsdp'))
- ffn_in: float32 [512, 2048], P(('dp', 'fsdp')), may hold values from -0.25 to 0.25
- ffn_out: float32 [2048, 512], P(('dp', 'fsdp')), may hold values from -0.125 to 0.125
- vectors: float32 [17, 512], P(None, ('dp', 'fsdp'))
- attn_first: float32 [8, 512, 512], P(None, ('dp', 'fsdp')), may hold values from -0.0029296875 to 0.0029296875
- attn_second: float32 [8, 512, 512], P(None, ('dp', 'fsdp')), may hold values from 2.3792484e-07 to 9.5169935e-07
- ffn_in_first: float32 [512, 2048], P(('dp', 'fsdp')), may hold values from -0.0029296875 to 0.0029296875
- ffn_in_second: float32 [512, 2048], P(('dp', 'fsdp')), may hold values from 2.855098e-08 to 1.1896242e-07
- ffn_out_first: float32 [2048, 512], P(('dp', 'fsdp')), may hold values from -0.0029296875 to 0.0029296875
- ffn_out_second: float32 [2048, 512], P(('dp', 'fsdp')), may hold values from 2.3792484e-07 to 9.5169935e-07
- vector_first: float32 [17, 512], P(None, ('dp', 'fsdp')), may hold values from -0.0029296875 to 0.0029296875
- vector_second: float32 [17, 512], P(None, ('dp', 'fsdp')), may hold values from 2.3792484e-07 to 9.5169935e-07
Outputs:
- output: float32 [128, 256, 512], P(('dp', 'fsdp'))
- input_grad: float32 [128, 256, 512], P(('dp', 'fsdp'))
- memory_grad: float32 [128, 512, 512], P(('dp', 'fsdp'))
- grad_norm: float32 [1], replicated
- new_attn_weights: float32 [8, 512, 512], P(None, ('dp', 'fsdp'))
- new_attn_first: float32 [8, 512, 512], P(None, ('dp', 'fsdp'))
- new_attn_second: float32 [8, 512, 512], P(None, ('dp', 'fsdp'))
- new_ffn_in: float32 [512, 2048], P(('dp', 'fsdp'))
- new_ffn_in_first: float32 [512, 2048], P(('dp', 'fsdp'))
- new_ffn_in_second: float32 [512, 2048], P(('dp', 'fsdp'))
- new_ffn_out: float32 [2048, 512], P(('dp', 'fsdp'))
- new_ffn_out_first: float32 [2048, 512], P(('dp', 'fsdp'))
- new_ffn_out_second: float32 [2048, 512], P(('dp', 'fsdp'))
- new_vectors: float32 [17, 512], P(None, ('dp', 'fsdp'))
- new_vector_first: float32 [17, 512], P(None, ('dp', 'fsdp'))
- new_vector_second: float32 [17, 512], P(None, ('dp', 'fsdp'))
Inputs may be any that keep to these rules, and one draw needn't show every extreme that they name: `lengths`: positions at or past a sequence's length are padding. `mem_lengths`: memory positions at or past this length are padding.
All inputs are finite; a program needn't handle non-finite values.
Results may differ from a plain program's by a relative error of at most 0.018.
The roundings to bfloat16 on the way count: a program that leaves them out, or rounds other values in their place, can miss the bound.
Values may be sent and summed in bfloat16 or wider, within the bound.
No kernel may reach another device: no remote copies, remote signals or barrier semaphores. Data moves between devices by JAX's collectives and lax.ppermute only.
A program may use at most 192 MiB of HBM per device.

v0:
```python
from functools import partial

import jax
import jax.numpy as jnp
from jax import lax
from jax.sharding import PartitionSpec as P

HEADS = 8
HEAD_DIM = 64
STEP = 5


def layer_norm(values, gain, shift):
    center = values - jnp.mean(values, -1, keepdims=True)
    spread = jnp.mean(center * center, -1, keepdims=True)
    return center * lax.rsqrt(spread + 1e-05) * (1.0 + gain) + shift


def plain_dot(left, right):
    return jnp.dot(left, right, preferred_element_type=jnp.float32)


def left_dot(left, right):
    return lax.dot_general(
        left, right, (((0,), (0,)), ((), ())), preferred_element_type=jnp.float32
    )


def right_dot(left, right):
    return lax.dot_general(
        left, right, (((1,), (1,)), ((), ())), preferred_element_type=jnp.float32
    )


def column_sum(values):
    return jnp.sum(values.astype(jnp.float32), 0)


def score_block(queries, keys, mask):
    scores = jnp.einsum(
        "sqhe,skhe->shqk", queries, keys, preferred_element_type=jnp.float32
    ) * HEAD_DIM ** (-0.5)
    return jnp.where(mask, scores, -1e30)


def attend_forward(queries, keys, values, mask):
    scores = score_block(queries, keys, mask)
    top = jnp.max(scores, -1, keepdims=True)
    expo = jnp.exp(scores - top)
    total = jnp.sum(expo, -1, keepdims=True)
    probs = (expo / total).astype(jnp.bfloat16)
    mixed = jnp.einsum("shqk,skhe->sqhe", probs, values, preferred_element_type=jnp.float32)
    return (mixed, top + jnp.log(total))


def attend_backward(queries, keys, values, mask, logsum, grad_mixed):
    scores = score_block(queries, keys, mask)
    probs = jnp.exp(scores - logsum)
    grad_probs = jnp.einsum(
        "sqhe,skhe->shqk", grad_mixed, values, preferred_element_type=jnp.float32
    )
    inner = jnp.sum(probs * grad_probs, -1, keepdims=True)
    grad_scores = (probs * (grad_probs - inner)).astype(jnp.bfloat16)
    scale = HEAD_DIM ** (-0.5)
    grad_query = (
        jnp.einsum("shqk,skhe->sqhe", grad_scores, keys, preferred_element_type=jnp.float32) * scale
    )
    grad_key = (
        jnp.einsum("shqk,sqhe->skhe", grad_scores, queries, preferred_element_type=jnp.float32)
        * scale
    )
    grad_value = jnp.einsum(
        "shqk,sqhe->skhe",
        probs.astype(jnp.bfloat16),
        grad_mixed,
        preferred_element_type=jnp.float32,
    )
    return (grad_query, grad_key, grad_value)


def adam_update(weight, grad, first, second, clip_scale, step, rate):
    clipped = grad * clip_scale
    first_new = 0.5 * first + 0.5 * clipped
    second_new = 0.55 * second + 0.45 * clipped * clipped
    fix_first = 1.0 - jnp.power(0.5, step)
    fix_second = 1.0 - jnp.power(0.55, step)
    weight_new = weight - rate * (
        first_new / fix_first / (jnp.sqrt(second_new / fix_second) + 1e-08) + 0.01 * weight
    )
    return (weight_new, first_new, second_new)


def local(
    inputs,
    memory,
    cotangent,
    lengths,
    mem_lengths,
    attn_weights,
    ffn_in,
    ffn_out,
    vectors,
    attn_first,
    attn_second,
    ffn_in_first,
    ffn_in_second,
    ffn_out_first,
    ffn_out_second,
    vector_first,
    vector_second,
):
    copies = (
        attn_weights.astype(jnp.bfloat16),
        ffn_in.astype(jnp.bfloat16),
        ffn_out.astype(jnp.bfloat16),
        vectors.astype(jnp.bfloat16),
    )
    attn_full, ffn_in_full, ffn_out_full, table_full = (
        lax.all_gather(copies[0], ("dp", "fsdp"), axis=1, tiled=True),
        lax.all_gather(copies[1], ("dp", "fsdp"), axis=0, tiled=True),
        lax.all_gather(copies[2], ("dp", "fsdp"), axis=0, tiled=True),
        lax.all_gather(copies[3], ("dp", "fsdp"), axis=1, tiled=True),
    )
    table = table_full.astype(jnp.float32)
    seqs, length, width = inputs.shape
    mem_len = memory.shape[1]
    tokens = seqs * length
    positions = jnp.arange(length)
    valid = positions[None, :] < lengths[:, None]
    self_mask = (positions[:, None] >= positions[None, :])[None, None] & valid[:, None, None, :]
    cross_mask = (jnp.arange(mem_len)[None, :] < mem_lengths[:, None])[:, None, None, :]

    def split_heads(flat, rows):
        return flat.reshape(seqs, rows, HEADS, HEAD_DIM)

    def join_heads(grid):
        return grid.reshape(-1, width)

    resid = inputs.astype(jnp.float32).reshape(tokens, width)
    mem_flat = memory.reshape(seqs * mem_len, width)
    normed_one, norm_one_back = jax.vjp(layer_norm, resid, table[0], table[1])
    act_one = normed_one.astype(jnp.bfloat16)
    query_self = (plain_dot(act_one, attn_full[0]) + table[6]).astype(jnp.bfloat16)
    key_self = plain_dot(act_one, attn_full[1]).astype(jnp.bfloat16)
    value_self = (plain_dot(act_one, attn_full[2]) + table[7]).astype(jnp.bfloat16)
    mixed_self, logsum_self = attend_forward(
        split_heads(query_self, length),
        split_heads(key_self, length),
        split_heads(value_self, length),
        self_mask,
    )
    mixed_self = join_heads(mixed_self).astype(jnp.bfloat16)
    resid_one = resid + plain_dot(mixed_self, attn_full[3]) + table[8]
    normed_two, norm_two_back = jax.vjp(layer_norm, resid_one, table[2], table[3])
    act_two = normed_two.astype(jnp.bfloat16)
    query_cross = (plain_dot(act_two, attn_full[4]) + table[9]).astype(jnp.bfloat16)
    key_cross = plain_dot(mem_flat, attn_full[5]).astype(jnp.bfloat16)
    value_cross = (plain_dot(mem_flat, attn_full[6]) + table[10]).astype(jnp.bfloat16)
    mixed_cross, logsum_cross = attend_forward(
        split_heads(query_cross, length),
        split_heads(key_cross, mem_len),
        split_heads(value_cross, mem_len),
        cross_mask,
    )
    mixed_cross = join_heads(mixed_cross).astype(jnp.bfloat16)
    resid_two = resid_one + plain_dot(mixed_cross, attn_full[7]) + table[11]
    normed_three, norm_three_back = jax.vjp(layer_norm, resid_two, table[4], table[5])
    act_three = normed_three.astype(jnp.bfloat16)
    hidden_pre = plain_dot(act_three, ffn_in_full) + table[13:].reshape(-1)
    hidden, gelu_back = jax.vjp(partial(jax.nn.gelu, approximate=False), hidden_pre)
    hidden_low = hidden.astype(jnp.bfloat16)
    output = resid_two + plain_dot(hidden_low, ffn_out_full) + table[12]
    attn_back, ffn_in_back, ffn_out_back = (
        lax.all_gather(copies[0], ("dp", "fsdp"), axis=1, tiled=True),
        lax.all_gather(copies[1], ("dp", "fsdp"), axis=0, tiled=True),
        lax.all_gather(copies[2], ("dp", "fsdp"), axis=0, tiled=True),
    )
    grad_out = cotangent.astype(jnp.float32).reshape(tokens, width) * valid.reshape(tokens)[
        :, None
    ].astype(jnp.float32)
    grad_branch = grad_out.astype(jnp.bfloat16)
    grad_ffn_out = left_dot(hidden_low, grad_branch)
    grad_out_bias = column_sum(grad_branch)
    grad_hidden = right_dot(grad_branch, ffn_out_back)
    grad_pre = gelu_back(grad_hidden)[0].astype(jnp.bfloat16)
    grad_ffn_in = left_dot(act_three, grad_pre)
    grad_in_bias = column_sum(grad_pre)
    back_three = norm_three_back(right_dot(grad_pre, ffn_in_back))
    grad_two = grad_out + back_three[0]
    branch_two = grad_two.astype(jnp.bfloat16)
    grad_wo_cross = left_dot(mixed_cross, branch_two)
    grad_bo_cross = column_sum(branch_two)
    grad_mixed_cross = right_dot(branch_two, attn_back[7]).astype(jnp.bfloat16)
    cross_grads = attend_backward(
        split_heads(query_cross, length),
        split_heads(key_cross, mem_len),
        split_heads(value_cross, mem_len),
        cross_mask,
        logsum_cross,
        split_heads(grad_mixed_cross, length),
    )
    grad_query_cross = join_heads(cross_grads[0]).astype(jnp.bfloat16)
    grad_key_cross = join_heads(cross_grads[1]).astype(jnp.bfloat16)
    grad_value_cross = join_heads(cross_grads[2]).astype(jnp.bfloat16)
    grad_wq_cross = left_dot(act_two, grad_query_cross)
    grad_bq_cross = column_sum(grad_query_cross)
    grad_wk_cross = left_dot(mem_flat, grad_key_cross)
    grad_wv_cross = left_dot(mem_flat, grad_value_cross)
    grad_bv_cross = column_sum(grad_value_cross)
    grad_memory = right_dot(grad_key_cross, attn_back[5]) + right_dot(
        grad_value_cross, attn_back[6]
    )
    back_two = norm_two_back(right_dot(grad_query_cross, attn_back[4]))
    grad_one = grad_two + back_two[0]
    grad_cross_stack = jnp.stack([grad_wq_cross, grad_wk_cross, grad_wv_cross, grad_wo_cross])
    branch_one = grad_one.astype(jnp.bfloat16)
    grad_wo_self = left_dot(mixed_self, branch_one)
    grad_bo_self = column_sum(branch_one)
    grad_mixed_self = right_dot(branch_one, attn_back[3]).astype(jnp.bfloat16)
    self_grads = attend_backward(
        split_heads(query_self, length),
        split_heads(key_self, length),
        split_heads(value_self, length),
        self_mask,
        logsum_self,
        split_heads(grad_mixed_self, length),
    )
    grad_query_self = join_heads(self_grads[0]).astype(jnp.bfloat16)
    grad_key_self = join_heads(self_grads[1]).astype(jnp.bfloat16)
    grad_value_self = join_heads(self_grads[2]).astype(jnp.bfloat16)
    grad_wq_self = left_dot(act_one, grad_query_self)
    grad_wk_self = left_dot(act_one, grad_key_self)
    grad_wv_self = left_dot(act_one, grad_value_self)
    grad_bq_self = column_sum(grad_query_self)
    grad_bv_self = column_sum(grad_value_self)
    grad_act_one = (
        right_dot(grad_query_self, attn_back[0])
        + right_dot(grad_key_self, attn_back[1])
        + right_dot(grad_value_self, attn_back[2])
    )
    back_one = norm_one_back(grad_act_one)
    grad_input = grad_one + back_one[0]
    grad_self_stack = jnp.stack([grad_wq_self, grad_wk_self, grad_wv_self, grad_wo_self])
    small_rows = jnp.stack(
        [
            back_one[1],
            back_one[2],
            back_two[1],
            back_two[2],
            back_three[1],
            back_three[2],
            grad_bq_self,
            grad_bv_self,
            grad_bo_self,
            grad_bq_cross,
            grad_bv_cross,
            grad_bo_cross,
            grad_out_bias,
        ]
    )
    grad_table = jnp.concatenate([small_rows, grad_in_bias.reshape(-1, width)], 0)
    grad_attn = jnp.concatenate([grad_self_stack, grad_cross_stack], 0)
    shares = (
        lax.psum_scatter(grad_attn, ("dp", "fsdp"), scatter_dimension=1, tiled=True),
        lax.psum_scatter(grad_ffn_in, ("dp", "fsdp"), scatter_dimension=0, tiled=True),
        lax.psum_scatter(grad_ffn_out, ("dp", "fsdp"), scatter_dimension=0, tiled=True),
        lax.psum_scatter(grad_table, ("dp", "fsdp"), scatter_dimension=1, tiled=True),
    )
    local_squares = (
        jnp.sum(shares[0] * shares[0])
        + jnp.sum(shares[1] * shares[1])
        + jnp.sum(shares[2] * shares[2])
        + jnp.sum(shares[3] * shares[3])
    )
    total_squares = lax.psum(local_squares, ("dp", "fsdp"))
    grad_norm = jnp.sqrt(total_squares)
    clip_scale = jnp.minimum(1.0, 1.0 / (grad_norm + 1e-06))
    step = jnp.float32(STEP)
    attn_new = adam_update(attn_weights, shares[0], attn_first, attn_second, clip_scale, step, 0.04)
    first_new = adam_update(ffn_in, shares[1], ffn_in_first, ffn_in_second, clip_scale, step, 0.04)
    second_new = adam_update(
        ffn_out, shares[2], ffn_out_first, ffn_out_second, clip_scale, step, 0.04
    )
    table_new = adam_update(vectors, shares[3], vector_first, vector_second, clip_scale, step, 0.25)
    return (
        output.reshape(seqs, length, width),
        grad_input.reshape(seqs, length, width),
        grad_memory.reshape(seqs, mem_len, width),
        grad_norm.reshape(1),
        attn_new[0],
        attn_new[1],
        attn_new[2],
        first_new[0],
        first_new[1],
        first_new[2],
        second_new[0],
        second_new[1],
        second_new[2],
        table_new[0],
        table_new[1],
        table_new[2],
    )


def solution(mesh):
    return jax.shard_map(
        local,
        mesh=mesh,
        in_specs=(
            P(("dp", "fsdp"), None, None),
            P(("dp", "fsdp"), None, None),
            P(("dp", "fsdp"), None, None),
            P(("dp", "fsdp")),
            P(("dp", "fsdp")),
            P(None, ("dp", "fsdp"), None),
            P(("dp", "fsdp"), None),
            P(("dp", "fsdp"), None),
            P(None, ("dp", "fsdp")),
            P(None, ("dp", "fsdp"), None),
            P(None, ("dp", "fsdp"), None),
            P(("dp", "fsdp"), None),
            P(("dp", "fsdp"), None),
            P(("dp", "fsdp"), None),
            P(("dp", "fsdp"), None),
            P(None, ("dp", "fsdp")),
            P(None, ("dp", "fsdp")),
        ),
        out_specs=(
            P(("dp", "fsdp"), None, None),
            P(("dp", "fsdp"), None, None),
            P(("dp", "fsdp"), None, None),
            P(),
            P(None, ("dp", "fsdp"), None),
            P(None, ("dp", "fsdp"), None),
            P(None, ("dp", "fsdp"), None),
            P(("dp", "fsdp"), None),
            P(("dp", "fsdp"), None),
            P(("dp", "fsdp"), None),
            P(("dp", "fsdp"), None),
            P(("dp", "fsdp"), None),
            P(("dp", "fsdp"), None),
            P(None, ("dp", "fsdp")),
            P(None, ("dp", "fsdp")),
            P(None, ("dp", "fsdp")),
        ),
        check_vma=False,
    )
```

profile of v0, /device:TPU:0, one launch (start us, length us, event | category | flops | bytes accessed | tf_op | source)
XLA Modules:
  0.0 926.9 jit_solution(15040983730191304902)
XLA Ops:
  13.1 43.6 %all_gather.15 = bf16[17,512]{0,1:T(8,128)(2,1)S(1)} all-gather(bf16[17,16]{0,1:T(8,128)(2,1)S(1)} %convert_element_type.229), channel_id=1, replica_groups=mesh['dp'=4,'fsdp'=8] {'dp','fsdp'}, dimensions={1}, use_global_device_ids=true | all-gather | bytes 17952 | tf_op jit(solution)/shard_map/all_gather | solution.py:122
  63.7 2.3 slice_reduce_fusion
  66.0 2.1 convert_reduce_fusion.3
  71.1 5.0 all-gather.4.cloned.1.call-done
  76.1 3.0 add_convert_fusion.6
  79.1 4.2 reshape.487
  83.3 3.0 copy.152
  86.3 3.0 add_convert_fusion.5
  89.3 3.9 reshape.488
  93.2 3.0 copy.150
  96.3 3.0 convolution_convert_fusion.3
  99.3 3.9 reshape.489
  103.2 3.0 copy.151
  106.2 3.6 add_convert_fusion.1
  109.8 6.1 reshape.490
  115.9 5.7 copy.160
  121.6 3.6 convolution_convert_fusion
  125.2 6.1 reshape.492
  131.4 6.0 copy.159
  137.4 3.1 fusion.88
  146.3 2.3 fusion.89
  151.7 2.1 reshape.491
  153.8 2.2 copy.158
  156.0 4.7 fusion.90
  160.7 4.1 fusion
  164.9 2.2 copy-done.1
  167.1 5.9 fusion.40
  178.3 24.5 %multiply_convert_fusion.2 = (bf16[1024,2048]{1,0:T(8,128)(2,1)}, f32[1024,2048]{1,0:T(8,128)}, f32[1024,2048]{1,0:T(8,128)}) fusion(f32[2048]{0:T(1024)S(1)} %bitcast.310, bf16[512,2048]{1,0:T(8,128)(2,1)} %all-gather.6.cloned.1.call-done, f32[1024,512]{1,0:T(8,128)} %copy-done.4, f32[512]{0:T(512)S(1)} %get-tuple-element.59, ...), kind=kOutput, calls=%fused_computation.17 | convolution fusion | flops 2288517120 | bytes 25186304 | tf_op jit(solution)/shard_map/dot_general | solution.py:20
  202.8 9.4 %convert_reduce_fusion = (f32[2048]{0:T(1024)S(1)}, bf16[1024,2048]{1,0:T(8,128)(2,1)S(1)}) fusion(f32[1024,2048]{1,0:T(8,128)} %get-tuple-element.92, bf16[1024,512]{1,0:T(8,128)(2,1)S(1)} %copy-done.47, bf16[2048,512]{1,0:T(8,128)(2,1)} %all-gather.8.cloned.1.call-done, f32[1024,2048]{1,0:T(8,128)} %get-tuple-element.110, f32[2048]{0:T(1024)S(1)} %bitcast.311), kind=kOutput, calls=%fused_computation.11 | convolution fusion | flops 2183133184 | bytes 24133632 | tf_op jit(solution)/shard_map/dot_general | solution.py:30
  212.3 2.9 multiply_reduce_fusion.2
  220.6 2.1 reshape.493
  222.7 2.2 copy.164
  224.9 8.5 convert_reduce_fusion.1
  233.4 11.8 %multiply_reduce_fusion = (f32[4,8,256]{2,1,0:T(8,128)S(1)}, f32[4,8,256,512]{3,2,1,0:T(8,128)}) fusion(f32[4,8,256,512]{3,2,1,0:T(8,128)} %copy-done.1, f32[4,8,256]{2,1,0:T(8,128)S(1)} %log_add_fusion.1, bf16[4,256,8,64]{1,3,2,0:T(8,128)(2,1)S(1)} %copy.164, bf16[4,512,8,64]{1,3,2,0:T(8,128)(2,1)S(1)} %copy-done.25), kind=kOutput, calls=%fused_computation.1 | convolution fusion | flops 549445632 | bytes 36765696 | tf_op jit(solution)/shard_map/sqhe,skhe->shqk/dot_general | solution.py:59
  245.2 12.3 %multiply_convert_fusion = bf16[4,8,256,512]{3,2,1,0:T(8,128)(2,1)S(1)} fusion(f32[4,8,256,512]{3,2,1,0:T(8,128)} %get-tuple-element.113, f32[4,8,256,512]{3,2,1,0:T(8,128)} %copy-done.1, f32[4,8,256]{2,1,0:T(8,128)S(1)} %get-tuple-element.112, f32[4,8,256]{2,1,0:T(8,128)S(1)} %log_add_fusion.1), kind=kLoop, calls=%fused_computation | loop fusion | flops 16777216 | bytes 42008576 | tf_op jit(solution)/shard_map/convert_element_type | solution.py:63
  257.6 2.7 convert_reduce_fusion.5
  262.4 2.4 multiply_reduce_fusion.3
  270.4 2.1 reshape.494
  272.5 2.2 copy.169
  274.8 5.9 convert_reduce_fusion.7
  280.7 5.6 multiply_reduce_fusion.1
  286.3 2.1 multiply_convert_fusion.1
  288.5 2.4 fusion.47
  290.8 1.9 convert_reduce_fusion.8
  295.1 2.0 copy.176
  298.5 2.2 fusion.57
  302.6 2.4 fusion.79
  308.6 6.8 fusion.92
  315.6 7.3 fusion.77
  323.2 3.3 copy.183
  327.1 5.7 fusion.34
  342.2 2.1 fusion.51
  344.3 2.3 fusion.50
  346.7 2.6 fusion.49
  351.6 3.2 fusion.60
  354.8 4.6 convolution_add_fusion
  359.4 3.7 add_add_fusion.7
  363.1 77.6 %reduce-scatter.13.cloned.1.call-done = f32[16,17]{1,0:T(8,128)} async-done(((f32[512,17]{1,0:T(8,128)}), f32[16,17]{1,0:T(8,128)}) %reduce-scatter.13.cloned.1.call-update) | async-done | bytes 1104
  442.1 137.6 %reduce-scatter.11.cloned.1.call-done = f32[64,512]{1,0:T(8,128)} async-done(((f32[2048,512]{1,0:T(8,128)}), f32[64,512]{1,0:T(8,128)}) %reduce-scatter.11.cloned.1.call-update) | async-done | bytes 131088 | tf_op jit(solution)/shard_map/reduce_scatter | solution.py:266
  581.2 137.4 %reduce-scatter.9.cloned.1.call-done = f32[16,2048]{1,0:T(8,128)} async-done(((f32[512,2048]{1,0:T(8,128)}), f32[16,2048]{1,0:T(8,128)}) %reduce-scatter.9.cloned.1.call-update) | async-done | bytes 131088 | tf_op jit(solution)/shard_map/reduce_scatter | solution.py:265
  720.1 145.4 %reduce-scatter.7.cloned.1.call-done = f32[8,16,512]{2,1,0:T(8,128)} async-done(((f32[8,512,512]{2,1,0:T(8,128)}), f32[8,16,512]{2,1,0:T(8,128)}) %reduce-scatter.7.cloned.1.call-update) | async-done | bytes 262160 | tf_op jit(solution)/shard_map/reduce_scatter | solution.py:264
  869.8 3.9 add_add_fusion.3
  873.7 36.8 %psum.7 = f32[]{:T(128)} all-reduce(f32[]{:T(128)S(6)} %add.344), channel_id=1, replica_groups=mesh['dp'=4,'fsdp'=8] {'dp','fsdp'}, use_global_device_ids=true, to_apply=%region_40.41 | all-reduce | flops 1 | bytes 8 | tf_op jit(solution)/shard_map/psum | solution.py:275
  916.4 2.1 multiply_subtract_fusion
  (255 shorter events, 75.9 us)
Async XLA Ops:
  7.2 99.0 %copy-start = (bf16[4,512,512]{2,1,0:T(8,128)(2,1)S(1)}, bf16[4,512,512]{2,1,0:T(8,128)(2,1)}, u32[]{:S(2)}) copy-start(bf16[4,512,512]{2,1,0:T(8,128)(2,1)} %param.18) | copy-start | bytes 6291460
  7.2 55.4 %copy-start.73 = (s32[4]{0:T(128)S(1)}, s32[4]{0:T(128)}, u32[]{:S(2)}) copy-start(s32[4]{0:T(128)} %param.20) | copy-start | bytes 52
  7.2 68.9 %all-gather.4.cloned.1.call-start = ((), (), s32[]{:S(2)}) async-start(), calls=%async_computation.4 | async-start | bytes 4325376 | tf_op jit(solution)/shard_map/all_gather | solution.py:119
  9.0 169.3 %all-gather.6.cloned.1.call-start = ((), (), s32[]{:S(2)}) async-start(), calls=%async_computation.5 | async-start | bytes 2162688 | tf_op jit(solution)/shard_map/all_gather | solution.py:120
  10.7 192.1 %all-gather.8.cloned.1.call-start = ((), (), s32[]{:S(2)}) async-start(), calls=%async_computation.6 | async-start | bytes 2162688 | tf_op jit(solution)/shard_map/all_gather | solution.py:121
  12.3 428.4 %reduce-scatter.13.cloned.1.call-start = ((), (), s32[]{:S(2)}) async-start(), calls=%async_computation.10 | async-start | bytes 270336
  59.6 10.0 %copy-start.7 = (bf16[4,256,512]{2,1,0:T(8,128)(2,1)S(1)}, bf16[4,256,512]{2,1,0:T(8,128)(2,1)}, u32[]{:S(2)}) copy-start(bf16[4,256,512]{2,1,0:T(8,128)(2,1)} %param.17) | copy-start | bytes 3145732
  62.6 8.5 copy-start.56
  63.7 4.4 copy-start.19
  66.0 3.6 copy-start.58
  66.0 83.8 %copy-start.67 = (f32[512]{0:T(512)}, f32[512]{0:T(512)S(1)}, u32[]{:S(2)}) copy-start(f32[512]{0:T(512)S(1)} %get-tuple-element.64) | copy-start | bytes 6148
  66.0 83.8 %copy-start.71 = (f32[512]{0:T(512)}, f32[512]{0:T(512)S(1)}, u32[]{:S(2)}) copy-start(f32[512]{0:T(512)S(1)} %get-tuple-element.63) | copy-start | bytes 6148
  140.4 3.2 copy-start.2
  140.4 3.2 copy-start.32
  148.6 5.2 copy-start.62
  149.0 4.7 copy-start.65
  156.0 4.7 copy-start.28
  160.7 6.3 copy-start.1
  160.7 6.3 copy-start.24
  174.1 4.2 copy-start.43
  178.3 24.5 %copy-start.47 = (bf16[1024,512]{1,0:T(8,128)(2,1)S(1)}, bf16[1024,512]{1,0:T(8,128)(2,1)}, u32[]{:S(2)}) copy-start(bf16[1024,512]{1,0:T(8,128)(2,1)} %fusion.31) | copy-start | bytes 3145732
  202.8 9.5 %copy-start.5 = (f32[1024,512]{1,0:T(8,128)S(1)}, f32[1024,512]{1,0:T(8,128)}, u32[]{:S(2)}) copy-start(f32[1024,512]{1,0:T(8,128)} %copy-done.4) | copy-start | bytes 6291460
  202.8 9.5 %copy-start.75 = (bf16[512,2048]{1,0:T(8,128)(2,1)S(1)}, bf16[512,2048]{1,0:T(8,128)(2,1)}, u32[]{:S(2)}) copy-start(bf16[512,2048]{1,0:T(8,128)(2,1)} %all-gather.6.cloned.1.call-done) | copy-start | bytes 6291460
  212.2 2.9 copy-start.26
  224.9 8.5 copy-start.25
  245.2 12.3 %copy-start.11 = (bf16[4,512,8,64]{1,3,2,0:T(8,128)(2,1)S(1)}, bf16[4,512,8,64]{1,3,2,0:T(8,128)(2,1)}, u32[]{:S(2)}) copy-start(bf16[4,512,8,64]{1,3,2,0:T(8,128)(2,1)} %copy.159) | copy-start | bytes 6291460
  257.6 3.2 copy-start.3
  261.6 3.2 copy-start.61
  261.9 3.0 copy-start.48
  268.6 6.1 copy-start.53
  274.7 5.9 copy-start.33
  274.7 11.5 %slice-start = ((s8[8388608]{0:T(1024)(128)(4,1)}), s8[4194304]{0:T(1024)(128)(4,1)S(1)}, s32[]{:S(2)}) async-start(s8[8388608]{0:T(1024)(128)(4,1)} %bitcast.261), calls=%async_computation.11 | async-start | bytes 8388608
  280.7 5.6 slice-start.1
  288.4 2.4 copy-start.31
  293.8 3.6 copy-start.45
  297.3 5.2 copy-start.36
  298.4 4.1 copy-start.8
  298.4 4.1 copy-start.34
  298.4 4.1 copy-start.55
  298.5 4.1 copy-start.59
  302.6 2.5 copy-start.64
  302.6 5.0 copy-start.69
  308.6 271.1 %reduce-scatter.11.cloned.1.call-start = ((), (), s32[]{:S(2)}) async-start(), calls=%async_computation.9 | async-start | bytes 4325376 | tf_op jit(solution)/shard_map/reduce_scatter | solution.py:266
  315.5 403.1 %reduce-scatter.9.cloned.1.call-start = ((), (), s32[]{:S(2)}) async-start(), calls=%async_computation.8 | async-start | bytes 4325376 | tf_op jit(solution)/shard_map/reduce_scatter | solution.py:265
  322.9 542.7 %reduce-scatter.7.cloned.1.call-start = ((), (), s32[]{:S(2)}) async-start(), calls=%async_computation.7 | async-start | bytes 8650752 | tf_op jit(solution)/shard_map/reduce_scatter | solution.py:264
  323.2 3.9 copy-start.29
  327.1 19.6 %copy-start.22 = (bf16[64,8,4,512]{3,1,2,0:T(8,128)(2,1)}, bf16[64,8,4,512]{3,1,2,0:T(8,128)(2,1)S(1)}, u32[]{:S(2)}) copy-start(bf16[64,8,4,512]{3,1,2,0:T(8,128)(2,1)S(1)} %copy.222) | copy-start | bytes 6291460
  334.5 2.4 copy-start.37
  335.2 9.2 copy-start.27
  335.2 3.6 copy-start.35
  336.9 3.6 copy-start.10
  336.9 3.6 copy-start.42
  338.7 3.5 copy-start.15
  338.7 3.5 copy-start.49
  338.7 3.5 copy-start.72
  346.7 2.6 copy-start.44
  346.7 2.6 copy-start.52
  351.6 3.2 copy-start.23
  354.8 4.6 copy-start.6
  354.8 4.6 copy-start.70
  354.8 4.6 copy-start.74
  354.8 4.6 copy-start.76
  363.1 549.6 %copy-start.54 = (f32[16,2048]{1,0:T(8,128)S(1)}, f32[16,2048]{1,0:T(8,128)}, u32[]{:S(2)}) copy-start(f32[16,2048]{1,0:T(8,128)} %param.23) | copy-start | bytes 393220
  869.8 46.6 %copy-start.50 = (f32[8,16,512]{2,1,0:T(8,128)S(1)}, f32[8,16,512]{2,1,0:T(8,128)}, u32[]{:S(2)}) copy-start(f32[8,16,512]{2,1,0:T(8,128)} %param.22) | copy-start | bytes 786436
  (22 other events, 37.8 us)
Sparse Core Ops, SparseCore 0:
  11.5 64.5 all-gather.3
  79.5 54.7 all-gather.5
  137.8 55.2 all-gather.7
  308.7 131.9 reduce-scatter.12
  442.9 136.6 reduce-scatter.10
  581.9 136.6 reduce-scatter.8
  721.0 144.5 reduce-scatter.6
where the time goes:
time: 934 us; the launch traced here: 927 us
  waiting for transfers between devices  503 us (54%)
  matrix products  173 us (19%)
  local copies, waits for them, and re-layouts  89.9 us (10%)
  blocking collectives  80.4 us (9%)
  other arithmetic  60.2 us (6%)
  between operations  20.2 us (2%)
    reduce_scatter x1, waiting for transfers between devices, local(): lax.psum_scatter(grad_attn, ('dp', 'fsdp'), scatter_dimension=1, tiled=True)  145 us
    reduce_scatter x1, waiting for transfers between devices, local(): lax.psum_scatter(grad_ffn_out, ('dp', 'fsdp'), scatter_dimension=0, tiled...  138 us
    reduce_scatter x1, waiting for transfers between devices, local(): lax.psum_scatter(grad_ffn_in, ('dp', 'fsdp'), scatter_dimension=0, tiled=...  137 us
    unnamed x8, waiting for transfers between devices  77.8 us
    reshape x16, local copies, waits for them, and re-layouts, split_heads(): return flat.reshape(seqs, rows, HEADS, HEAD_DIM)  57.8 us
    dot_general x10, matrix products, plain_dot(): return jnp.dot(left, right, preferred_element_type=jnp.float32)  50.4 us
    all_gather x1, blocking collectives, local(): lax.all_gather(copies[3], ('dp', 'fsdp'), axis=1, tiled=True)  43.6 us
    psum x1, blocking collectives, local(): total_squares = lax.psum(local_squares, ('dp', 'fsdp'))  36.8 us
  transfers between devices with their start and end apart: 7, of which 5 were waited for; matrix products, arithmetic and copies ran while one was open for 21% of the time, Pallas kernels for 0%

commit v1 on v0

--- a/solution.py
+++ b/solution.py
@@ -90,7 +90,52 @@
     return (weight_new, first_new, second_new)
 
 
+AXES = ("dp", "fsdp")
+
+
+class Grid:
+    def __init__(self, dp, fsdp):
+        self.sizes = (dp, fsdp // 2, 2)
+        self.strides = (fsdp, 2, 1)
+        self.devices = dp * fsdp
+        index = lax.axis_index("fsdp")
+        self.place = (lax.axis_index("dp"), index // 2, index % 2)
+
+    def swap(self, values, stage, step):
+        stride = self.strides[stage]
+        pairs = [(i, i ^ (step * stride)) for i in range(self.devices)]
+        return lax.ppermute(values, AXES, pairs)
+
+    def gather(self, chunk):
+        held = chunk
+        for stage in range(3):
+            size, place = self.sizes[stage], self.place[stage]
+            parts = [held] + [self.swap(held, stage, step) for step in range(1, size)]
+            if size == 2:
+                first = jnp.where(place == 0, parts[0], parts[1])
+                second = jnp.where(place == 0, parts[1], parts[0])
+                held = jnp.stack([first, second], stage)
+            else:
+                whole = jnp.zeros(held.shape[:stage] + (size,) + held.shape[stage:], held.dtype)
+                for step in range(size):
+                    whole = lax.dynamic_update_index_in_dim(whole, parts[step], place ^ step, stage)
+                held = whole
+        return held
+
+    def scatter(self, parts):
+        held = parts
+        for stage in (2, 1, 0):
+            size, place = self.sizes[stage], self.place[stage]
+            total = lax.dynamic_index_in_dim(held, place, stage, False).astype(jnp.float32)
+            for step in range(1, size):
+                piece = lax.dynamic_index_in_dim(held, place ^ step, stage, False)
+                total = total + self.swap(piece.astype(jnp.bfloat16), stage, step).astype(jnp.float32)
+            held = total
+        return held
+
+
 def local(
+    grid,
     inputs,
     memory,
     cotangent,
@@ -109,18 +154,40 @@
     vector_first,
     vector_second,
 ):
-    copies = (
-        attn_weights.astype(jnp.bfloat16),
-        ffn_in.astype(jnp.bfloat16),
-        ffn_out.astype(jnp.bfloat16),
-        vectors.astype(jnp.bfloat16),
-    )
-    attn_full, ffn_in_full, ffn_out_full, table_full = (
-        lax.all_gather(copies[0], ("dp", "fsdp"), axis=1, tiled=True),
-        lax.all_gather(copies[1], ("dp", "fsdp"), axis=0, tiled=True),
-        lax.all_gather(copies[2], ("dp", "fsdp"), axis=0, tiled=True),
-        lax.all_gather(copies[3], ("dp", "fsdp"), axis=1, tiled=True),
-    )
+    width = inputs.shape[2]
+    own = attn_weights.shape[1]
+    spots = grid.sizes
+
+    def fold(array):
+        return array.reshape(-1, width)
+
+    vec_count = vectors.shape[0]
+    table_rows = -(-vec_count * own // width)
+
+    def fold_table(array, lead=()):
+        flat = array.reshape(lead + (vec_count * own,))
+        pad = [(0, 0)] * len(lead) + [(0, table_rows * width - vec_count * own)]
+        return jnp.pad(flat, pad).reshape(lead + (table_rows, width))
+
+    def attn_unfold(full):
+        return jnp.moveaxis(full.reshape(grid.devices, -1, own, width), 1, 0).reshape(-1, width, width)
+
+    low = jnp.bfloat16
+    first_chunk = jnp.concatenate(
+        [fold(attn_weights[:4].astype(low)), fold_table(vectors.astype(low))], 0
+    )
+    first_full = grid.gather(first_chunk)
+    second_full = grid.gather(fold(attn_weights[4:].astype(low)))
+    ffn_chunk = jnp.concatenate([ffn_out.astype(low), fold(ffn_in.astype(low))], 0)
+    ffn_full = grid.gather(ffn_chunk)
+    out_rows = ffn_out.shape[0]
+    attn_full = jnp.concatenate([attn_unfold(first_full[..., : 4 * own, :]), attn_unfold(second_full)])
+    ffn_out_full = ffn_full[..., :out_rows, :].reshape(-1, width)
+    ffn_in_full = ffn_full[..., out_rows:, :].reshape(width, -1)
+    table_full = first_full[..., 4 * own :, :].reshape(grid.devices, table_rows * width)
+    table_full = table_full[:, : vec_count * own].reshape(grid.devices, vec_count, own)
+    table_full = jnp.moveaxis(table_full, 1, 0).reshape(vec_count, width)
+    attn_back, ffn_in_back, ffn_out_back = attn_full, ffn_in_full, ffn_out_full
     table = table_full.astype(jnp.float32)
     seqs, length, width = inputs.shape
     mem_len = memory.shape[1]
@@ -170,11 +237,6 @@
     hidden, gelu_back = jax.vjp(partial(jax.nn.gelu, approximate=False), hidden_pre)
     hidden_low = hidden.astype(jnp.bfloat16)
     output = resid_two + plain_dot(hidden_low, ffn_out_full) + table[12]
-    attn_back, ffn_in_back, ffn_out_back = (
-        lax.all_gather(copies[0], ("dp", "fsdp"), axis=1, tiled=True),
-        lax.all_gather(copies[1], ("dp", "fsdp"), axis=0, tiled=True),
-        lax.all_gather(copies[2], ("dp", "fsdp"), axis=0, tiled=True),
-    )
     grad_out = cotangent.astype(jnp.float32).reshape(tokens, width) * valid.reshape(tokens)[
         :, None
     ].astype(jnp.float32)
@@ -259,12 +321,36 @@
         ]
     )
     grad_table = jnp.concatenate([small_rows, grad_in_bias.reshape(-1, width)], 0)
-    grad_attn = jnp.concatenate([grad_self_stack, grad_cross_stack], 0)
+
+    def attn_fold(stack):
+        parts = stack.reshape(4, grid.devices, own, width)
+        return jnp.moveaxis(parts, 0, 1).reshape(grid.devices, 4 * own, width)
+
+    grad_parts = jnp.moveaxis(grad_table.reshape(vec_count, grid.devices, own), 0, 1)
+    last_parts = jnp.concatenate(
+        [attn_fold(grad_self_stack), fold_table(grad_parts, (grid.devices,))], 1
+    )
+    ffn_parts = jnp.concatenate(
+        [
+            grad_ffn_out.reshape(grid.devices, -1, width),
+            grad_ffn_in.reshape(grid.devices, -1, width),
+        ],
+        1,
+    )
+
+    def reduce(parts):
+        return grid.scatter(parts.reshape(spots + parts.shape[1:]))
+
+    ffn_share = reduce(ffn_parts)
+    cross_share = reduce(attn_fold(grad_cross_stack))
+    last_share = reduce(last_parts)
+    self_share = last_share[: 4 * own].reshape(4, own, width)
+    table_share = last_share[4 * own :].reshape(-1)[: vec_count * own].reshape(vec_count, own)
     shares = (
-        lax.psum_scatter(grad_attn, ("dp", "fsdp"), scatter_dimension=1, tiled=True),
-        lax.psum_scatter(grad_ffn_in, ("dp", "fsdp"), scatter_dimension=0, tiled=True),
-        lax.psum_scatter(grad_ffn_out, ("dp", "fsdp"), scatter_dimension=0, tiled=True),
-        lax.psum_scatter(grad_table, ("dp", "fsdp"), scatter_dimension=1, tiled=True),
+        jnp.concatenate([self_share, cross_share.reshape(4, own, width)], 0),
+        ffn_share[out_rows:].reshape(ffn_in.shape),
+        ffn_share[:out_rows],
+        table_share,
     )
     local_squares = (
         jnp.sum(shares[0] * shares[0])
@@ -272,7 +358,8 @@
         + jnp.sum(shares[2] * shares[2])
         + jnp.sum(shares[3] * shares[3])
     )
-    total_squares = lax.psum(local_squares, ("dp", "fsdp"))
+    spread = jnp.broadcast_to(local_squares, (grid.devices, 8, 128))
+    total_squares = jnp.sum(lax.all_to_all(spread, AXES, 0, 0)[:, 0, 0])
     grad_norm = jnp.sqrt(total_squares)
     clip_scale = jnp.minimum(1.0, 1.0 / (grad_norm + 1e-06))
     step = jnp.float32(STEP)
@@ -303,8 +390,11 @@
 
 
 def solution(mesh):
+    def whole(*arrays):
+        return local(Grid(mesh.shape["dp"], mesh.shape["fsdp"]), *arrays)
+
     return jax.shard_map(
-        local,
+        whole,
         mesh=mesh,
         in_specs=(
             P(("dp", "fsdp"), None, None),

time: 934 us -> 534 us (0.57)
  waiting for transfers between devices: 503 us -> 63.5 us
  blocking collectives: 80.4 us -> 0 us
  local copies, waits for them, and re-layouts: 89.9 us -> 148 us
  starting transfers between devices: 0.5 us -> 55.9 us
  other arithmetic: 60.2 us -> 99.5 us
  matrix products: 173 us -> 151 us
  between operations: 20.2 us -> 7.68 us
    reduce_scatter x3 -> x0, waiting for transfers between devices: 420 us -> none  [the longest x1 145 us: local(): lax.psum_scatter(grad_attn, ('dp', 'fsdp'), scatter_dimension=1, tiled=True)]
    unnamed x8 -> x0, waiting for transfers between devices: 77.8 us -> none
    ppermute x0 -> x42, waiting for transfers between devices: none -> 59.7 us  [swap(): return lax.ppermute(values, AXES, pairs)]
    ppermute x0 -> x42, starting transfers between devices: none -> 51.8 us  [swap(): return lax.ppermute(values, AXES, pairs)]
    all_gather x1 -> x0, blocking collectives: 43.6 us -> none  [local(): lax.all_gather(copies[3], ('dp', 'fsdp'), axis=1, tiled=True)]
    psum x1 -> x0, blocking collectives: 36.8 us -> none  [local(): total_squares = lax.psum(local_squares, ('dp', 'fsdp'))]
    convert_element_type x6, other arithmetic: 6.92 us -> 25.2 us  [the longest x1 20 us: local(): hidden_low = hidden.astype(jnp.bfloat16)]
    unnamed x172 -> x302, local copies, waits for them, and re-layouts: 18.8 us -> 33.7 us
  transfers between devices with their start and end apart: 7 -> 43, of which waited for: 5 -> 15; matrix products, arithmetic and copies ran while one was open for 21% -> 35% of each run, Pallas kernels for 0% -> 0%
where the time goes in v1:
time: 534 us; the launch traced here: 526 us
  matrix products  151 us (28%)
  local copies, waits for them, and re-layouts  148 us (28%)
  other arithmetic  99.5 us (19%)
  waiting for transfers between devices  63.5 us (12%)
  starting transfers between devices  55.9 us (10%)
  between operations  7.68 us (1%)
    ppermute x42, waiting for transfers between devices, swap(): return lax.ppermute(values, AXES, pairs)  59.7 us
    ppermute x42, starting transfers between devices, swap(): return lax.ppermute(values, AXES, pairs)  51.8 us
    reshape x14, local copies, waits for them, and re-layouts, split_heads(): return flat.reshape(seqs, rows, HEADS, HEAD_DIM)  45.2 us
    dot_general x10, matrix products, plain_dot(): return jnp.dot(left, right, preferred_element_type=jnp.float32)  42.8 us
    unnamed x302, local copies, waits for them, and re-layouts  33.7 us
    dot_general x10, matrix products, right_dot(): lax.dot_general(left, right, (((1,), (1,)), ((), ())), preferred_element_...  26.5 us
    dot_general x10, matrix products, left_dot(): lax.dot_general(left, right, (((0,), (0,)), ((), ())), preferred_element_...  25.4 us
    convert_element_type x1, other arithmetic, local(): hidden_low = hidden.astype(jnp.bfloat16)  20 us
  transfers between devices with their start and end apart: 43, of which 15 were waited for; matrix products, arithmetic and copies ran while one was open for 35% of the time, Pallas kernels for 0%

profile of v1, /device:TPU:0, one launch (start us, length us, event | category | flops | bytes accessed | tf_op | source)
XLA Modules:
  0.0 526.5 jit_solution(7610748770273542526)
XLA Ops:
  2.5 5.0 collective-permute-start.9
  27.3 2.5 convert_reduce_fusion.3
  36.5 3.0 collective-permute-start.14
  41.4 2.7 collective-permute-start.12
  47.9 2.4 collective-permute-start.5
  62.8 7.4 %collective-permute-done.3 = bf16[4,65,512]{2,1,0:T(8,128)(2,1)S(1)} collective-permute-done((bf16[4,65,512]{2,1,0:T(8,128)(2,1)S(1)}, bf16[4,65,512]{2,1,0:T(8,128)(2,1)S(1)}, u32[]{:S(2)}, u32[]{:S(2)}) %collective-permute-start.3) | collective-permute-done | bytes 266272 | tf_op jit(solution)/shard_map/ppermute | solution.py:107
  71.7 6.5 %collective-permute-done.4 = bf16[4,65,512]{2,1,0:T(8,128)(2,1)S(1)} collective-permute-done((bf16[4,65,512]{2,1,0:T(8,128)(2,1)S(1)}, bf16[4,65,512]{2,1,0:T(8,128)(2,1)S(1)}, u32[]{:S(2)}, u32[]{:S(2)}) %collective-permute-start.4) | collective-permute-done | bytes 266272 | tf_op jit(solution)/shard_map/ppermute | solution.py:107
  80.4 8.7 %collective-permute-done.17 = bf16[4,128,512]{2,1,0:T(8,128)(2,1)S(1)} collective-permute-done((bf16[4,128,512]{2,1,0:T(8,128)(2,1)}, bf16[4,128,512]{2,1,0:T(8,128)(2,1)S(1)}, u32[]{:S(2)}, u32[]{:S(2)}) %collective-permute-start.17) | collective-permute-done | bytes 524320 | tf_op jit(solution)/shard_map/ppermute | solution.py:107
  94.0 2.6 fusion.44
  96.6 4.7 reshape.696
  105.0 2.9 fusion.153
  113.9 2.7 add_convert_fusion.6
  116.6 3.9 reshape.723
  120.5 3.0 copy.918
  123.5 3.0 add_convert_fusion.5
  126.5 3.9 reshape.724
  130.4 3.0 copy.916
  133.4 3.0 convolution_convert_fusion.3
  136.5 3.9 reshape.725
  140.3 3.0 copy.917
  143.4 3.8 fusion.43
  147.2 4.9 reshape.694
  152.1 3.1 fusion.156
  168.7 5.2 fusion.158
  173.9 4.1 fusion
  180.3 7.0 %fusion.82 = bf16[4,256,8,64]{1,3,2,0:T(8,128)(2,1)} fusion(f32[4,8,256,512]{3,2,1,0:T(8,128)S(1)} %get-tuple-element.274, f32[4,8,256]{2,1,0:T(8,128)S(1)} %fusion, f32[4,8,256]{2,1,0:T(8,128)S(1)} %get-tuple-element.273, bf16[4,512,8,64]{1,0,3,2:T(4,128)(2,1)S(1)} %copy-done.24), kind=kOutput, calls=%fused_computation.165 | convolution fusion | flops 549978112 | bytes 19988480 | tf_op jit(solution)/shard_map/shqk,skhe->sqhe/dot_general | solution.py:52
  200.4 2.5 select_bitcast_fusion.1
  205.0 4.4 reshape.698
  209.4 21.4 %fusion.2 = (f32[1024,2048]{1,0:T(8,128)S(1)}, f32[1024,2048]{1,0:T(8,128)S(1)}) fusion(f32[2048]{0:T(1024)S(1)} %add.492, bf16[512,2048]{1,0:T(8,128)(2,1)} %reshape.698, f32[1024,512]{1,0:T(8,128)} %copy-done.3, f32[512]{0:T(512)} %add.489, f32[512]{0:T(512)} %mul.462, f32[1024]{0:T(1024)S(1)} %fusion.132, f32[1024]{0:T(1024)S(1)} %broadcast_multiply_fusion), kind=kOutput, calls=%fused_computation.14 | convolution fusion | flops 2282225664 | bytes 20992000 | tf_op jit(solution)/shard_map/dot_general | solution.py:20
  230.8 20.0 %fusion.5 = bf16[2048,1024]{0,1:T(8,128)(2,1)} fusion(f32[1024,2048]{1,0:T(8,128)S(1)} %get-tuple-element.278, f32[2048]{0:T(1024)S(1)} %add.492), kind=kLoop, calls=%fused_computation.17 | loop fusion | flops 138412032 | bytes 12591104 | tf_op jit(solution)/shard_map/convert_element_type | solution.py:238
  250.9 7.4 %convert_reduce_fusion = (f32[2048]{0:T(1024)}, bf16[1024,2048]{1,0:T(8,128)(2,1)S(1)}) fusion(f32[1024,2048]{1,0:T(8,128)S(1)} %get-tuple-element.277, bf16[1024,512]{1,0:T(8,128)(2,1)} %bitcast.575, bf16[2048,512]{1,0:T(8,128)(2,1)} %bitcast.538, f32[1024,2048]{1,0:T(8,128)S(1)} %get-tuple-element.278, f32[2048]{0:T(1024)S(1)} %add.492), kind=kOutput, calls=%fused_computation.36 | convolution fusion | flops 2183133184 | bytes 24133632 | tf_op jit(solution)/shard_map/dot_general | solution.py:30
  258.3 5.0 multiply_reduce_fusion.2
  263.3 4.6 fusion.141
  273.2 4.0 reshape.727
  279.5 8.5 %convert_reduce_fusion.1 = (f32[8,64]{1,0:T(8,128)S(1)}, bf16[4,512,8,64]{1,3,2,0:T(8,128)(2,1)}) fusion(bf16[4,256,8,64]{1,3,2,0:T(8,128)(2,1)S(1)} %copy.945, f32[4,8,256,512]{3,2,1,0:T(8,128)} %copy-done.1, f32[4,8,256]{2,1,0:T(8,128)S(1)} %log_add_fusion.1), kind=kOutput, calls=%fused_computation.79 | convolution fusion | flops 548404736 | bytes 19957760 | tf_op jit(solution)/shard_map/shqk,sqhe->skhe/dot_general | solution.py:72
  288.0 11.9 %multiply_reduce_fusion = (f32[4,8,256]{2,1,0:T(8,128)S(1)}, f32[4,8,256,512]{3,2,1,0:T(8,128)}) fusion(f32[4,8,256,512]{3,2,1,0:T(8,128)} %copy-done.1, f32[4,8,256]{2,1,0:T(8,128)S(1)} %log_add_fusion.1, bf16[4,256,8,64]{1,3,2,0:T(8,128)(2,1)S(1)} %copy.945, bf16[4,512,8,64]{1,0,3,2:T(4,128)(2,1)S(1)} %copy-done.25), kind=kOutput, calls=%fused_computation.1 | convolution fusion | flops 549445632 | bytes 36765696 | tf_op jit(solution)/shard_map/sqhe,skhe->shqk/dot_general | solution.py:59
  299.9 11.9 %multiply_convert_fusion = bf16[4,8,256,512]{3,2,1,0:T(8,128)(2,1)S(1)} fusion(f32[4,8,256,512]{3,2,1,0:T(8,128)} %get-tuple-element.281, f32[4,8,256,512]{3,2,1,0:T(8,128)} %copy-done.1, f32[4,8,256]{2,1,0:T(8,128)S(1)} %get-tuple-element.280, f32[4,8,256]{2,1,0:T(8,128)S(1)} %log_add_fusion.1), kind=kLoop, calls=%fused_computation | loop fusion | flops 16777216 | bytes 42008576 | tf_op jit(solution)/shard_map/convert_element_type | solution.py:63
  311.9 2.8 convert_reduce_fusion.5
  314.7 2.9 fusion.72
  329.0 5.9 %convert_reduce_fusion.7 = (f32[8,64]{1,0:T(8,128)S(1)}, bf16[4,256,8,64]{1,3,2,0:T(8,128)(2,1)}) fusion(bf16[4,256,8,64]{1,3,2,0:T(8,128)(2,1)S(1)} %copy.950, f32[4,8,256,256]{2,3,1,0:T(8,128)} %copy-done.2, f32[4,8,256]{2,1,0:T(8,128)S(1)} %log_add_fusion), kind=kOutput, calls=%fused_computation.127 | convolution fusion | flops 274202112 | bytes 10520576 | tf_op jit(solution)/shard_map/shqk,sqhe->skhe/dot_general | solution.py:72
  334.9 5.6 %multiply_reduce_fusion.1 = (f32[4,8,256]{2,1,0:T(8,128)S(1)}, f32[4,8,256,256]{2,3,1,0:T(8,128)S(1)}) fusion(f32[4,8,256,256]{2,3,1,0:T(8,128)} %copy-done.2, f32[4,8,256]{2,1,0:T(8,128)S(1)} %log_add_fusion, bf16[4,256,8,64]{1,3,2,0:T(8,128)(2,1)S(1)} %copy.950, bf16[4,256,8,64]{1,3,2,0:T(8,128)(2,1)S(1)} %copy-done.43), kind=kOutput, calls=%fused_computation.38 | convolution fusion | flops 274718720 | bytes 18939904 | tf_op jit(solution)/shard_map/sqhe,skhe->shqk/dot_general | solution.py:59
  355.2 3.7 add_add_fusion.6
  358.9 6.4 %copy.984 = bf16[2048,1024]{1,0:T(8,128)(2,1)} copy(bf16[2048,1024]{0,1:T(8,128)(2,1)} %fusion.5) | data formatting | bytes 8388608 | tf_op jit(solution)/shard_map/convert_element_type | solution.py:238
  365.3 5.4 %concatenate.78 = f32[4,4,2,64,512]{4,3,2,1,0:T(8,128)} reshape(f32[512,2048]{1,0:T(8,128)} %fusion.141) | data formatting | bytes 8388608 | tf_op jit(solution)/shard_map/concatenate | solution.py:333
  370.8 3.3 convolution_bitcast_fusion
  374.5 3.2 copy.964
  391.3 2.9 convolution_bitcast_fusion.1
  394.4 3.0 fusion.163
  406.5 2.4 maximum_bitcast_fusion
  409.0 2.6 copy.969
  426.5 3.4 convolution_add_fusion
  442.4 4.8 collective-permute-done.31
  448.1 6.7 %collective-permute-done.30 = bf16[4,64,512]{2,1,0:T(8,128)(2,1)S(1)} collective-permute-done((bf16[4,64,512]{2,1,0:T(8,128)(2,1)S(1)}, bf16[4,64,512]{2,1,0:T(8,128)(2,1)S(1)}, u32[]{:S(2)}, u32[]{:S(2)}) %collective-permute-start.30) | collective-permute-done | bytes 262176 | tf_op jit(solution)/shard_map/ppermute | solution.py:107
  455.7 3.3 collective-permute-start.34
  466.6 2.5 collective-permute-start.26
  469.1 4.3 collective-permute-done.33
  473.5 3.0 collective-permute-done.36
  477.6 5.9 %collective-permute-done.38 = bf16[4,128,512]{2,1,0:T(8,128)(2,1)S(1)} collective-permute-done((bf16[4,128,512]{2,1,0:T(8,128)(2,1)S(1)}, bf16[4,128,512]{2,1,0:T(8,128)(2,1)S(1)}, u32[]{:S(2)}, u32[]{:S(2)}) %collective-permute-start.38) | collective-permute-done | bytes 524320 | tf_op jit(solution)/shard_map/ppermute | solution.py:107
  486.1 3.1 collective-permute-start.41
  491.1 2.5 collective-permute-done.41
  493.6 4.3 collective-permute-done.40
  501.9 4.1 all-to-all-start
  506.0 4.4 add_add_fusion.3
  510.4 3.8 all-to-all-done
  (577 shorter events, 204.6 us)
Async XLA Ops:
  0.6 92.5 %copy-start = (bf16[4,512,512]{2,1,0:T(8,128)(2,1)S(1)}, bf16[4,512,512]{2,1,0:T(8,128)(2,1)}, u32[]{:S(2)}) copy-start(bf16[4,512,512]{2,1,0:T(8,128)(2,1)} %param.18) | copy-start | bytes 6291460
  0.7 18.2 %copy-start.10 = (bf16[4,256,512]{2,1,0:T(8,128)(2,1)S(1)}, bf16[4,256,512]{2,1,0:T(8,128)(2,1)}, u32[]{:S(2)}) copy-start(bf16[4,256,512]{2,1,0:T(8,128)(2,1)} %param.17) | copy-start | bytes 3145732
  0.7 19.9 %copy-start.127 = (s32[4]{0:T(128)S(1)}, s32[4]{0:T(128)}, u32[]{:S(2)}) copy-start(s32[4]{0:T(128)} %param.20) | copy-start | bytes 52
  0.7 20.5 %copy-start.121 = (f32[17,16]{0,1:T(8,128)S(1)}, f32[17,16]{0,1:T(8,128)}, u32[]{:S(2)}) copy-start(f32[17,16]{0,1:T(8,128)} %param.32) | copy-start | bytes 3268
  0.7 21.2 %copy-start.122 = (f32[17,16]{0,1:T(8,128)S(1)}, f32[17,16]{0,1:T(8,128)}, u32[]{:S(2)}) copy-start(f32[17,16]{0,1:T(8,128)} %param.33) | copy-start | bytes 3268
  0.7 21.9 %copy-start.75 = (f32[64,512]{1,0:T(8,128)S(1)}, f32[64,512]{1,0:T(8,128)}, u32[]{:S(2)}) copy-start(f32[64,512]{1,0:T(8,128)} %param.24) | copy-start | bytes 393220
  2.5 34.0 %collective-permute-start.9 = (bf16[64,512]{1,0:T(8,128)(2,1)}, bf16[64,512]{1,0:T(8,128)(2,1)}, u32[]{:S(2)}, u32[]{:S(2)}) collective-permute-start(bf16[64,512]{1,0:T(8,128)(2,1)} %bitcast.29), channel_id=1, source_target_pairs={{0,24},{1,25},{2,26},{3,27},{4,28},{5,29},{6,30},{7,31},{8,16},{9,... | collective-permute-start | bytes 196616 | tf_op jit(solution)/shard_map/ppermute | solution.py:107
  7.5 26.6 %collective-permute-start.8 = (bf16[64,512]{1,0:T(8,128)(2,1)}, bf16[64,512]{1,0:T(8,128)(2,1)}, u32[]{:S(2)}, u32[]{:S(2)}) collective-permute-start(bf16[64,512]{1,0:T(8,128)(2,1)} %bitcast.29), channel_id=1, source_target_pairs={{0,16},{1,17},{2,18},{3,19},{4,20},{5,21},{6,22},{7,23},{8,24},{9,... | collective-permute-start | bytes 196616 | tf_op jit(solution)/shard_map/ppermute | solution.py:107
  7.5 25.7 %collective-permute-start.7 = (bf16[64,512]{1,0:T(8,128)(2,1)}, bf16[64,512]{1,0:T(8,128)(2,1)}, u32[]{:S(2)}, u32[]{:S(2)}) collective-permute-start(bf16[64,512]{1,0:T(8,128)(2,1)} %bitcast.29), channel_id=1, source_target_pairs={{0,8},{1,9},{2,10},{3,11},{4,12},{5,13},{6,14},{7,15},{8,0},{9,1},... | collective-permute-start | bytes 196616 | tf_op jit(solution)/shard_map/ppermute | solution.py:107
  9.7 31.8 %collective-permute-start.1 = (bf16[65,512]{1,0:T(8,128)(2,1)}, bf16[65,512]{1,0:T(8,128)(2,1)}, u32[]{:S(2)}, u32[]{:S(2)}) collective-permute-start(bf16[65,512]{1,0:T(8,128)(2,1)} %pad_maximum_fusion.5), channel_id=1, source_target_pairs={{0,16},{1,17},{2,18},{3,19},{4,20},{5,21},{6,22},{7,23},{8,24},{9,... | collective-permute-start | bytes 199688 | tf_op jit(solution)/shard_map/ppermute | solution.py:107
  12.0 28.4 %collective-permute-start = (bf16[65,512]{1,0:T(8,128)(2,1)}, bf16[65,512]{1,0:T(8,128)(2,1)}, u32[]{:S(2)}, u32[]{:S(2)}) collective-permute-start(bf16[65,512]{1,0:T(8,128)(2,1)} %pad_maximum_fusion.5), channel_id=1, source_target_pairs={{0,8},{1,9},{2,10},{3,11},{4,12},{5,13},{6,14},{7,15},{8,0},{9,1},... | collective-permute-start | bytes 199688 | tf_op jit(solution)/shard_map/ppermute | solution.py:107
  30.5 9.9 %copy-start.92 = (bf16[128,512]{1,0:T(8,128)(2,1)S(1)}, bf16[128,512]{1,0:T(8,128)(2,1)}, u32[]{:S(2)}) copy-start(bf16[128,512]{1,0:T(8,128)(2,1)} %pad_maximum_fusion.4) | copy-start | bytes 393220
  33.2 11.9 %collective-permute-start.2 = (bf16[65,512]{1,0:T(8,128)(2,1)}, bf16[65,512]{1,0:T(8,128)(2,1)S(1)}, u32[]{:S(2)}, u32[]{:S(2)}) collective-permute-start(bf16[65,512]{1,0:T(8,128)(2,1)} %pad_maximum_fusion.5), channel_id=1, source_target_pairs={{0,24},{1,25},{2,26},{3,27},{4,28},{5,29},{6,30},{7,31},{8,16},{9,... | collective-permute-start | bytes 199688 | tf_op jit(solution)/shard_map/ppermute | solution.py:107
  34.1 13.8 %collective-permute-start.15 = (bf16[128,512]{1,0:T(8,128)(2,1)}, bf16[128,512]{1,0:T(8,128)(2,1)S(1)}, u32[]{:S(2)}, u32[]{:S(2)}) collective-permute-start(bf16[128,512]{1,0:T(8,128)(2,1)} %pad_maximum_fusion.4), channel_id=1, source_target_pairs={{0,16},{1,17},{2,18},{3,19},{4,20},{5,21},{6,22},{7,23},{8,24},{9,... | collective-permute-start | bytes 393224 | tf_op jit(solution)/shard_map/ppermute | solution.py:107
  36.5 9.3 %collective-permute-start.14 = (bf16[128,512]{1,0:T(8,128)(2,1)}, bf16[128,512]{1,0:T(8,128)(2,1)S(1)}, u32[]{:S(2)}, u32[]{:S(2)}) collective-permute-start(bf16[128,512]{1,0:T(8,128)(2,1)} %pad_maximum_fusion.4), channel_id=1, source_target_pairs={{0,8},{1,9},{2,10},{3,11},{4,12},{5,13},{6,14},{7,15},{8,0},{9,1},... | collective-permute-start | bytes 393224 | tf_op jit(solution)/shard_map/ppermute | solution.py:107
  40.5 10.6 %collective-permute-start.16 = (bf16[128,512]{1,0:T(8,128)(2,1)S(1)}, bf16[128,512]{1,0:T(8,128)(2,1)S(1)}, u32[]{:S(2)}, u32[]{:S(2)}) collective-permute-start(bf16[128,512]{1,0:T(8,128)(2,1)S(1)} %copy-done.92), channel_id=1, source_target_pairs={{0,24},{1,25},{2,26},{3,27},{4,28},{5,29},{6,30},{7,31},{8,16},{9,... | collective-permute-start | bytes 393224 | tf_op jit(solution)/shard_map/ppermute | solution.py:107
  41.4 19.6 %collective-permute-start.12 = (bf16[4,64,512]{2,1,0:T(8,128)(2,1)S(1)}, bf16[4,64,512]{2,1,0:T(8,128)(2,1)S(1)}, u32[]{:S(2)}, u32[]{:S(2)}) collective-permute-start(bf16[4,64,512]{2,1,0:T(8,128)(2,1)S(1)} %bitcast_dynamic-update-slice_fusion.20), channel_id=1, source_target_pairs={{0,6},{1,7},{2,4},{3,5},{4,2},{5,3},{6,0},{7,1},{8,14},{9,15},{10,... | collective-permute-start | bytes 786440 | tf_op jit(solution)/shard_map/ppermute | solution.py:107
  45.0 15.6 %collective-permute-start.11 = (bf16[4,64,512]{2,1,0:T(8,128)(2,1)S(1)}, bf16[4,64,512]{2,1,0:T(8,128)(2,1)S(1)}, u32[]{:S(2)}, u32[]{:S(2)}) collective-permute-start(bf16[4,64,512]{2,1,0:T(8,128)(2,1)S(1)} %bitcast_dynamic-update-slice_fusion.20), channel_id=1, source_target_pairs={{0,4},{1,5},{2,6},{3,7},{4,0},{5,1},{6,2},{7,3},{8,12},{9,13},{10,... | collective-permute-start | bytes 786440 | tf_op jit(solution)/shard_map/ppermute | solution.py:107
  45.8 11.8 %collective-permute-start.10 = (bf16[4,64,512]{2,1,0:T(8,128)(2,1)S(1)}, bf16[4,64,512]{2,1,0:T(8,128)(2,1)S(1)}, u32[]{:S(2)}, u32[]{:S(2)}) collective-permute-start(bf16[4,64,512]{2,1,0:T(8,128)(2,1)S(1)} %bitcast_dynamic-update-slice_fusion.20), channel_id=1, source_target_pairs={{0,2},{1,3},{2,0},{3,1},{4,6},{5,7},{6,4},{7,5},{8,10},{9,11},{10,... | collective-permute-start | bytes 786440 | tf_op jit(solution)/shard_map/ppermute | solution.py:107
  47.9 30.3 %collective-permute-start.5 = (bf16[4,65,512]{2,1,0:T(8,128)(2,1)S(1)}, bf16[4,65,512]{2,1,0:T(8,128)(2,1)S(1)}, u32[]{:S(2)}, u32[]{:S(2)}) collective-permute-start(bf16[4,65,512]{2,1,0:T(8,128)(2,1)S(1)} %bitcast_dynamic-update-slice_fusion.16), channel_id=1, source_target_pairs={{0,6},{1,7},{2,4},{3,5},{4,2},{5,3},{6,0},{7,1},{8,14},{9,15},{10,... | collective-permute-start | bytes 798728 | tf_op jit(solution)/shard_map/ppermute | solution.py:107
  51.0 27.2 %collective-permute-start.4 = (bf16[4,65,512]{2,1,0:T(8,128)(2,1)S(1)}, bf16[4,65,512]{2,1,0:T(8,128)(2,1)S(1)}, u32[]{:S(2)}, u32[]{:S(2)}) collective-permute-start(bf16[4,65,512]{2,1,0:T(8,128)(2,1)S(1)} %bitcast_dynamic-update-slice_fusion.16), channel_id=1, source_target_pairs={{0,4},{1,5},{2,6},{3,7},{4,0},{5,1},{6,2},{7,3},{8,12},{9,13},{10,... | collective-permute-start | bytes 798728 | tf_op jit(solution)/shard_map/ppermute | solution.py:107
  57.6 12.7 %collective-permute-start.3 = (bf16[4,65,512]{2,1,0:T(8,128)(2,1)S(1)}, bf16[4,65,512]{2,1,0:T(8,128)(2,1)S(1)}, u32[]{:S(2)}, u32[]{:S(2)}) collective-permute-start(bf16[4,65,512]{2,1,0:T(8,128)(2,1)S(1)} %bitcast_dynamic-update-slice_fusion.16), channel_id=1, source_target_pairs={{0,2},{1,3},{2,0},{3,1},{4,6},{5,7},{6,4},{7,5},{8,10},{9,11},{10,... | collective-permute-start | bytes 798728 | tf_op jit(solution)/shard_map/ppermute | solution.py:107
  60.7 30.0 %collective-permute-start.19 = (bf16[4,128,512]{2,1,0:T(8,128)(2,1)}, bf16[4,128,512]{2,1,0:T(8,128)(2,1)S(1)}, u32[]{:S(2)}, u32[]{:S(2)}) collective-permute-start(bf16[4,128,512]{2,1,0:T(8,128)(2,1)} %bitcast_dynamic-update-slice_fusion.12), channel_id=1, source_target_pairs={{0,6},{1,7},{2,4},{3,5},{4,2},{5,3},{6,0},{7,1},{8,14},{9,15},{10,... | collective-permute-start | bytes 1572872 | tf_op jit(solution)/shard_map/ppermute | solution.py:107
  61.0 28.9 %collective-permute-start.18 = (bf16[4,128,512]{2,1,0:T(8,128)(2,1)}, bf16[4,128,512]{2,1,0:T(8,128)(2,1)S(1)}, u32[]{:S(2)}, u32[]{:S(2)}) collective-permute-start(bf16[4,128,512]{2,1,0:T(8,128)(2,1)} %bitcast_dynamic-update-slice_fusion.12), channel_id=1, source_target_pairs={{0,4},{1,5},{2,6},{3,7},{4,0},{5,1},{6,2},{7,3},{8,12},{9,13},{10,... | collective-permute-start | bytes 1572872 | tf_op jit(solution)/shard_map/ppermute | solution.py:107
  70.2 18.8 %collective-permute-start.17 = (bf16[4,128,512]{2,1,0:T(8,128)(2,1)}, bf16[4,128,512]{2,1,0:T(8,128)(2,1)S(1)}, u32[]{:S(2)}, u32[]{:S(2)}) collective-permute-start(bf16[4,128,512]{2,1,0:T(8,128)(2,1)} %bitcast_dynamic-update-slice_fusion.12), channel_id=1, source_target_pairs={{0,2},{1,3},{2,0},{3,1},{4,6},{5,7},{6,4},{7,5},{8,10},{9,11},{10,... | collective-permute-start | bytes 1572872 | tf_op jit(solution)/shard_map/ppermute | solution.py:107
  78.2 13.4 %collective-permute-start.13 = (bf16[4,4,64,512]{3,2,1,0:T(8,128)(2,1)S(1)}, bf16[4,4,64,512]{3,2,1,0:T(8,128)(2,1)S(1)}, u32[]{:S(2)}, u32[]{:S(2)}) collective-permute-start(bf16[4,4,64,512]{3,2,1,0:T(8,128)(2,1)S(1)} %bitcast_dynamic-update-slice_fusion.11), channel_id=1, source_target_pairs={{0,1},{1,0},{2,3},{3,2},{4,5},{5,4},{6,7},{7,6},{8,9},{9,8},{10,11... | collective-permute-start | bytes 3145736 | tf_op jit(solution)/shard_map/ppermute | solution.py:107
  78.3 13.3 %copy-start.29 = (bf16[4,4,65,512]{3,2,1,0:T(8,128)(2,1)}, bf16[4,4,65,512]{3,2,1,0:T(8,128)(2,1)S(1)}, u32[]{:S(2)}) copy-start(bf16[4,4,65,512]{3,2,1,0:T(8,128)(2,1)S(1)} %bitcast_dynamic-update-slice_fusion.7) | copy-start | bytes 3194884
  79.9 21.5 %collective-permute-start.6 = (bf16[4,4,65,512]{3,1,2,0:T(4,128)(2,1)}, bf16[4,4,65,512]{3,1,2,0:T(4,128)(2,1)}, u32[]{:S(2)}, u32[]{:S(2)}) collective-permute-start(bf16[4,4,65,512]{3,1,2,0:T(4,128)(2,1)} %copy.904), channel_id=1, source_target_pairs={{0,1},{1,0},{2,3},{3,2},{4,5},{5,4},{6,7},{7,6},{8,9},{9,8},{10,11... | collective-permute-start | bytes 3194888 | tf_op jit(solution)/shard_map/ppermute | solution.py:107
  91.6 108.8 %collective-permute-start.20 = (bf16[4,4,128,512]{3,2,1,0:T(8,128)(2,1)}, bf16[4,4,128,512]{3,2,1,0:T(8,128)(2,1)}, u32[]{:S(2)}, u32[]{:S(2)}) collective-permute-start(bf16[4,4,128,512]{3,2,1,0:T(8,128)(2,1)} %bitcast_dynamic-update-slice_fusion.3), channel_id=1, source_target_pairs={{0,1},{1,0},{2,3},{3,2},{4,5},{5,4},{6,7},{7,6},{8,9},{9,8},{10,11... | collective-permute-start | bytes 6291464 | tf_op jit(solution)/shard_map/ppermute | solution.py:107
  162.2 29.0 %copy-start.95 = (f32[1024]{0:T(1024)}, f32[1024]{0:T(1024)S(1)}, u32[]{:S(2)}) copy-start(f32[1024]{0:T(1024)S(1)} %broadcast_multiply_fusion.1) | copy-start | bytes 12292
  162.7 28.6 %copy-start.104 = (f32[1024]{0:T(1024)}, f32[1024]{0:T(1024)S(1)}, u32[]{:S(2)}) copy-start(f32[1024]{0:T(1024)S(1)} %fusion.131) | copy-start | bytes 12292
  230.8 20.1 %copy-start.16 = (f32[1024,2048]{1,0:T(8,128)}, f32[1024,2048]{1,0:T(8,128)S(1)}, u32[]{:S(2)}) copy-start(f32[1024,2048]{1,0:T(8,128)S(1)} %get-tuple-element.278) | copy-start | bytes 25165828
  230.8 27.5 %copy-start.38 = (f32[1024,2048]{1,0:T(8,128)}, f32[1024,2048]{1,0:T(8,128)S(1)}, u32[]{:S(2)}) copy-start(f32[1024,2048]{1,0:T(8,128)S(1)} %get-tuple-element.277) | copy-start | bytes 25165828
  299.9 11.9 %copy-start.17 = (bf16[4,512,8,64]{1,0,3,2:T(4,128)(2,1)S(1)}, bf16[4,512,8,64]{1,0,3,2:T(4,128)(2,1)}, u32[]{:S(2)}) copy-start(bf16[4,512,8,64]{1,0,3,2:T(4,128)(2,1)} %reshape.696) | copy-start | bytes 6291460
  329.0 11.5 %slice-start = ((s8[8388608]{0:T(1024)(128)(4,1)}), s8[4194304]{0:T(1024)(128)(4,1)S(1)}, s32[]{:S(2)}) async-start(s8[8388608]{0:T(1024)(128)(4,1)} %bitcast.517), calls=%async_computation.1 | async-start | bytes 8388608
  344.3 10.8 %slice-start.4 = ((s8[8388608]{0:T(1024)(128)(4,1)}), s8[4194304]{0:T(1024)(128)(4,1)S(1)}, s32[]{:S(2)}) async-start(s8[8388608]{0:T(1024)(128)(4,1)} %bitcast.532), calls=%async_computation.5 | async-start | bytes 8388608
  387.1 68.6 %collective-permute-start.35 = (bf16[4,4,128,512]{3,2,1,0:T(8,128)(2,1)}, bf16[4,4,128,512]{3,2,1,0:T(8,128)(2,1)}, u32[]{:S(2)}, u32[]{:S(2)}) collective-permute-start(bf16[4,4,128,512]{3,2,1,0:T(8,128)(2,1)} %fusion.49), channel_id=1, source_target_pairs={{0,1},{1,0},{2,3},{3,2},{4,5},{5,4},{6,7},{7,6},{8,9},{9,8},{10,11... | collective-permute-start | bytes 6291464 | tf_op jit(solution)/shard_map/ppermute | solution.py:107
  406.1 23.8 %collective-permute-start.28 = (bf16[4,4,64,512]{3,2,1,0:T(8,128)(2,1)}, bf16[4,4,64,512]{3,2,1,0:T(8,128)(2,1)}, u32[]{:S(2)}, u32[]{:S(2)}) collective-permute-start(bf16[4,4,64,512]{3,2,1,0:T(8,128)(2,1)} %fusion.95), channel_id=1, source_target_pairs={{0,1},{1,0},{2,3},{3,2},{4,5},{5,4},{6,7},{7,6},{8,9},{9,8},{10,11... | collective-permute-start | bytes 3145736 | tf_op jit(solution)/shard_map/ppermute | solution.py:107
  422.5 12.8 %collective-permute-start.21 = (bf16[4,4,65,512]{3,1,2,0:T(4,128)(2,1)S(1)}, bf16[4,4,65,512]{3,1,2,0:T(4,128)(2,1)S(1)}, u32[]{:S(2)}, u32[]{:S(2)}) collective-permute-start(bf16[4,4,65,512]{3,1,2,0:T(4,128)(2,1)S(1)} %copy.974), channel_id=1, source_target_pairs={{0,1},{1,0},{2,3},{3,2},{4,5},{5,4},{6,7},{7,6},{8,9},{9,8},{10,11... | collective-permute-start | bytes 3194888 | tf_op jit(solution)/shard_map/ppermute | solution.py:107
  431.7 9.2 %collective-permute-start.29 = (bf16[4,64,512]{2,1,0:T(8,128)(2,1)S(1)}, bf16[4,64,512]{2,1,0:T(8,128)(2,1)S(1)}, u32[]{:S(2)}, u32[]{:S(2)}) collective-permute-start(bf16[4,64,512]{2,1,0:T(8,128)(2,1)S(1)} %get-tuple-element.222), channel_id=1, source_target_pairs={{0,2},{1,3},{2,0},{3,1},{4,6},{5,7},{6,4},{7,5},{8,10},{9,11},{10,... | collective-permute-start | bytes 786440 | tf_op jit(solution)/shard_map/ppermute | solution.py:107
  433.3 13.9 %collective-permute-start.31 = (bf16[4,64,512]{2,1,0:T(8,128)(2,1)S(1)}, bf16[4,64,512]{2,1,0:T(8,128)(2,1)S(1)}, u32[]{:S(2)}, u32[]{:S(2)}) collective-permute-start(bf16[4,64,512]{2,1,0:T(8,128)(2,1)S(1)} %get-tuple-element.223), channel_id=1, source_target_pairs={{0,6},{1,7},{2,4},{3,5},{4,2},{5,3},{6,0},{7,1},{8,14},{9,15},{10,... | collective-permute-start | bytes 786440 | tf_op jit(solution)/shard_map/ppermute | solution.py:107
  434.3 20.5 %collective-permute-start.30 = (bf16[4,64,512]{2,1,0:T(8,128)(2,1)S(1)}, bf16[4,64,512]{2,1,0:T(8,128)(2,1)S(1)}, u32[]{:S(2)}, u32[]{:S(2)}) collective-permute-start(bf16[4,64,512]{2,1,0:T(8,128)(2,1)S(1)} %get-tuple-element.224), channel_id=1, source_target_pairs={{0,4},{1,5},{2,6},{3,7},{4,0},{5,1},{6,2},{7,3},{8,12},{9,13},{10,... | collective-permute-start | bytes 786440 | tf_op jit(solution)/shard_map/ppermute | solution.py:107
  436.9 22.1 %copy-start.21 = (f32[4,4,2,64,512]{4,3,2,1,0:T(8,128)S(1)}, f32[4,4,2,64,512]{4,3,2,1,0:T(8,128)}, u32[]{:S(2)}) copy-start(f32[4,4,2,64,512]{4,3,2,1,0:T(8,128)} %copy-done.20) | copy-start | bytes 12582916
  438.5 20.4 %copy-start.9 = (f32[4,4,2,64,512]{4,3,2,1,0:T(8,128)S(1)}, f32[4,4,2,64,512]{4,3,2,1,0:T(8,128)}, u32[]{:S(2)}) copy-start(f32[4,4,2,64,512]{4,3,2,1,0:T(8,128)} %concatenate.78) | copy-start | bytes 12582916
  438.8 22.7 %collective-permute-start.23 = (bf16[4,65,512]{2,0,1:T(4,128)(2,1)S(1)}, bf16[4,65,512]{2,0,1:T(4,128)(2,1)S(1)}, u32[]{:S(2)}, u32[]{:S(2)}) collective-permute-start(bf16[4,65,512]{2,0,1:T(4,128)(2,1)S(1)} %bitcast.599), channel_id=1, source_target_pairs={{0,4},{1,5},{2,6},{3,7},{4,0},{5,1},{6,2},{7,3},{8,12},{9,13},{10,... | collective-permute-start | bytes 798728 | tf_op jit(solution)/shard_map/ppermute | solution.py:107
  440.9 21.4 %collective-permute-start.24 = (bf16[4,65,512]{2,0,1:T(4,128)(2,1)S(1)}, bf16[4,65,512]{2,0,1:T(4,128)(2,1)S(1)}, u32[]{:S(2)}, u32[]{:S(2)}) collective-permute-start(bf16[4,65,512]{2,0,1:T(4,128)(2,1)S(1)} %bitcast.598), channel_id=1, source_target_pairs={{0,6},{1,7},{2,4},{3,5},{4,2},{5,3},{6,0},{7,1},{8,14},{9,15},{10,... | collective-permute-start | bytes 798728 | tf_op jit(solution)/shard_map/ppermute | solution.py:107
  447.2 16.7 %collective-permute-start.22 = (bf16[4,65,512]{2,0,1:T(4,128)(2,1)S(1)}, bf16[4,65,512]{2,0,1:T(4,128)(2,1)S(1)}, u32[]{:S(2)}, u32[]{:S(2)}) collective-permute-start(bf16[4,65,512]{2,0,1:T(4,128)(2,1)S(1)} %bitcast.597), channel_id=1, source_target_pairs={{0,2},{1,3},{2,0},{3,1},{4,6},{5,7},{6,4},{7,5},{8,10},{9,11},{10,... | collective-permute-start | bytes 798728 | tf_op jit(solution)/shard_map/ppermute | solution.py:107
  455.1 10.9 %collective-permute-start.32 = (bf16[64,512]{1,0:T(8,128)(2,1)S(1)}, bf16[64,512]{1,0:T(8,128)(2,1)S(1)}, u32[]{:S(2)}, u32[]{:S(2)}) collective-permute-start(bf16[64,512]{1,0:T(8,128)(2,1)S(1)} %get-tuple-element.241), channel_id=1, source_target_pairs={{0,8},{1,9},{2,10},{3,11},{4,12},{5,13},{6,14},{7,15},{8,0},{9,1},... | collective-permute-start | bytes 196616 | tf_op jit(solution)/shard_map/ppermute | solution.py:107
  455.7 10.9 %collective-permute-start.34 = (bf16[64,512]{1,0:T(8,128)(2,1)S(1)}, bf16[64,512]{1,0:T(8,128)(2,1)S(1)}, u32[]{:S(2)}, u32[]{:S(2)}) collective-permute-start(bf16[64,512]{1,0:T(8,128)(2,1)S(1)} %get-tuple-element.242), channel_id=1, source_target_pairs={{0,24},{1,25},{2,26},{3,27},{4,28},{5,29},{6,30},{7,31},{8,16},{9,... | collective-permute-start | bytes 196616 | tf_op jit(solution)/shard_map/ppermute | solution.py:107
  461.6 14.9 %collective-permute-start.36 = (bf16[4,128,512]{2,1,0:T(8,128)(2,1)S(1)}, bf16[4,128,512]{2,1,0:T(8,128)(2,1)S(1)}, u32[]{:S(2)}, u32[]{:S(2)}) collective-permute-start(bf16[4,128,512]{2,1,0:T(8,128)(2,1)S(1)} %get-tuple-element.210), channel_id=1, source_target_pairs={{0,2},{1,3},{2,0},{3,1},{4,6},{5,7},{6,4},{7,5},{8,10},{9,11},{10,... | collective-permute-start | bytes 1572872 | tf_op jit(solution)/shard_map/ppermute | solution.py:107
  462.4 21.1 %collective-permute-start.38 = (bf16[4,128,512]{2,1,0:T(8,128)(2,1)S(1)}, bf16[4,128,512]{2,1,0:T(8,128)(2,1)S(1)}, u32[]{:S(2)}, u32[]{:S(2)}) collective-permute-start(bf16[4,128,512]{2,1,0:T(8,128)(2,1)S(1)} %get-tuple-element.211), channel_id=1, source_target_pairs={{0,6},{1,7},{2,4},{3,5},{4,2},{5,3},{6,0},{7,1},{8,14},{9,15},{10,... | collective-permute-start | bytes 1572872 | tf_op jit(solution)/shard_map/ppermute | solution.py:107
  463.9 21.0 %collective-permute-start.37 = (bf16[4,128,512]{2,1,0:T(8,128)(2,1)S(1)}, bf16[4,128,512]{2,1,0:T(8,128)(2,1)S(1)}, u32[]{:S(2)}, u32[]{:S(2)}) collective-permute-start(bf16[4,128,512]{2,1,0:T(8,128)(2,1)S(1)} %get-tuple-element.212), channel_id=1, source_target_pairs={{0,4},{1,5},{2,6},{3,7},{4,0},{5,1},{6,2},{7,3},{8,12},{9,13},{10,... | collective-permute-start | bytes 1572872 | tf_op jit(solution)/shard_map/ppermute | solution.py:107
  465.9 7.5 %collective-permute-start.33 = (bf16[64,512]{1,0:T(8,128)(2,1)S(1)}, bf16[64,512]{1,0:T(8,128)(2,1)S(1)}, u32[]{:S(2)}, u32[]{:S(2)}) collective-permute-start(bf16[64,512]{1,0:T(8,128)(2,1)S(1)} %get-tuple-element.243), channel_id=1, source_target_pairs={{0,16},{1,17},{2,18},{3,19},{4,20},{5,21},{6,22},{7,23},{8,24},{9,... | collective-permute-start | bytes 196616 | tf_op jit(solution)/shard_map/ppermute | solution.py:107
  466.6 22.6 %collective-permute-start.26 = (bf16[65,512]{1,0:T(8,128)(2,1)S(1)}, bf16[65,512]{1,0:T(8,128)(2,1)S(1)}, u32[]{:S(2)}, u32[]{:S(2)}) collective-permute-start(bf16[65,512]{1,0:T(8,128)(2,1)S(1)} %bitcast.602), channel_id=1, source_target_pairs={{0,16},{1,17},{2,18},{3,19},{4,20},{5,21},{6,22},{7,23},{8,24},{9,... | collective-permute-start | bytes 199688 | tf_op jit(solution)/shard_map/ppermute | solution.py:107
  473.5 16.2 %collective-permute-start.27 = (bf16[65,512]{1,0:T(8,128)(2,1)S(1)}, bf16[65,512]{1,0:T(8,128)(2,1)S(1)}, u32[]{:S(2)}, u32[]{:S(2)}) collective-permute-start(bf16[65,512]{1,0:T(8,128)(2,1)S(1)} %bitcast.601), channel_id=1, source_target_pairs={{0,24},{1,25},{2,26},{3,27},{4,28},{5,29},{6,30},{7,31},{8,16},{9,... | collective-permute-start | bytes 199688 | tf_op jit(solution)/shard_map/ppermute | solution.py:107
  473.5 16.3 %copy-start.58 = (f32[64,512]{1,0:T(8,128)}, f32[64,512]{1,0:T(8,128)S(1)}, u32[]{:S(2)}) copy-start(f32[64,512]{1,0:T(8,128)S(1)} %fusion.126) | copy-start | bytes 393220
  476.5 13.2 %collective-permute-start.25 = (bf16[65,512]{1,0:T(8,128)(2,1)S(1)}, bf16[65,512]{1,0:T(8,128)(2,1)S(1)}, u32[]{:S(2)}, u32[]{:S(2)}) collective-permute-start(bf16[65,512]{1,0:T(8,128)(2,1)S(1)} %bitcast.600), channel_id=1, source_target_pairs={{0,8},{1,9},{2,10},{3,11},{4,12},{5,13},{6,14},{7,15},{8,0},{9,1},... | collective-permute-start | bytes 199688 | tf_op jit(solution)/shard_map/ppermute | solution.py:107
  485.5 5.5 %collective-permute-start.39 = (bf16[128,512]{1,0:T(8,128)(2,1)S(1)}, bf16[128,512]{1,0:T(8,128)(2,1)S(1)}, u32[]{:S(2)}, u32[]{:S(2)}) collective-permute-start(bf16[128,512]{1,0:T(8,128)(2,1)S(1)} %get-tuple-element.235), channel_id=1, source_target_pairs={{0,8},{1,9},{2,10},{3,11},{4,12},{5,13},{6,14},{7,15},{8,0},{9,1},... | collective-permute-start | bytes 393224 | tf_op jit(solution)/shard_map/ppermute | solution.py:107
  486.1 7.5 %collective-permute-start.41 = (bf16[128,512]{1,0:T(8,128)(2,1)S(1)}, bf16[128,512]{1,0:T(8,128)(2,1)S(1)}, u32[]{:S(2)}, u32[]{:S(2)}) collective-permute-start(bf16[128,512]{1,0:T(8,128)(2,1)S(1)} %get-tuple-element.236), channel_id=1, source_target_pairs={{0,24},{1,25},{2,26},{3,27},{4,28},{5,29},{6,30},{7,31},{8,16},{9,... | collective-permute-start | bytes 393224 | tf_op jit(solution)/shard_map/ppermute | solution.py:107
  489.2 8.7 %collective-permute-start.40 = (bf16[128,512]{1,0:T(8,128)(2,1)S(1)}, bf16[128,512]{1,0:T(8,128)(2,1)S(1)}, u32[]{:S(2)}, u32[]{:S(2)}) collective-permute-start(bf16[128,512]{1,0:T(8,128)(2,1)S(1)} %get-tuple-element.237), channel_id=1, source_target_pairs={{0,16},{1,17},{2,18},{3,19},{4,20},{5,21},{6,22},{7,23},{8,24},{9,... | collective-permute-start | bytes 393224 | tf_op jit(solution)/shard_map/ppermute | solution.py:107
  501.9 12.3 %all-to-all-start = ((f32[32,8,128]{2,1,0:T(8,128)}), f32[32,8,128]{2,1,0:T(8,128)}, u32[]{:S(2)}, u32[]{:S(2)}) async-start(f32[32,8,128]{2,1,0:T(8,128)} %broadcast_in_dim.213), calls=%async_computation | async-start | bytes 262144 | tf_op jit(solution)/shard_map/all_to_all | solution.py:362
  510.4 13.7 %copy-start.76 = (f32[16,2048]{1,0:T(8,128)S(1)}, f32[16,2048]{1,0:T(8,128)}, u32[]{:S(2)}) copy-start(f32[16,2048]{1,0:T(8,128)} %param.23) | copy-start | bytes 393220
  510.4 13.7 %copy-start.90 = (f32[16,2048]{1,0:T(8,128)S(1)}, f32[16,2048]{1,0:T(8,128)}, u32[]{:S(2)}) copy-start(f32[16,2048]{1,0:T(8,128)} %param.29) | copy-start | bytes 393220
  510.4 13.7 %copy-start.91 = (f32[16,2048]{1,0:T(8,128)S(1)}, f32[16,2048]{1,0:T(8,128)}, u32[]{:S(2)}) copy-start(f32[16,2048]{1,0:T(8,128)} %param.28) | copy-start | bytes 393220
  (113 other events, 368.7 us)

commit v2 on v1

v2 whole, which is shorter than its diff:
```python
import jax
import jax.numpy as jnp
from jax import lax
from jax.experimental import pallas as pl
from jax.experimental.pallas import tpu as pltpu
from jax.sharding import PartitionSpec as P

HEADS = 8
HEAD_DIM = 64
STEP = 5
PAIR = 2 * HEAD_DIM
SCALE = HEAD_DIM ** (-0.5)
LOW = jnp.bfloat16
F32 = jnp.float32
LIMIT = 60 * 1024 * 1024


def dot_nn(left, right):
    return lax.dot_general(left, right, (((1,), (0,)), ((), ())), preferred_element_type=F32)


def dot_nt(left, right):
    return lax.dot_general(left, right, (((1,), (1,)), ((), ())), preferred_element_type=F32)


def dot_tn(left, right):
    return lax.dot_general(left, right, (((0,), (0,)), ((), ())), preferred_element_type=F32)


def normalize(values):
    center = values - jnp.mean(values, -1, keepdims=True)
    inverse = lax.rsqrt(jnp.mean(center * center, -1, keepdims=True) + 1e-05)
    return center * inverse, inverse


def normalize_back(grad, hat, inverse, gain):
    grad_hat = grad * (1.0 + gain)
    first = jnp.mean(grad_hat, -1, keepdims=True)
    second = jnp.mean(grad_hat * hat, -1, keepdims=True)
    return inverse * (grad_hat - first - hat * second)


def column_sum(values):
    return jnp.sum(values.astype(F32), 0, keepdims=True)


def half_of(pair, odd):
    lane = lax.broadcasted_iota(jnp.int32, pair.shape, 1)
    keep = lane >= HEAD_DIM if odd else lane < HEAD_DIM
    return jnp.where(keep, pair, jnp.zeros_like(pair))


def self_bias(size, count):
    key = lax.broadcasted_iota(jnp.int32, (size, size), 0)
    query = lax.broadcasted_iota(jnp.int32, (size, size), 1)
    return jnp.where((key <= query) & (key < count), 0.0, -1e30)


def cross_bias(keys, queries, count):
    key = lax.broadcasted_iota(jnp.int32, (keys, queries), 0)
    return jnp.where(key < count, 0.0, -1e30)


def attend(query, key, value, bias_ref, mixed_ref, lse_ref):
    value_t = value.T
    for pair in range(HEADS // 2):
        cols = slice(pair * PAIR, (pair + 1) * PAIR)
        query_pair, key_pair = query[:, cols] * SCALE, key[:, cols]
        for odd in range(2):
            head = 2 * pair + odd
            rows = slice(head * HEAD_DIM, (head + 1) * HEAD_DIM)
            scores = dot_nt(half_of(key_pair, odd), query_pair) + bias_ref[...]
            top = jnp.max(scores, 0, keepdims=True)
            expo = jnp.exp(scores - top)
            total = jnp.sum(expo, 0, keepdims=True)
            probs = (expo * (1.0 / total)).astype(LOW)
            mixed_ref[rows] = dot_nn(value_t[rows], probs)
            lse_ref[0, head : head + 1] = top + jnp.log(total)


def attend_back(query_ref, key_ref, value_ref, grad, bias_ref, lse_ref, gq_ref, gk_ref, gv_ref):
    key_t = key_ref[0].T
    for pair in range(HEADS // 2):
        cols = slice(pair * PAIR, (pair + 1) * PAIR)
        query_pair = query_ref[0, :, cols] * SCALE
        key_pair, value_pair, grad_pair = key_ref[0, :, cols], value_ref[0, :, cols], grad[:, cols]
        grad_key = grad_value = None
        for odd in range(2):
            head = 2 * pair + odd
            rows = slice(head * HEAD_DIM, (head + 1) * HEAD_DIM)
            scores = dot_nt(half_of(key_pair, odd), query_pair) + bias_ref[...]
            probs = jnp.exp(scores - lse_ref[0, head : head + 1])
            grad_probs = dot_nt(half_of(value_pair, odd), grad_pair)
            inner = jnp.sum(probs * grad_probs, 0, keepdims=True)
            grad_scores = (probs * (grad_probs - inner)).astype(LOW)
            to_value = dot_nn(probs.astype(LOW), half_of(grad_pair, odd))
            to_key = dot_nn(grad_scores, half_of(query_pair, odd))
            grad_value = to_value if grad_value is None else grad_value + to_value
            grad_key = to_key if grad_key is None else grad_key + to_key
            gq_ref[rows] = dot_nn(key_t[rows], grad_scores)
        gk_ref[:, cols] = grad_key.astype(LOW)
        gv_ref[:, cols] = grad_value.astype(LOW)


def self_forward_kernel(
    count_ref, x_ref, w_ref, table_ref,
    act_ref, query_ref, key_ref, value_ref, mixed_ref, lse_ref, out_ref,
    bias, mixed_t,
):
    bias[...] = self_bias(bias.shape[0], count_ref[pl.program_id(0)])
    x = x_ref[0].astype(F32)
    hat, _ = normalize(x)
    act = (hat * (1.0 + table_ref[0:1]) + table_ref[1:2]).astype(LOW)
    act_ref[0] = act
    query = (dot_nn(act, w_ref[0]) + table_ref[6:7]).astype(LOW)
    key = dot_nn(act, w_ref[1]).astype(LOW)
    value = (dot_nn(act, w_ref[2]) + table_ref[7:8]).astype(LOW)
    query_ref[0], key_ref[0], value_ref[0] = query, key, value
    attend(query, key, value, bias, mixed_t, lse_ref)
    mixed = mixed_t[...].T.astype(LOW)
    mixed_ref[0] = mixed
    out_ref[0] = x + dot_nn(mixed, w_ref[3]) + table_ref[8:9]


def cross_forward_kernel(
    count_ref, x_ref, mem_ref, w_ref, table_ref,
    act_ref, query_ref, key_ref, value_ref, mixed_ref, lse_ref, out_ref,
    bias, mixed_t,
):
    bias[...] = cross_bias(*bias.shape, count_ref[pl.program_id(0)])
    x = x_ref[0]
    hat, _ = normalize(x)
    act = (hat * (1.0 + table_ref[2:3]) + table_ref[3:4]).astype(LOW)
    act_ref[0] = act
    query = (dot_nn(act, w_ref[0]) + table_ref[9:10]).astype(LOW)
    key = dot_nn(mem_ref[0], w_ref[1]).astype(LOW)
    value = (dot_nn(mem_ref[0], w_ref[2]) + table_ref[10:11]).astype(LOW)
    query_ref[0], key_ref[0], value_ref[0] = query, key, value
    attend(query, key, value, bias, mixed_t, lse_ref)
    mixed = mixed_t[...].T.astype(LOW)
    mixed_ref[0] = mixed
    out_ref[0] = x + dot_nn(mixed, w_ref[3]) + table_ref[11:12]


def ffn_kernel(
    count_ref, x_ref, cot_ref, w_in_ref, w_out_ref, table_ref, bias_ref,
    out_ref, grad_ref, gw_in_ref, gw_out_ref, gb_in_ref, small_ref,
    act, gf, hidden, gpre, back,
):
    step = pl.program_id(0)
    seqs, length, width = x_ref.shape

    def valid(seq):
        row = lax.broadcasted_iota(jnp.int32, (length, 1), 0)
        return (row < count_ref[seq]).astype(F32)

    @pl.when(step == 0)
    def _():
        small_ref[...] = jnp.zeros_like(small_ref)
        for seq in range(seqs):
            x = x_ref[seq]
            hat, _ = normalize(x)
            act[seq] = (hat * (1.0 + table_ref[4:5]) + table_ref[5:6]).astype(LOW)
            grad = (cot_ref[seq].astype(F32) * valid(seq)).astype(LOW)
            gf[seq] = grad
            small_ref[2:3] += column_sum(grad)
            out_ref[seq] = x + table_ref[12:13]
            back[seq] = jnp.zeros_like(back[seq])

    sums = jnp.zeros((1, w_in_ref.shape[1]), F32)
    for seq in range(seqs):
        pre = dot_nn(act[seq], w_in_ref[...]) + bias_ref[...]
        cdf = 0.5 + 0.5 * lax.erf(pre * 0.5**0.5)
        slope = cdf + pre * (jnp.exp(pre * pre * -0.5) * 0.3989422804014327)
        unit = (pre * cdf).astype(LOW)
        hidden[seq] = unit
        grad_pre = (dot_nt(gf[seq], w_out_ref[...]) * slope).astype(LOW)
        gpre[seq] = grad_pre
        sums += column_sum(grad_pre)
        out_ref[seq] += dot_nn(unit, w_out_ref[...])
        back[seq] += dot_nt(grad_pre, w_in_ref[...])
    gb_in_ref[...] = sums
    tokens = seqs * length
    hidden_all, gf_all = hidden[...].reshape(tokens, -1), gf[...].reshape(tokens, -1)
    act_all, gpre_all = act[...].reshape(tokens, -1), gpre[...].reshape(tokens, -1)
    gw_out_ref[...] = dot_tn(hidden_all, gf_all).astype(gw_out_ref.dtype)
    gw_in_ref[...] = dot_tn(act_all, gpre_all).astype(gw_in_ref.dtype)

    @pl.when(step == pl.num_programs(0) - 1)
    def _():
        for seq in range(seqs):
            hat, inverse = normalize(x_ref[seq])
            grad = back[seq]
            small_ref[0:1] += column_sum(grad * hat)
            small_ref[1:2] += column_sum(grad)
            grad_ref[seq] = cot_ref[seq].astype(F32) * valid(seq) + normalize_back(
                grad, hat, inverse, table_ref[4:5]
            )


def cross_back_kernel(
    count_ref, grad_ref, x_ref, act_ref, mem_ref, query_ref, key_ref, value_ref, mixed_ref, lse_ref,
    w_ref, table_ref,
    out_ref, gmem_ref, gw_ref, small_ref,
    bias, gq_t, gk, gv,
):
    step = pl.program_id(0)

    @pl.when(step == 0)
    def _():
        gw_ref[...] = jnp.zeros_like(gw_ref)
        small_ref[...] = jnp.zeros_like(small_ref)

    bias[...] = cross_bias(*bias.shape, count_ref[step])
    grad = grad_ref[0]
    low = grad.astype(LOW)
    gw_ref[3] += dot_tn(mixed_ref[0], low)
    small_ref[4:5] += column_sum(low)
    grad_mixed = dot_nt(low, w_ref[3]).astype(LOW)
    attend_back(query_ref, key_ref, value_ref, grad_mixed, bias, lse_ref, gq_t, gk, gv)
    gq = (gq_t[...] * SCALE).T.astype(LOW)
    small_ref[2:3] += column_sum(gq)
    small_ref[3:4] += column_sum(gv[...])
    gw_ref[0] += dot_tn(act_ref[0], gq)
    gw_ref[1] += dot_tn(mem_ref[0], gk[...])
    gw_ref[2] += dot_tn(mem_ref[0], gv[...])
    gmem_ref[0] = dot_nt(gk[...], w_ref[1]) + dot_nt(gv[...], w_ref[2])
    back = dot_nt(gq, w_ref[0])
    hat, inverse = normalize(x_ref[0])
    small_ref[0:1] += column_sum(back * hat)
    small_ref[1:2] += column_sum(back)
    out_ref[0] = grad + normalize_back(back, hat, inverse, table_ref[2:3])


def self_back_kernel(
    count_ref, grad_ref, x_ref, act_ref, query_ref, key_ref, value_ref, mixed_ref, lse_ref,
    w_ref, table_ref,
    out_ref, gw_ref, small_ref,
    bias, gq_t, gk, gv,
):
    step = pl.program_id(0)

    @pl.when(step == 0)
    def _():
        gw_ref[...] = jnp.zeros_like(gw_ref)
        small_ref[...] = jnp.zeros_like(small_ref)

    bias[...] = self_bias(bias.shape[0], count_ref[step])
    grad = grad_ref[0]
    low = grad.astype(LOW)
    gw_ref[3] += dot_tn(mixed_ref[0], low)
    small_ref[4:5] += column_sum(low)
    grad_mixed = dot_nt(low, w_ref[3]).astype(LOW)
    attend_back(query_ref, key_ref, value_ref, grad_mixed, bias, lse_ref, gq_t, gk, gv)
    gq = (gq_t[...] * SCALE).T.astype(LOW)
    small_ref[2:3] += column_sum(gq)
    small_ref[3:4] += column_sum(gv[...])
    gw_ref[0] += dot_tn(act_ref[0], gq)
    gw_ref[1] += dot_tn(act_ref[0], gk[...])
    gw_ref[2] += dot_tn(act_ref[0], gv[...])
    back = dot_nt(gq, w_ref[0]) + dot_nt(gk[...], w_ref[1]) + dot_nt(gv[...], w_ref[2])
    hat, inverse = normalize(x_ref[0].astype(F32))
    small_ref[0:1] += column_sum(back * hat)
    small_ref[1:2] += column_sum(back)
    out_ref[0] = grad + normalize_back(back, hat, inverse, table_ref[0:1])


def by_seq(*tail):
    return pl.BlockSpec((1,) + tail, lambda seq, *_: (seq,) + (0,) * len(tail))


def fixed(*shape):
    return pl.BlockSpec(shape, lambda *_: (0,) * len(shape))


def call(kernel, name, grid, counts, args, in_specs, outs, out_specs, scratch):
    return pl.pallas_call(
        kernel,
        out_shape=[jax.ShapeDtypeStruct(*out) for out in outs],
        grid_spec=pltpu.PrefetchScalarGridSpec(
            num_scalar_prefetch=1, grid=grid, in_specs=in_specs, out_specs=out_specs, scratch_shapes=scratch
        ),
        compiler_params=pltpu.CompilerParams(vmem_limit_bytes=LIMIT),
        name=name,
    )(counts, *args)


def self_forward(lengths, x, weights, table):
    seqs, length, width = x.shape
    shape = (seqs, length, width)
    block = by_seq(length, width)
    return call(
        self_forward_kernel, "self_forward", (seqs,), lengths, (x, weights, table),
        [block, fixed(4, width, width), fixed(*table.shape)],
        [(shape, LOW)] * 5 + [((seqs, HEADS, length), F32), (shape, F32)],
        [block] * 5 + [by_seq(HEADS, length), block],
        [pltpu.VMEM((length, length), F32), pltpu.VMEM((width, length), F32)],
    )


def cross_forward(mem_lengths, x, memory, weights, table):
    seqs, length, width = x.shape
    mem_len = memory.shape[1]
    block, mem_block = by_seq(length, width), by_seq(mem_len, width)
    shape, mem_shape = x.shape, memory.shape
    return call(
        cross_forward_kernel, "cross_forward", (seqs,), mem_lengths, (x, memory, weights, table),
        [block, mem_block, fixed(4, width, width), fixed(*table.shape)],
        [(shape, LOW), (shape, LOW), (mem_shape, LOW), (mem_shape, LOW), (shape, LOW), ((seqs, HEADS, length), F32), (shape, F32)],
        [block, block, mem_block, mem_block, block, by_seq(HEADS, length), block],
        [pltpu.VMEM((mem_len, length), F32), pltpu.VMEM((width, length), F32)],
    )


def ffn(lengths, x, cotangent, w_in, w_out, table, grad_type=LOW):
    seqs, length, width = x.shape
    hidden = w_in.shape[1]
    chunk = 512
    bias = table[13:].reshape(1, hidden)
    act = pltpu.VMEM((seqs, length, width), LOW)
    wide = pltpu.VMEM((seqs, length, chunk), LOW)
    cols = pl.BlockSpec((width, chunk), lambda i, *_: (0, i))
    rows = pl.BlockSpec((chunk, width), lambda i, *_: (i, 0))
    flat = pl.BlockSpec((1, chunk), lambda i, *_: (0, i))
    return call(
        ffn_kernel, "ffn", (hidden // chunk,), lengths, (x, cotangent, w_in, w_out, table, bias),
        [fixed(*x.shape), fixed(*x.shape), cols, rows, fixed(*table.shape), flat],
        [(x.shape, F32), (x.shape, F32), (w_in.shape, grad_type), (w_out.shape, grad_type), ((1, hidden), F32), ((8, width), F32)],
        [fixed(*x.shape), fixed(*x.shape), cols, rows, flat, fixed(8, width)],
        [act, act, wide, wide, pltpu.VMEM((seqs, length, width), F32)],
    )


def cross_back(mem_lengths, grad, x, act, memory, query, key, value, mixed, lse, weights, table):
    seqs, length, width = x.shape
    mem_len = memory.shape[1]
    block, mem_block = by_seq(length, width), by_seq(mem_len, width)
    return call(
        cross_back_kernel, "cross_back", (seqs,), mem_lengths,
        (grad, x, act, memory, query, key, value, mixed, lse, weights, table),
        [block, block, block, mem_block, block, mem_block, mem_block, block, by_seq(HEADS, length),
         fixed(4, width, width), fixed(*table.shape)],
        [(x.shape, F32), (memory.shape, F32), (weights.shape, F32), ((8, width), F32)],
        [block, mem_block, fixed(4, width, width), fixed(8, width)],
        [pltpu.VMEM((mem_len, length), F32), pltpu.VMEM((width, length), F32),
         pltpu.VMEM((mem_len, width), LOW), pltpu.VMEM((mem_len, width), LOW)],
    )


def self_back(lengths, grad, x, act, query, key, value, mixed, lse, weights, table):
    seqs, length, width = x.shape
    block = by_seq(length, width)
    return call(
        self_back_kernel, "self_back", (seqs,), lengths,
        (grad, x, act, query, key, value, mixed, lse, weights, table),
        [block] * 7 + [by_seq(HEADS, length), fixed(4, width, width), fixed(*table.shape)],
        [(x.shape, F32), (weights.shape, F32), ((8, width), F32)],
        [block, fixed(4, width, width), fixed(8, width)],
        [pltpu.VMEM((length, length), F32), pltpu.VMEM((width, length), F32),
         pltpu.VMEM((length, width), LOW), pltpu.VMEM((length, width), LOW)],
    )


def adam_update(weight, grad, first, second, clip_scale, step, rate):
    clipped = grad * clip_scale
    first_new = 0.5 * first + 0.5 * clipped
    second_new = 0.55 * second + 0.45 * clipped * clipped
    fix_first = 1.0 - jnp.power(0.5, step)
    fix_second = 1.0 - jnp.power(0.55, step)
    weight_new = weight - rate * (
        first_new / fix_first / (jnp.sqrt(second_new / fix_second) + 1e-08) + 0.01 * weight
    )
    return (weight_new, first_new, second_new)


AXES = ("dp", "fsdp")


class Grid:
    def __init__(self, dp, fsdp):
        self.sizes = (dp, fsdp // 2, 2)
        self.strides = (fsdp, 2, 1)
        self.devices = dp * fsdp
        index = lax.axis_index("fsdp")
        self.place = (lax.axis_index("dp"), index // 2, index % 2)

    def swap(self, values, stage, step):
        stride = self.strides[stage]
        pairs = [(i, i ^ (step * stride)) for i in range(self.devices)]
        return lax.ppermute(values, AXES, pairs)

    def gather(self, chunk):
        held = chunk
        for stage in range(3):
            size, place = self.sizes[stage], self.place[stage]
            parts = [held] + [self.swap(held, stage, step) for step in range(1, size)]
            if size == 2:
                first = jnp.where(place == 0, parts[0], parts[1])
                second = jnp.where(place == 0, parts[1], parts[0])
                held = jnp.stack([first, second], stage)
            else:
                whole = jnp.zeros(held.shape[:stage] + (size,) + held.shape[stage:], held.dtype)
                for step in range(size):
                    whole = lax.dynamic_update_index_in_dim(whole, parts[step], place ^ step, stage)
                held = whole
        return held

    def scatter(self, parts):
        held = parts
        for stage in (2, 1, 0):
            size, place = self.sizes[stage], self.place[stage]
            total = lax.dynamic_index_in_dim(held, place, stage, False).astype(jnp.float32)
            for step in range(1, size):
                piece = lax.dynamic_index_in_dim(held, place ^ step, stage, False)
                total = total + self.swap(piece.astype(jnp.bfloat16), stage, step).astype(jnp.float32)
            held = total
        return held


def local(
    grid,
    inputs,
    memory,
    cotangent,
    lengths,
    mem_lengths,
    attn_weights,
    ffn_in,
    ffn_out,
    vectors,
    attn_first,
    attn_second,
    ffn_in_first,
    ffn_in_second,
    ffn_out_first,
    ffn_out_second,
    vector_first,
    vector_second,
):
    width = inputs.shape[2]
    own = attn_weights.shape[1]
    spots = grid.sizes

    def fold(array):
        return array.reshape(-1, width)

    vec_count = vectors.shape[0]
    table_rows = -(-vec_count * own // width)

    def fold_table(array, lead=()):
        flat = array.reshape(lead + (vec_count * own,))
        pad = [(0, 0)] * len(lead) + [(0, table_rows * width - vec_count * own)]
        return jnp.pad(flat, pad).reshape(lead + (table_rows, width))

    def attn_unfold(full):
        return jnp.moveaxis(full.reshape(grid.devices, -1, own, width), 1, 0).reshape(-1, width, width)

    low = jnp.bfloat16
    first_chunk = jnp.concatenate(
        [fold(attn_weights[:4].astype(low)), fold_table(vectors.astype(low))], 0
    )
    first_full = grid.gather(first_chunk)
    second_full = grid.gather(fold(attn_weights[4:].astype(low)))
    ffn_chunk = jnp.concatenate([ffn_out.astype(low), fold(ffn_in.astype(low))], 0)
    ffn_full = grid.gather(ffn_chunk)
    out_rows = ffn_out.shape[0]
    self_full = attn_unfold(first_full[..., : 4 * own, :])
    cross_full = attn_unfold(second_full)
    ffn_out_full = ffn_full[..., :out_rows, :].reshape(-1, width)
    ffn_in_full = ffn_full[..., out_rows:, :].reshape(width, -1)
    table_full = first_full[..., 4 * own :, :].reshape(grid.devices, table_rows * width)
    table_full = table_full[:, : vec_count * own].reshape(grid.devices, vec_count, own)
    table_full = jnp.moveaxis(table_full, 1, 0).reshape(vec_count, width)
    table = table_full.astype(jnp.float32)
    act_one, query_one, key_one, value_one, mixed_one, lse_one, resid_one = self_forward(
        lengths, inputs, self_full, table
    )
    act_two, query_two, key_two, value_two, mixed_two, lse_two, resid_two = cross_forward(
        mem_lengths, resid_one, memory, cross_full, table
    )
    output, grad_two, grad_ffn_in, grad_ffn_out, grad_in_bias, small_three = ffn(
        lengths, resid_two, cotangent, ffn_in_full, ffn_out_full, table
    )
    grad_one, grad_memory, grad_cross_stack, small_two = cross_back(
        mem_lengths, grad_two, resid_one, act_two, memory, query_two, key_two, value_two, mixed_two,
        lse_two, cross_full, table,
    )
    grad_input, grad_self_stack, small_one = self_back(
        lengths, grad_one, inputs, act_one, query_one, key_one, value_one, mixed_one, lse_one,
        self_full, table,
    )
    grad_table = jnp.concatenate(
        [
            small_one[0:2],
            small_two[0:2],
            small_three[0:2],
            small_one[2:5],
            small_two[2:5],
            small_three[2:3],
            grad_in_bias.reshape(-1, width),
        ],
        0,
    )

    def attn_fold(stack):
        parts = stack.reshape(4, grid.devices, own, width)
        return jnp.moveaxis(parts, 0, 1).reshape(grid.devices, 4 * own, width)

    grad_parts = jnp.moveaxis(grad_table.reshape(vec_count, grid.devices, own), 0, 1)
    last_parts = jnp.concatenate(
        [attn_fold(grad_self_stack), fold_table(grad_parts, (grid.devices,))], 1
    )
    ffn_parts = jnp.concatenate(
        [
            grad_ffn_out.reshape(grid.devices, -1, width),
            grad_ffn_in.reshape(grid.devices, -1, width),
        ],
        1,
    )

    def reduce(parts):
        return grid.scatter(parts.reshape(spots + parts.shape[1:]))

    ffn_share = reduce(ffn_parts)
    cross_share = reduce(attn_fold(grad_cross_stack))
    last_share = reduce(last_parts)
    self_share = last_share[: 4 * own].reshape(4, own, width)
    table_share = last_share[4 * own :].reshape(-1)[: vec_count * own].reshape(vec_count, own)
    shares = (
        jnp.concatenate([self_share, cross_share.reshape(4, own, width)], 0),
        ffn_share[out_rows:].reshape(ffn_in.shape),
        ffn_share[:out_rows],
        table_share,
    )
    local_squares = (
        jnp.sum(shares[0] * shares[0])
        + jnp.sum(shares[1] * shares[1])
        + jnp.sum(shares[2] * shares[2])
        + jnp.sum(shares[3] * shares[3])
    )
    spread = jnp.broadcast_to(local_squares, (grid.devices, 8, 128))
    total_squares = jnp.sum(lax.all_to_all(spread, AXES, 0, 0)[:, 0, 0])
    grad_norm = jnp.sqrt(total_squares)
    clip_scale = jnp.minimum(1.0, 1.0 / (grad_norm + 1e-06))
    step = jnp.float32(STEP)
    attn_new = adam_update(attn_weights, shares[0], attn_first, attn_second, clip_scale, step, 0.04)
    first_new = adam_update(ffn_in, shares[1], ffn_in_first, ffn_in_second, clip_scale, step, 0.04)
    second_new = adam_update(
        ffn_out, shares[2], ffn_out_first, ffn_out_second, clip_scale, step, 0.04
    )
    table_new = adam_update(vectors, shares[3], vector_first, vector_second, clip_scale, step, 0.25)
    return (
        output,
        grad_input,
        grad_memory,
        grad_norm.reshape(1),
        attn_new[0],
        attn_new[1],
        attn_new[2],
        first_new[0],
        first_new[1],
        first_new[2],
        second_new[0],
        second_new[1],
        second_new[2],
        table_new[0],
        table_new[1],
        table_new[2],
    )


def solution(mesh):
    def whole(*arrays):
        return local(Grid(mesh.shape["dp"], mesh.shape["fsdp"]), *arrays)

    return jax.shard_map(
        whole,
        mesh=mesh,
        in_specs=(
            P(("dp", "fsdp"), None, None),
            P(("dp", "fsdp"), None, None),
            P(("dp", "fsdp"), None, None),
            P(("dp", "fsdp")),
            P(("dp", "fsdp")),
            P(None, ("dp", "fsdp"), None),
            P(("dp", "fsdp"), None),
            P(("dp", "fsdp"), None),
            P(None, ("dp", "fsdp")),
            P(None, ("dp", "fsdp"), None),
            P(None, ("dp", "fsdp"), None),
            P(("dp", "fsdp"), None),
            P(("dp", "fsdp"), None),
            P(("dp", "fsdp"), None),
            P(("dp", "fsdp"), None),
            P(None, ("dp", "fsdp")),
            P(None, ("dp", "fsdp")),
        ),
        out_specs=(
            P(("dp", "fsdp"), None, None),
            P(("dp", "fsdp"), None, None),
            P(("dp", "fsdp"), None, None),
            P(),
            P(None, ("dp", "fsdp"), None),
            P(None, ("dp", "fsdp"), None),
            P(None, ("dp", "fsdp"), None),
            P(("dp", "fsdp"), None),
            P(("dp", "fsdp"), None),
            P(("dp", "fsdp"), None),
            P(("dp", "fsdp"), None),
            P(("dp", "fsdp"), None),
            P(("dp", "fsdp"), None),
            P(None, ("dp", "fsdp")),
            P(None, ("dp", "fsdp")),
            P(None, ("dp", "fsdp")),
        ),
        check_vma=False,
    )
```

time: 534 us -> 342 us (0.64)
  matrix products: 151 us -> 0 us
  Pallas kernels: 0 us -> 120 us
  local copies, waits for them, and re-layouts: 148 us -> 43.7 us
  other arithmetic: 99.5 us -> 27 us
  waiting for transfers between devices: 63.5 us -> 77 us
  starting transfers between devices: 55.9 us -> 62.8 us
    dot_general x42 -> x0, matrix products: 151 us -> none  [the longest x10 42.8 us: plain_dot(): return jnp.dot(left, right, preferred_element_type=jnp.float32)]
    pallas_call x0 -> x5, Pallas kernels: none -> 120 us  [call(): pl.pallas_call(kernel, out_shape=[jax.ShapeDtypeStruct(*out) for out in o...]
    reshape x14 -> x3, local copies, waits for them, and re-layouts: 45.2 us -> 5.98 us  [the longest x2 5.28 us: attn_fold(): parts = stack.reshape(4, grid.devices, own, width)]
    convert_element_type x4 -> x0, other arithmetic: 34.8 us -> none  [the longest x1 20 us: local(): hidden_low = hidden.astype(jnp.bfloat16)]
    unnamed x302 -> x51, local copies, waits for them, and re-layouts: 33.7 us -> 10 us
    convert_element_type x9 -> x0, local copies, waits for them, and re-layouts: 17.5 us -> none  [the longest x1 6.41 us: local(): hidden_low = hidden.astype(jnp.bfloat16)]
    reduce_sum x12 -> x0, other arithmetic: 15.3 us -> none  [the longest x2 5.75 us: attend_forward(): total = jnp.sum(expo, -1, keepdims=True)]
    ppermute x42, waiting for transfers between devices: 59.7 us -> 69 us  [swap(): return lax.ppermute(values, AXES, pairs)]
  transfers between devices with their start and end apart: 43 -> 43, of which waited for: 15 -> 19; matrix products, arithmetic and copies ran while one was open for 35% -> 13% of each run, Pallas kernels for 0% -> 13%
where the time goes in v2:
time: 342 us; the launch traced here: 337 us
  Pallas kernels  120 us (35%)
  waiting for transfers between devices  77 us (23%)
  starting transfers between devices  62.8 us (18%)
  local copies, waits for them, and re-layouts  43.7 us (13%)
  other arithmetic  27 us (8%)
  between operations  6.19 us (2%)
    pallas_call x5, Pallas kernels, call(): pl.pallas_call(kernel, out_shape=[jax.ShapeDtypeStruct(*out) for out in o...  120 us
    ppermute x42, waiting for transfers between devices, swap(): return lax.ppermute(values, AXES, pairs)  69 us
    ppermute x42, starting transfers between devices, swap(): return lax.ppermute(values, AXES, pairs)  58.8 us
    unnamed x51, local copies, waits for them, and re-layouts  10 us
    all_to_all x1, waiting for transfers between devices, local(): total_squares = jnp.sum(lax.all_to_all(spread, AXES, 0, 0)[:, 0, 0])  7.96 us
    another operation x6, other arithmetic, gather(): held = jnp.stack([first, second], stage)  7.26 us
  transfers between devices with their start and end apart: 43, of which 19 were waited for; matrix products, arithmetic and copies ran while one was open for 13% of the time, Pallas kernels for 13%

profile of v2, /device:TPU:0, one launch (start us, length us, event | category | flops | bytes accessed | tf_op | source)
XLA Modules:
  0.0 337.0 jit_solution(11144494290143211751)
XLA Ops:
  2.6 3.1 collective-permute-start.14
  5.6 2.6 collective-permute-start.15
  10.2 3.5 %collective-permute-start.8 = (bf16[64,512]{1,0:T(8,128)(2,1)S(1)}, bf16[64,512]{1,0:T(8,128)(2,1)S(1)}, u32[]{:S(2)}, u32[]{:S(2)}) collective-permute-start(bf16[64,512]{1,0:T(8,128)(2,1)S(1)} %bitcast.245), channel_id=1, source_target_pairs={{0,16},{1,17},{2,18},{3,19},{4,20},{5,21},{6,22},{7,23},{8,24},{9,... | collective-permute-start | bytes 196616 | tf_op jit(solution)/shard_map/ppermute | solution.py:390
  14.8 1.4 collective-permute-done.7
  16.2 3.3 collective-permute-start.9
  19.5 5.4 %collective-permute-done.8 = bf16[64,512]{1,0:T(8,128)(2,1)S(1)} collective-permute-done((bf16[64,512]{1,0:T(8,128)(2,1)S(1)}, bf16[64,512]{1,0:T(8,128)(2,1)S(1)}, u32[]{:S(2)}, u32[]{:S(2)}) %collective-permute-start.8) | collective-permute-done | bytes 65568 | tf_op jit(solution)/shard_map/ppermute | solution.py:390
  24.9 3.1 collective-permute-start.1
  29.2 2.5 collective-permute-start.2
  31.9 1.5 collective-permute-start.10
  33.5 1.9 collective-permute-done.2
  35.4 1.5 collective-permute-start.11
  37.1 1.5 collective-permute-start.12
  40.1 1.6 collective-permute-start.4
  41.7 1.5 broadcast_in_dim.119
  44.1 1.4 collective-permute-start.5
  45.5 4.0 %collective-permute-done.11 = bf16[4,64,512]{2,1,0:T(8,128)(2,1)S(1)} collective-permute-done((bf16[4,64,512]{2,1,0:T(8,128)(2,1)S(1)}, bf16[4,64,512]{2,1,0:T(8,128)(2,1)S(1)}, u32[]{:S(2)}, u32[]{:S(2)}) %collective-permute-start.11) | collective-permute-done | bytes 262176 | tf_op jit(solution)/shard_map/ppermute | solution.py:390
  49.6 1.5 collective-permute-start.17
  51.1 1.6 collective-permute-start.18
  53.0 2.4 collective-permute-start.19
  55.5 15.1 %collective-permute-done.17 = bf16[4,128,512]{2,1,0:T(8,128)(2,1)S(1)} collective-permute-done((bf16[4,128,512]{2,1,0:T(8,128)(2,1)S(1)}, bf16[4,128,512]{2,1,0:T(8,128)(2,1)S(1)}, u32[]{:S(2)}, u32[]{:S(2)}) %collective-permute-start.17) | collective-permute-done | bytes 524320 | tf_op jit(solution)/shard_map/ppermute | solution.py:390
  71.4 8.7 %collective-permute-done.18 = bf16[4,128,512]{2,1,0:T(8,128)(2,1)S(1)} collective-permute-done((bf16[4,128,512]{2,1,0:T(8,128)(2,1)S(1)}, bf16[4,128,512]{2,1,0:T(8,128)(2,1)S(1)}, u32[]{:S(2)}, u32[]{:S(2)}) %collective-permute-start.18) | collective-permute-done | bytes 524320 | tf_op jit(solution)/shard_map/ppermute | solution.py:390
  82.9 1.4 select_bitcast_fusion.5
  84.5 1.5 copy.437
  86.0 1.5 collective-permute-done.6
  87.5 1.5 select_bitcast_fusion.2
  90.5 1.5 copy.430
  92.8 18.1 %self_forward.1 = (bf16[4,256,512]{2,1,0:T(8,128)(2,1)}, bf16[4,256,512]{2,1,0:T(8,128)(2,1)}, bf16[4,256,512]{2,1,0:T(8,128)(2,1)}, bf16[4,256,512]{2,1,0:T(8,1...) custom-call(s32[4]{0:T(128)} %count_ref.9, bf16[4,256,512]{2,1,0:T(8,128)(2,1)} %x_ref.3, ...), custom_call_target="tpu_custom_call" | custom-call | tf_op jit(solution)/shard_map/self_forward/pallas_call | solution.py:277
  110.9 24.2 %cross_forward.1 = (bf16[4,256,512]{2,1,0:T(8,128)(2,1)}, bf16[4,256,512]{2,1,0:T(8,128)(2,1)}, bf16[4,512,512]{2,1,0:T(8,128)(2,1)}, bf16[4,512,512]{2,1,0:T(8,...) custom-call(s32[4]{0:T(128)} %count_ref.8, ...), custom_call_target="tpu_custom_call" | custom-call | tf_op jit(solution)/shard_map/cross_forward/pallas_call | solution.py:277
  135.1 2.5 select_bitcast_fusion
  137.6 1.5 pad_maximum_fusion
  139.1 2.6 reshape.162.w_in_ref
  141.7 24.4 %ffn.1 = (f32[4,256,512]{2,1,0:T(8,128)}, f32[4,256,512]{2,1,0:T(8,128)}, bf16[512,2048]{1,0:T(8,128)(2,1)}, bf16[2048,512]{1,0:T(8,128)(2,1)}, f32[1,2048]{1,0:T(1,128)}, /*index=5*/f32[8,512]{1,0:T(8,128)}) custom-call(s32[4]{0:T(128)} %count_ref.9, f32[4,256,512]{2,1,0:T(8,128)} %get-tuple-element.44.x_ref, bf16[4,256,512]{2,1,0:T(8,128)(2,1)} %cot_ref.1, ...), custom_call_target="tpu_custom_call" | custom-call | tf_op jit(solution)/shard_map/ffn/pallas_call | solution.py:277
  166.1 31.1 %cross_back.1 = (f32[4,256,512]{2,1,0:T(8,128)}, f32[4,512,512]{2,1,0:T(8,128)}, f32[4,512,512]{2,1,0:T(8,128)}, f32[8,512]{1,0:T(8,128)}) custom-call(s32[4]{0:T(128)} %count_ref.8, f32[4,256,512]{2,1,0:T(8,128)} %get-tuple-element.46.grad_ref, f32[4,256,512]{2,1,0:T(8,128)} %get-tuple-element.43.x_ref, bf16[4,256,512]{2,1,0:T(8,128)(2,1)} %get-tuple-element.47.act_ref, ...), custom_call_target="tpu_custom_call" | custom-call | tf_op jit(solution)/shard_map/cross_back/pallas_call | solution.py:277
  197.2 22.6 %self_back.1 = (f32[4,256,512]{2,1,0:T(8,128)}, f32[4,512,512]{2,1,0:T(8,128)}, f32[8,512]{1,0:T(8,128)}) custom-call(s32[4]{0:T(128)} %count_ref.9, f32[4,256,512]{2,1,0:T(8,128)} %get-tuple-element.53.grad_ref, bf16[4,256,512]{2,1,0:T(8,128)(2,1)} %x_ref.3, bf16[4,256,512]{2,1,0:T(8,128)(2,1)} %get-tuple-element.54.act_ref, ...), custom_call_target="tpu_custom_call" | custom-call | tf_op jit(solution)/shard_map/self_back/pallas_call | solution.py:277
  221.3 3.3 concatenate.58
  224.5 3.3 fusion.6
  230.0 2.6 copy.453
  232.7 2.0 copy-done
  242.3 2.6 copy.443
  246.2 1.7 copy-done.1
  247.9 1.6 bitcast_add_fusion.1
  249.6 1.6 collective-permute-start.29
  251.2 1.4 collective-permute-start.30
  253.1 1.7 bitcast_add_fusion
  254.8 1.4 dynamic-slice_convert_fusion.6
  256.4 1.6 collective-permute-start.22
  258.8 1.4 collective-permute-start.23
  260.2 4.6 %collective-permute-done.30 = bf16[4,64,512]{2,1,0:T(8,128)(2,1)S(1)} collective-permute-done((bf16[4,64,512]{2,1,0:T(8,128)(2,1)S(1)}, bf16[4,64,512]{2,1,0:T(8,128)(2,1)S(1)}, u32[]{:S(2)}, u32[]{:S(2)}) %collective-permute-start.30) | collective-permute-done | bytes 262176 | tf_op jit(solution)/shard_map/ppermute | solution.py:390
  265.8 1.1 collective-permute-start.32
  266.9 2.0 collective-permute-start.33
  268.9 2.2 convert_add_fusion
  271.4 2.9 collective-permute-start.36
  274.3 1.5 collective-permute-done.23
  275.8 1.9 collective-permute-start.37
  279.1 2.0 collective-permute-start.34
  281.3 3.9 %collective-permute-done.34 = bf16[64,512]{1,0:T(8,128)(2,1)S(1)} collective-permute-done((bf16[64,512]{1,0:T(8,128)(2,1)S(1)}, bf16[64,512]{1,0:T(8,128)(2,1)S(1)}, u32[]{:S(2)}, u32[]{:S(2)}) %collective-permute-start.34) | collective-permute-done | bytes 65568 | tf_op jit(solution)/shard_map/ppermute | solution.py:390
  285.3 1.9 collective-permute-done.36
  287.2 2.2 collective-permute-start.27
  289.5 11.0 %collective-permute-done.37 = bf16[4,128,512]{2,1,0:T(8,128)(2,1)S(1)} collective-permute-done((bf16[4,128,512]{2,1,0:T(8,128)(2,1)S(1)}, bf16[4,128,512]{2,1,0:T(8,128)(2,1)S(1)}, u32[]{:S(2)}, u32[]{:S(2)}) %collective-permute-start.37) | collective-permute-done | bytes 524320 | tf_op jit(solution)/shard_map/ppermute | solution.py:390
  301.0 2.6 collective-permute-start.40
  303.7 1.8 collective-permute-start.41
  306.9 6.3 %collective-permute-done.40 = bf16[128,512]{1,0:T(8,128)(2,1)S(1)} collective-permute-done((bf16[128,512]{1,0:T(8,128)(2,1)S(1)}, bf16[128,512]{1,0:T(8,128)(2,1)S(1)}, u32[]{:S(2)}, u32[]{:S(2)}) %collective-permute-start.40) | collective-permute-done | bytes 131104 | tf_op jit(solution)/shard_map/ppermute | solution.py:390
  317.2 4.0 %all-to-all-start = ((f32[32,8,128]{2,1,0:T(8,128)}), f32[32,8,128]{2,1,0:T(8,128)S(1)}, u32[]{:S(2)}, u32[]{:S(2)}) async-start(f32[32,8,128]{2,1,0:T(8,128)} %broadcast_in_dim.129), calls=%async_computation | async-start | bytes 262144 | tf_op jit(solution)/shard_map/all_to_all | solution.py:542
  321.5 8.0 %all-to-all-done = f32[32,8,128]{2,1,0:T(8,128)S(1)} async-done(((f32[32,8,128]{2,1,0:T(8,128)}), f32[32,8,128]{2,1,0:T(8,128)S(1)}, u32[]{:S(2)}, u32[]{:S(2)}) %all-to-all-start) | async-done | bytes 131104 | tf_op jit(solution)/shard_map/all_to_all | solution.py:542
  (199 shorter events, 41.1 us)
Async XLA Ops:
  2.6 34.5 %collective-permute-start.14 = (bf16[128,512]{1,0:T(8,128)(2,1)S(1)}, bf16[128,512]{1,0:T(8,128)(2,1)}, u32[]{:S(2)}, u32[]{:S(2)}) collective-permute-start(bf16[128,512]{1,0:T(8,128)(2,1)S(1)} %pad_maximum_fusion.3), channel_id=1, source_target_pairs={{0,8},{1,9},{2,10},{3,11},{4,12},{5,13},{6,14},{7,15},{8,0},{9,1},... | collective-permute-start | bytes 393224 | tf_op jit(solution)/shard_map/ppermute | solution.py:390
  5.6 33.9 %collective-permute-start.15 = (bf16[128,512]{1,0:T(8,128)(2,1)S(1)}, bf16[128,512]{1,0:T(8,128)(2,1)S(1)}, u32[]{:S(2)}, u32[]{:S(2)}) collective-permute-start(bf16[128,512]{1,0:T(8,128)(2,1)S(1)} %pad_maximum_fusion.3), channel_id=1, source_target_pairs={{0,16},{1,17},{2,18},{3,19},{4,20},{5,21},{6,22},{7,23},{8,24},{9,... | collective-permute-start | bytes 393224 | tf_op jit(solution)/shard_map/ppermute | solution.py:390
  8.2 31.9 %collective-permute-start.16 = (bf16[128,512]{1,0:T(8,128)(2,1)S(1)}, bf16[128,512]{1,0:T(8,128)(2,1)S(1)}, u32[]{:S(2)}, u32[]{:S(2)}) collective-permute-start(bf16[128,512]{1,0:T(8,128)(2,1)S(1)} %pad_maximum_fusion.3), channel_id=1, source_target_pairs={{0,24},{1,25},{2,26},{3,27},{4,28},{5,29},{6,30},{7,31},{8,16},{9,... | collective-permute-start | bytes 393224 | tf_op jit(solution)/shard_map/ppermute | solution.py:390
  9.2 6.9 %collective-permute-start.7 = (bf16[64,512]{1,0:T(8,128)(2,1)S(1)}, bf16[64,512]{1,0:T(8,128)(2,1)S(1)}, u32[]{:S(2)}, u32[]{:S(2)}) collective-permute-start(bf16[64,512]{1,0:T(8,128)(2,1)S(1)} %bitcast.244), channel_id=1, source_target_pairs={{0,8},{1,9},{2,10},{3,11},{4,12},{5,13},{6,14},{7,15},{8,0},{9,1},... | collective-permute-start | bytes 196616 | tf_op jit(solution)/shard_map/ppermute | solution.py:390
  10.2 14.7 %collective-permute-start.8 = (bf16[64,512]{1,0:T(8,128)(2,1)S(1)}, bf16[64,512]{1,0:T(8,128)(2,1)S(1)}, u32[]{:S(2)}, u32[]{:S(2)}) collective-permute-start(bf16[64,512]{1,0:T(8,128)(2,1)S(1)} %bitcast.245), channel_id=1, source_target_pairs={{0,16},{1,17},{2,18},{3,19},{4,20},{5,21},{6,22},{7,23},{8,24},{9,... | collective-permute-start | bytes 196616 | tf_op jit(solution)/shard_map/ppermute | solution.py:390
  16.2 8.7 %collective-permute-start.9 = (bf16[64,512]{1,0:T(8,128)(2,1)S(1)}, bf16[64,512]{1,0:T(8,128)(2,1)S(1)}, u32[]{:S(2)}, u32[]{:S(2)}) collective-permute-start(bf16[64,512]{1,0:T(8,128)(2,1)S(1)} %bitcast.247), channel_id=1, source_target_pairs={{0,24},{1,25},{2,26},{3,27},{4,28},{5,29},{6,30},{7,31},{8,16},{9,... | collective-permute-start | bytes 196616 | tf_op jit(solution)/shard_map/ppermute | solution.py:390
  24.9 4.4 %collective-permute-start = (bf16[65,512]{1,0:T(8,128)(2,1)S(1)}, bf16[65,512]{1,0:T(8,128)(2,1)S(1)}, u32[]{:S(2)}, u32[]{:S(2)}) collective-permute-start(bf16[65,512]{1,0:T(8,128)(2,1)S(1)} %pad_maximum_fusion.4), channel_id=1, source_target_pairs={{0,8},{1,9},{2,10},{3,11},{4,12},{5,13},{6,14},{7,15},{8,0},{9,1},... | collective-permute-start | bytes 199688 | tf_op jit(solution)/shard_map/ppermute | solution.py:390
  24.9 7.0 %collective-permute-start.1 = (bf16[65,512]{1,0:T(8,128)(2,1)S(1)}, bf16[65,512]{1,0:T(8,128)(2,1)S(1)}, u32[]{:S(2)}, u32[]{:S(2)}) collective-permute-start(bf16[65,512]{1,0:T(8,128)(2,1)S(1)} %pad_maximum_fusion.4), channel_id=1, source_target_pairs={{0,16},{1,17},{2,18},{3,19},{4,20},{5,21},{6,22},{7,23},{8,24},{9,... | collective-permute-start | bytes 199688 | tf_op jit(solution)/shard_map/ppermute | solution.py:390
  29.2 6.2 %collective-permute-start.2 = (bf16[65,512]{1,0:T(8,128)(2,1)S(1)}, bf16[65,512]{1,0:T(8,128)(2,1)S(1)}, u32[]{:S(2)}, u32[]{:S(2)}) collective-permute-start(bf16[65,512]{1,0:T(8,128)(2,1)S(1)} %pad_maximum_fusion.4), channel_id=1, source_target_pairs={{0,24},{1,25},{2,26},{3,27},{4,28},{5,29},{6,30},{7,31},{8,16},{9,... | collective-permute-start | bytes 199688 | tf_op jit(solution)/shard_map/ppermute | solution.py:390
  31.9 12.1 %collective-permute-start.10 = (bf16[4,64,512]{2,1,0:T(8,128)(2,1)S(1)}, bf16[4,64,512]{2,1,0:T(8,128)(2,1)S(1)}, u32[]{:S(2)}, u32[]{:S(2)}) collective-permute-start(bf16[4,64,512]{2,1,0:T(8,128)(2,1)S(1)} %bitcast_dynamic-update-slice_fusion.20), channel_id=1, source_target_pairs={{0,2},{1,3},{2,0},{3,1},{4,6},{5,7},{6,4},{7,5},{8,10},{9,11},{10,... | collective-permute-start | bytes 786440 | tf_op jit(solution)/shard_map/ppermute | solution.py:390
  35.4 14.2 %collective-permute-start.11 = (bf16[4,64,512]{2,1,0:T(8,128)(2,1)S(1)}, bf16[4,64,512]{2,1,0:T(8,128)(2,1)S(1)}, u32[]{:S(2)}, u32[]{:S(2)}) collective-permute-start(bf16[4,64,512]{2,1,0:T(8,128)(2,1)S(1)} %bitcast_dynamic-update-slice_fusion.20), channel_id=1, source_target_pairs={{0,4},{1,5},{2,6},{3,7},{4,0},{5,1},{6,2},{7,3},{8,12},{9,13},{10,... | collective-permute-start | bytes 786440 | tf_op jit(solution)/shard_map/ppermute | solution.py:390
  37.1 14.0 %collective-permute-start.12 = (bf16[4,64,512]{2,1,0:T(8,128)(2,1)S(1)}, bf16[4,64,512]{2,1,0:T(8,128)(2,1)S(1)}, u32[]{:S(2)}, u32[]{:S(2)}) collective-permute-start(bf16[4,64,512]{2,1,0:T(8,128)(2,1)S(1)} %bitcast_dynamic-update-slice_fusion.20), channel_id=1, source_target_pairs={{0,6},{1,7},{2,4},{3,5},{4,2},{5,3},{6,0},{7,1},{8,14},{9,15},{10,... | collective-permute-start | bytes 786440 | tf_op jit(solution)/shard_map/ppermute | solution.py:390
  39.5 13.5 %collective-permute-start.3 = (bf16[4,65,512]{2,1,0:T(8,128)(2,1)S(1)}, bf16[4,65,512]{2,1,0:T(8,128)(2,1)S(1)}, u32[]{:S(2)}, u32[]{:S(2)}) collective-permute-start(bf16[4,65,512]{2,1,0:T(8,128)(2,1)S(1)} %bitcast_dynamic-update-slice_fusion.16), channel_id=1, source_target_pairs={{0,2},{1,3},{2,0},{3,1},{4,6},{5,7},{6,4},{7,5},{8,10},{9,11},{10,... | collective-permute-start | bytes 798728 | tf_op jit(solution)/shard_map/ppermute | solution.py:390
  40.1 41.6 %collective-permute-start.4 = (bf16[4,65,512]{2,1,0:T(8,128)(2,1)S(1)}, bf16[4,65,512]{2,1,0:T(8,128)(2,1)S(1)}, u32[]{:S(2)}, u32[]{:S(2)}) collective-permute-start(bf16[4,65,512]{2,1,0:T(8,128)(2,1)S(1)} %bitcast_dynamic-update-slice_fusion.16), channel_id=1, source_target_pairs={{0,4},{1,5},{2,6},{3,7},{4,0},{5,1},{6,2},{7,3},{8,12},{9,13},{10,... | collective-permute-start | bytes 798728 | tf_op jit(solution)/shard_map/ppermute | solution.py:390
  44.1 37.7 %collective-permute-start.5 = (bf16[4,65,512]{2,1,0:T(8,128)(2,1)S(1)}, bf16[4,65,512]{2,1,0:T(8,128)(2,1)S(1)}, u32[]{:S(2)}, u32[]{:S(2)}) collective-permute-start(bf16[4,65,512]{2,1,0:T(8,128)(2,1)S(1)} %bitcast_dynamic-update-slice_fusion.16), channel_id=1, source_target_pairs={{0,6},{1,7},{2,4},{3,5},{4,2},{5,3},{6,0},{7,1},{8,14},{9,15},{10,... | collective-permute-start | bytes 798728 | tf_op jit(solution)/shard_map/ppermute | solution.py:390
  49.6 21.0 %collective-permute-start.17 = (bf16[4,128,512]{2,1,0:T(8,128)(2,1)S(1)}, bf16[4,128,512]{2,1,0:T(8,128)(2,1)S(1)}, u32[]{:S(2)}, u32[]{:S(2)}) collective-permute-start(bf16[4,128,512]{2,1,0:T(8,128)(2,1)S(1)} %bitcast_dynamic-update-slice_fusion.12), channel_id=1, source_target_pairs={{0,2},{1,3},{2,0},{3,1},{4,6},{5,7},{6,4},{7,5},{8,10},{9,11},{10,... | collective-permute-start | bytes 1572872 | tf_op jit(solution)/shard_map/ppermute | solution.py:390
  51.1 28.9 %collective-permute-start.18 = (bf16[4,128,512]{2,1,0:T(8,128)(2,1)S(1)}, bf16[4,128,512]{2,1,0:T(8,128)(2,1)S(1)}, u32[]{:S(2)}, u32[]{:S(2)}) collective-permute-start(bf16[4,128,512]{2,1,0:T(8,128)(2,1)S(1)} %bitcast_dynamic-update-slice_fusion.12), channel_id=1, source_target_pairs={{0,4},{1,5},{2,6},{3,7},{4,0},{5,1},{6,2},{7,3},{8,12},{9,13},{10,... | collective-permute-start | bytes 1572872 | tf_op jit(solution)/shard_map/ppermute | solution.py:390
  53.0 27.9 %collective-permute-start.19 = (bf16[4,128,512]{2,1,0:T(8,128)(2,1)S(1)}, bf16[4,128,512]{2,1,0:T(8,128)(2,1)S(1)}, u32[]{:S(2)}, u32[]{:S(2)}) collective-permute-start(bf16[4,128,512]{2,1,0:T(8,128)(2,1)S(1)} %bitcast_dynamic-update-slice_fusion.12), channel_id=1, source_target_pairs={{0,6},{1,7},{2,4},{3,5},{4,2},{5,3},{6,0},{7,1},{8,14},{9,15},{10,... | collective-permute-start | bytes 1572872 | tf_op jit(solution)/shard_map/ppermute | solution.py:390
  70.6 12.4 %collective-permute-start.13 = (bf16[4,4,64,512]{3,2,1,0:T(8,128)(2,1)S(1)}, bf16[4,4,64,512]{3,2,1,0:T(8,128)(2,1)}, u32[]{:S(2)}, u32[]{:S(2)}) collective-permute-start(bf16[4,4,64,512]{3,2,1,0:T(8,128)(2,1)S(1)} %bitcast_dynamic-update-slice_fusion.11), channel_id=1, source_target_pairs={{0,1},{1,0},{2,3},{3,2},{4,5},{5,4},{6,7},{7,6},{8,9},{9,8},{10,11... | collective-permute-start | bytes 3145736 | tf_op jit(solution)/shard_map/ppermute | solution.py:390
  81.7 53.4 %collective-permute-start.20 = (bf16[4,4,128,512]{3,2,1,0:T(8,128)(2,1)}, bf16[4,4,128,512]{3,2,1,0:T(8,128)(2,1)}, u32[]{:S(2)}, u32[]{:S(2)}) collective-permute-start(bf16[4,4,128,512]{3,2,1,0:T(8,128)(2,1)} %bitcast_dynamic-update-slice_fusion.3), channel_id=1, source_target_pairs={{0,1},{1,0},{2,3},{3,2},{4,5},{5,4},{6,7},{7,6},{8,9},{9,8},{10,11... | collective-permute-start | bytes 6291464 | tf_op jit(solution)/shard_map/ppermute | solution.py:390
  82.4 5.2 %collective-permute-start.6 = (bf16[4,4,65,512]{3,1,2,0:T(4,128)(2,1)S(1)}, bf16[4,4,65,512]{3,1,2,0:T(4,128)(2,1)}, u32[]{:S(2)}, u32[]{:S(2)}) collective-permute-start(bf16[4,4,65,512]{3,1,2,0:T(4,128)(2,1)S(1)} %copy.426), channel_id=1, source_target_pairs={{0,1},{1,0},{2,3},{3,2},{4,5},{5,4},{6,7},{7,6},{8,9},{9,8},{10,11... | collective-permute-start | bytes 3194888 | tf_op jit(solution)/shard_map/ppermute | solution.py:390
  197.2 24.0 %copy-start.13 = (f32[8,512]{1,0:T(8,128)S(1)}, f32[8,512]{1,0:T(8,128)}, u32[]{:S(2)}) copy-start(f32[8,512]{1,0:T(8,128)} %get-tuple-element.64) | copy-start | bytes 49156
  228.1 38.8 %collective-permute-start.35 = (bf16[4,4,128,512]{3,2,0,1:T(8,128)(2,1)S(1)}, bf16[4,4,128,512]{3,2,0,1:T(8,128)(2,1)}, u32[]{:S(2)}, u32[]{:S(2)}) collective-permute-start(bf16[4,4,128,512]{3,2,0,1:T(8,128)(2,1)S(1)} %bitcast.231), channel_id=1, source_target_pairs={{0,1},{1,0},{2,3},{3,2},{4,5},{5,4},{6,7},{7,6},{8,9},{9,8},{10,11... | collective-permute-start | bytes 6291464 | tf_op jit(solution)/shard_map/ppermute | solution.py:390
  232.7 2.0 copy-start
  232.7 6.4 %copy-start.16 = (f32[1,2048]{1,0:T(1,128)S(1)}, f32[1,2048]{1,0:T(1,128)}, u32[]{:S(2)}) copy-start(f32[1,2048]{1,0:T(1,128)} %get-tuple-element.66) | copy-start | bytes 24580
  234.8 11.4 %collective-permute-start.28 = (bf16[4,4,64,512]{3,2,1,0:T(8,128)(2,1)S(1)}, bf16[4,4,64,512]{3,2,1,0:T(8,128)(2,1)}, u32[]{:S(2)}, u32[]{:S(2)}) collective-permute-start(bf16[4,4,64,512]{3,2,1,0:T(8,128)(2,1)S(1)} %fusion.8), channel_id=1, source_target_pairs={{0,1},{1,0},{2,3},{3,2},{4,5},{5,4},{6,7},{7,6},{8,9},{9,8},{10,11... | collective-permute-start | bytes 3145736 | tf_op jit(solution)/shard_map/ppermute | solution.py:390
  245.7 2.2 copy-start.1
  245.7 7.4 %collective-permute-start.21 = (bf16[4,4,65,512]{3,1,2,0:T(4,128)(2,1)S(1)}, bf16[4,4,65,512]{3,1,2,0:T(4,128)(2,1)S(1)}, u32[]{:S(2)}, u32[]{:S(2)}) collective-permute-start(bf16[4,4,65,512]{3,1,2,0:T(4,128)(2,1)S(1)} %copy.448), channel_id=1, source_target_pairs={{0,1},{1,0},{2,3},{3,2},{4,5},{5,4},{6,7},{7,6},{8,9},{9,8},{10,11... | collective-permute-start | bytes 3194888 | tf_op jit(solution)/shard_map/ppermute | solution.py:390
  249.6 9.2 %collective-permute-start.29 = (bf16[4,64,512]{2,1,0:T(8,128)(2,1)S(1)}, bf16[4,64,512]{2,1,0:T(8,128)(2,1)S(1)}, u32[]{:S(2)}, u32[]{:S(2)}) collective-permute-start(bf16[4,64,512]{2,1,0:T(8,128)(2,1)S(1)} %get-tuple-element.258), channel_id=1, source_target_pairs={{0,2},{1,3},{2,0},{3,1},{4,6},{5,7},{6,4},{7,5},{8,10},{9,11},{10,... | collective-permute-start | bytes 786440 | tf_op jit(solution)/shard_map/ppermute | solution.py:390
  251.2 13.7 %collective-permute-start.30 = (bf16[4,64,512]{2,1,0:T(8,128)(2,1)S(1)}, bf16[4,64,512]{2,1,0:T(8,128)(2,1)S(1)}, u32[]{:S(2)}, u32[]{:S(2)}) collective-permute-start(bf16[4,64,512]{2,1,0:T(8,128)(2,1)S(1)} %get-tuple-element.260), channel_id=1, source_target_pairs={{0,4},{1,5},{2,6},{3,7},{4,0},{5,1},{6,2},{7,3},{8,12},{9,13},{10,... | collective-permute-start | bytes 786440 | tf_op jit(solution)/shard_map/ppermute | solution.py:390
  252.5 13.0 %collective-permute-start.31 = (bf16[4,64,512]{2,1,0:T(8,128)(2,1)S(1)}, bf16[4,64,512]{2,1,0:T(8,128)(2,1)S(1)}, u32[]{:S(2)}, u32[]{:S(2)}) collective-permute-start(bf16[4,64,512]{2,1,0:T(8,128)(2,1)S(1)} %get-tuple-element.259), channel_id=1, source_target_pairs={{0,6},{1,7},{2,4},{3,5},{4,2},{5,3},{6,0},{7,1},{8,14},{9,15},{10,... | collective-permute-start | bytes 786440 | tf_op jit(solution)/shard_map/ppermute | solution.py:390
  256.4 15.0 %collective-permute-start.22 = (bf16[4,65,512]{2,0,1:T(4,128)(2,1)S(1)}, bf16[4,65,512]{2,0,1:T(4,128)(2,1)S(1)}, u32[]{:S(2)}, u32[]{:S(2)}) collective-permute-start(bf16[4,65,512]{2,0,1:T(4,128)(2,1)S(1)} %bitcast.243), channel_id=1, source_target_pairs={{0,2},{1,3},{2,0},{3,1},{4,6},{5,7},{6,4},{7,5},{8,10},{9,11},{10,... | collective-permute-start | bytes 798728 | tf_op jit(solution)/shard_map/ppermute | solution.py:390
  258.1 10.8 %copy-start.2 = (bf16[4,4,1,128,512]{4,3,2,1,0:T(8,128)(2,1)S(1)}, bf16[4,4,1,128,512]{4,3,2,1,0:T(8,128)(2,1)}, u32[]{:S(2)}) copy-start(bf16[4,4,1,128,512]{4,3,2,1,0:T(8,128)(2,1)} %get-tuple-element.247) | copy-start | bytes 6291460
  258.8 16.9 %collective-permute-start.23 = (bf16[4,65,512]{2,0,1:T(4,128)(2,1)S(1)}, bf16[4,65,512]{2,0,1:T(4,128)(2,1)S(1)}, u32[]{:S(2)}, u32[]{:S(2)}) collective-permute-start(bf16[4,65,512]{2,0,1:T(4,128)(2,1)S(1)} %bitcast.242), channel_id=1, source_target_pairs={{0,4},{1,5},{2,6},{3,7},{4,0},{5,1},{6,2},{7,3},{8,12},{9,13},{10,... | collective-permute-start | bytes 798728 | tf_op jit(solution)/shard_map/ppermute | solution.py:390
  264.8 12.8 %collective-permute-start.24 = (bf16[4,65,512]{2,0,1:T(4,128)(2,1)S(1)}, bf16[4,65,512]{2,0,1:T(4,128)(2,1)S(1)}, u32[]{:S(2)}, u32[]{:S(2)}) collective-permute-start(bf16[4,65,512]{2,0,1:T(4,128)(2,1)S(1)} %bitcast.241), channel_id=1, source_target_pairs={{0,6},{1,7},{2,4},{3,5},{4,2},{5,3},{6,0},{7,1},{8,14},{9,15},{10,... | collective-permute-start | bytes 798728 | tf_op jit(solution)/shard_map/ppermute | solution.py:390
  265.8 13.3 %collective-permute-start.32 = (bf16[64,512]{1,0:T(8,128)(2,1)S(1)}, bf16[64,512]{1,0:T(8,128)(2,1)S(1)}, u32[]{:S(2)}, u32[]{:S(2)}) collective-permute-start(bf16[64,512]{1,0:T(8,128)(2,1)S(1)} %get-tuple-element.269), channel_id=1, source_target_pairs={{0,8},{1,9},{2,10},{3,11},{4,12},{5,13},{6,14},{7,15},{8,0},{9,1},... | collective-permute-start | bytes 196616 | tf_op jit(solution)/shard_map/ppermute | solution.py:390
  266.9 14.4 %collective-permute-start.33 = (bf16[64,512]{1,0:T(8,128)(2,1)S(1)}, bf16[64,512]{1,0:T(8,128)(2,1)S(1)}, u32[]{:S(2)}, u32[]{:S(2)}) collective-permute-start(bf16[64,512]{1,0:T(8,128)(2,1)S(1)} %get-tuple-element.271), channel_id=1, source_target_pairs={{0,16},{1,17},{2,18},{3,19},{4,20},{5,21},{6,22},{7,23},{8,24},{9,... | collective-permute-start | bytes 196616 | tf_op jit(solution)/shard_map/ppermute | solution.py:390
  271.4 15.8 %collective-permute-start.36 = (bf16[4,128,512]{2,1,0:T(8,128)(2,1)S(1)}, bf16[4,128,512]{2,1,0:T(8,128)(2,1)S(1)}, u32[]{:S(2)}, u32[]{:S(2)}) collective-permute-start(bf16[4,128,512]{2,1,0:T(8,128)(2,1)S(1)} %get-tuple-element.244), channel_id=1, source_target_pairs={{0,2},{1,3},{2,0},{3,1},{4,6},{5,7},{6,4},{7,5},{8,10},{9,11},{10,... | collective-permute-start | bytes 1572872 | tf_op jit(solution)/shard_map/ppermute | solution.py:390
  275.8 24.7 %collective-permute-start.37 = (bf16[4,128,512]{2,1,0:T(8,128)(2,1)S(1)}, bf16[4,128,512]{2,1,0:T(8,128)(2,1)S(1)}, u32[]{:S(2)}, u32[]{:S(2)}) collective-permute-start(bf16[4,128,512]{2,1,0:T(8,128)(2,1)S(1)} %get-tuple-element.246), channel_id=1, source_target_pairs={{0,4},{1,5},{2,6},{3,7},{4,0},{5,1},{6,2},{7,3},{8,12},{9,13},{10,... | collective-permute-start | bytes 1572872 | tf_op jit(solution)/shard_map/ppermute | solution.py:390
  277.6 22.9 %collective-permute-start.38 = (bf16[4,128,512]{2,1,0:T(8,128)(2,1)S(1)}, bf16[4,128,512]{2,1,0:T(8,128)(2,1)S(1)}, u32[]{:S(2)}, u32[]{:S(2)}) collective-permute-start(bf16[4,128,512]{2,1,0:T(8,128)(2,1)S(1)} %get-tuple-element.245), channel_id=1, source_target_pairs={{0,6},{1,7},{2,4},{3,5},{4,2},{5,3},{6,0},{7,1},{8,14},{9,15},{10,... | collective-permute-start | bytes 1572872 | tf_op jit(solution)/shard_map/ppermute | solution.py:390
  279.1 6.2 %collective-permute-start.34 = (bf16[64,512]{1,0:T(8,128)(2,1)S(1)}, bf16[64,512]{1,0:T(8,128)(2,1)S(1)}, u32[]{:S(2)}, u32[]{:S(2)}) collective-permute-start(bf16[64,512]{1,0:T(8,128)(2,1)S(1)} %get-tuple-element.270), channel_id=1, source_target_pairs={{0,24},{1,25},{2,26},{3,27},{4,28},{5,29},{6,30},{7,31},{8,16},{9,... | collective-permute-start | bytes 196616 | tf_op jit(solution)/shard_map/ppermute | solution.py:390
  281.2 22.4 %collective-permute-start.25 = (bf16[65,512]{1,0:T(8,128)(2,1)S(1)}, bf16[65,512]{1,0:T(8,128)(2,1)S(1)}, u32[]{:S(2)}, u32[]{:S(2)}) collective-permute-start(bf16[65,512]{1,0:T(8,128)(2,1)S(1)} %bitcast.250), channel_id=1, source_target_pairs={{0,8},{1,9},{2,10},{3,11},{4,12},{5,13},{6,14},{7,15},{8,0},{9,1},... | collective-permute-start | bytes 199688 | tf_op jit(solution)/shard_map/ppermute | solution.py:390
  285.3 20.2 %collective-permute-start.26 = (bf16[65,512]{1,0:T(8,128)(2,1)S(1)}, bf16[65,512]{1,0:T(8,128)(2,1)S(1)}, u32[]{:S(2)}, u32[]{:S(2)}) collective-permute-start(bf16[65,512]{1,0:T(8,128)(2,1)S(1)} %bitcast.249), channel_id=1, source_target_pairs={{0,16},{1,17},{2,18},{3,19},{4,20},{5,21},{6,22},{7,23},{8,24},{9,... | collective-permute-start | bytes 199688 | tf_op jit(solution)/shard_map/ppermute | solution.py:390
  287.2 18.2 %collective-permute-start.27 = (bf16[65,512]{1,0:T(8,128)(2,1)S(1)}, bf16[65,512]{1,0:T(8,128)(2,1)S(1)}, u32[]{:S(2)}, u32[]{:S(2)}) collective-permute-start(bf16[65,512]{1,0:T(8,128)(2,1)S(1)} %bitcast.248), channel_id=1, source_target_pairs={{0,24},{1,25},{2,26},{3,27},{4,28},{5,29},{6,30},{7,31},{8,16},{9,... | collective-permute-start | bytes 199688 | tf_op jit(solution)/shard_map/ppermute | solution.py:390
  300.8 20.4 %copy-start.12 = (f32[17,16]{0,1:T(8,128)S(1)}, f32[17,16]{0,1:T(8,128)}, u32[]{:S(2)}) copy-start(f32[17,16]{0,1:T(8,128)} %param.25) | copy-start | bytes 3268
  300.8 20.5 %copy-start.14 = (f32[17,16]{0,1:T(8,128)S(1)}, f32[17,16]{0,1:T(8,128)}, u32[]{:S(2)}) copy-start(f32[17,16]{0,1:T(8,128)} %param.32) | copy-start | bytes 3268
  300.8 20.6 %copy-start.15 = (f32[17,16]{0,1:T(8,128)S(1)}, f32[17,16]{0,1:T(8,128)}, u32[]{:S(2)}) copy-start(f32[17,16]{0,1:T(8,128)} %param.33) | copy-start | bytes 3268
  300.8 32.2 %copy-start.4 = (f32[64,512]{1,0:T(8,128)S(1)}, f32[64,512]{1,0:T(8,128)}, u32[]{:S(2)}) copy-start(f32[64,512]{1,0:T(8,128)} %param.24) | copy-start | bytes 393220
  300.8 32.2 %copy-start.8 = (f32[64,512]{1,0:T(8,128)S(1)}, f32[64,512]{1,0:T(8,128)}, u32[]{:S(2)}) copy-start(f32[64,512]{1,0:T(8,128)} %param.31) | copy-start | bytes 393220
  300.8 32.1 %copy-start.9 = (f32[64,512]{1,0:T(8,128)S(1)}, f32[64,512]{1,0:T(8,128)}, u32[]{:S(2)}) copy-start(f32[64,512]{1,0:T(8,128)} %param.30) | copy-start | bytes 393220
  300.9 5.9 %collective-permute-start.39 = (bf16[128,512]{1,0:T(8,128)(2,1)S(1)}, bf16[128,512]{1,0:T(8,128)(2,1)S(1)}, u32[]{:S(2)}, u32[]{:S(2)}) collective-permute-start(bf16[128,512]{1,0:T(8,128)(2,1)S(1)} %get-tuple-element.263), channel_id=1, source_target_pairs={{0,8},{1,9},{2,10},{3,11},{4,12},{5,13},{6,14},{7,15},{8,0},{9,1},... | collective-permute-start | bytes 393224 | tf_op jit(solution)/shard_map/ppermute | solution.py:390
  301.0 12.2 %collective-permute-start.40 = (bf16[128,512]{1,0:T(8,128)(2,1)S(1)}, bf16[128,512]{1,0:T(8,128)(2,1)S(1)}, u32[]{:S(2)}, u32[]{:S(2)}) collective-permute-start(bf16[128,512]{1,0:T(8,128)(2,1)S(1)} %get-tuple-element.265), channel_id=1, source_target_pairs={{0,16},{1,17},{2,18},{3,19},{4,20},{5,21},{6,22},{7,23},{8,24},{9,... | collective-permute-start | bytes 393224 | tf_op jit(solution)/shard_map/ppermute | solution.py:390
  303.6 30.2 %copy-start.3 = (f32[8,16,512]{2,1,0:T(8,128)S(1)}, f32[8,16,512]{2,1,0:T(8,128)}, u32[]{:S(2)}) copy-start(f32[8,16,512]{2,1,0:T(8,128)} %param.22) | copy-start | bytes 786436
  303.6 30.2 %copy-start.6 = (f32[8,16,512]{2,1,0:T(8,128)S(1)}, f32[8,16,512]{2,1,0:T(8,128)}, u32[]{:S(2)}) copy-start(f32[8,16,512]{2,1,0:T(8,128)} %param.27) | copy-start | bytes 786436
  303.6 30.2 %copy-start.7 = (f32[8,16,512]{2,1,0:T(8,128)S(1)}, f32[8,16,512]{2,1,0:T(8,128)}, u32[]{:S(2)}) copy-start(f32[8,16,512]{2,1,0:T(8,128)} %param.26) | copy-start | bytes 786436
  303.7 9.6 %collective-permute-start.41 = (bf16[128,512]{1,0:T(8,128)(2,1)S(1)}, bf16[128,512]{1,0:T(8,128)(2,1)S(1)}, u32[]{:S(2)}, u32[]{:S(2)}) collective-permute-start(bf16[128,512]{1,0:T(8,128)(2,1)S(1)} %get-tuple-element.264), channel_id=1, source_target_pairs={{0,24},{1,25},{2,26},{3,27},{4,28},{5,29},{6,30},{7,31},{8,16},{9,... | collective-permute-start | bytes 393224 | tf_op jit(solution)/shard_map/ppermute | solution.py:390
  313.3 21.6 %copy-start.5 = (f32[16,2048]{1,0:T(8,128)S(1)}, f32[16,2048]{1,0:T(8,128)}, u32[]{:S(2)}) copy-start(f32[16,2048]{1,0:T(8,128)} %param.23) | copy-start | bytes 393220
  313.3 21.6 %copy-start.10 = (f32[16,2048]{1,0:T(8,128)S(1)}, f32[16,2048]{1,0:T(8,128)}, u32[]{:S(2)}) copy-start(f32[16,2048]{1,0:T(8,128)} %param.29) | copy-start | bytes 393220
  313.3 21.6 %copy-start.11 = (f32[16,2048]{1,0:T(8,128)S(1)}, f32[16,2048]{1,0:T(8,128)}, u32[]{:S(2)}) copy-start(f32[16,2048]{1,0:T(8,128)} %param.28) | copy-start | bytes 393220
  317.2 12.2 %all-to-all-start = ((f32[32,8,128]{2,1,0:T(8,128)}), f32[32,8,128]{2,1,0:T(8,128)S(1)}, u32[]{:S(2)}, u32[]{:S(2)}) async-start(f32[32,8,128]{2,1,0:T(8,128)} %broadcast_in_dim.129), calls=%async_computation | async-start | bytes 262144 | tf_op jit(solution)/shard_map/all_to_all | solution.py:542

commit v3 on v2

v3 whole, which is shorter than its diff:
```python
from functools import partial

import jax
import jax.numpy as jnp
from jax import lax
from jax.experimental import pallas as pl
from jax.experimental.pallas import tpu as pltpu
from jax.sharding import PartitionSpec as P

HEADS = 8
HEAD_DIM = 64
STEP = 5
AXES = ("dp", "fsdp")
PAIR = 2 * HEAD_DIM
SCALE = HEAD_DIM ** (-0.5)
LOW = jnp.bfloat16
F32 = jnp.float32
LIMIT = 60 * 1024 * 1024


def dot_nn(left, right):
    return lax.dot_general(left, right, (((1,), (0,)), ((), ())), preferred_element_type=F32)


def dot_nt(left, right):
    return lax.dot_general(left, right, (((1,), (1,)), ((), ())), preferred_element_type=F32)


def dot_tn(left, right):
    return lax.dot_general(left, right, (((0,), (0,)), ((), ())), preferred_element_type=F32)


def normalize(values):
    center = values - jnp.mean(values, -1, keepdims=True)
    inverse = lax.rsqrt(jnp.mean(center * center, -1, keepdims=True) + 1e-05)
    return center * inverse, inverse


def normalize_back(grad, hat, inverse, gain):
    grad_hat = grad * (1.0 + gain)
    first = jnp.mean(grad_hat, -1, keepdims=True)
    second = jnp.mean(grad_hat * hat, -1, keepdims=True)
    return inverse * (grad_hat - first - hat * second)


def column_sum(values):
    return jnp.sum(values.astype(F32), 0, keepdims=True)


def half_of(pair, odd):
    lane = lax.broadcasted_iota(jnp.int32, pair.shape, 1)
    keep = lane >= HEAD_DIM if odd else lane < HEAD_DIM
    return jnp.where(keep, pair, jnp.zeros_like(pair))


def self_bias(size, count):
    key = lax.broadcasted_iota(jnp.int32, (size, size), 0)
    query = lax.broadcasted_iota(jnp.int32, (size, size), 1)
    return jnp.where((key <= query) & (key < count), 0.0, -1e30)


def cross_bias(keys, queries, count):
    key = lax.broadcasted_iota(jnp.int32, (keys, queries), 0)
    return jnp.where(key < count, 0.0, -1e30)


def attend(query, key, value, bias_ref, mixed_ref, lse_ref):
    value_t = value.T
    for pair in range(HEADS // 2):
        cols = slice(pair * PAIR, (pair + 1) * PAIR)
        query_pair, key_pair = query[:, cols] * SCALE, key[:, cols]
        for odd in range(2):
            head = 2 * pair + odd
            rows = slice(head * HEAD_DIM, (head + 1) * HEAD_DIM)
            scores = dot_nt(half_of(key_pair, odd), query_pair) + bias_ref[...]
            top = jnp.max(scores, 0, keepdims=True)
            expo = jnp.exp(scores - top)
            total = jnp.sum(expo, 0, keepdims=True)
            probs = (expo * (1.0 / total)).astype(LOW)
            mixed_ref[rows] = dot_nn(value_t[rows], probs)
            lse_ref[0, head : head + 1] = top + jnp.log(total)


def attend_back(query_ref, key_ref, value_ref, grad, bias_ref, lse_ref, gq_ref, gk_ref, gv_ref):
    key_t = key_ref[0].T
    for pair in range(HEADS // 2):
        cols = slice(pair * PAIR, (pair + 1) * PAIR)
        query_pair = query_ref[0, :, cols] * SCALE
        key_pair, value_pair, grad_pair = key_ref[0, :, cols], value_ref[0, :, cols], grad[:, cols]
        grad_key = grad_value = None
        for odd in range(2):
            head = 2 * pair + odd
            rows = slice(head * HEAD_DIM, (head + 1) * HEAD_DIM)
            scores = dot_nt(half_of(key_pair, odd), query_pair) + bias_ref[...]
            probs = jnp.exp(scores - lse_ref[0, head : head + 1])
            grad_probs = dot_nt(half_of(value_pair, odd), grad_pair)
            inner = jnp.sum(probs * grad_probs, 0, keepdims=True)
            grad_scores = (probs * (grad_probs - inner)).astype(LOW)
            to_value = dot_nn(probs.astype(LOW), half_of(grad_pair, odd))
            to_key = dot_nn(grad_scores, half_of(query_pair, odd))
            grad_value = to_value if grad_value is None else grad_value + to_value
            grad_key = to_key if grad_key is None else grad_key + to_key
            gq_ref[rows] = dot_nn(key_t[rows], grad_scores)
        gk_ref[0, :, cols] = grad_key.astype(LOW)
        gv_ref[0, :, cols] = grad_value.astype(LOW)


def place_weights(place_ref, mine_ref, other_ref, blocks, outs, turned=None, table_ref=None):
    planes, depths = mine_ref.shape[:2]
    for plane in range(planes):
        for depth in range(depths):
            base = ((depth ^ place_ref[0]) * planes + (plane ^ place_ref[1])) * 2
            for ref, core in ((mine_ref, place_ref[2]), (other_ref, 1 - place_ref[2])):
                for out, row, own, col in blocks:
                    first = pl.multiple_of((base + core) * own, own)
                    piece = ref[plane, depth, row : row + own]
                    if isinstance(col, int):
                        outs[out][col, pl.ds(first, own)] = piece
                    else:
                        outs[out][pl.ds(first, own), col] = piece
                if turned is not None:
                    row = blocks[-1][1] + blocks[-1][2]
                    piece = ref[plane, depth, row : row + 8].astype(F32)
                    first = pl.multiple_of((base + core) * 16, 16)
                    turned[pl.ds(first, 8)] = piece[:, :128]
                    turned[pl.ds(pl.multiple_of(first + 8, 8), 8)] = piece[:, 128:256]
    if turned is not None:
        table_ref[...] = turned[...].T[: table_ref.shape[0]]


def attn_blocks(own):
    return [(0, i * own, own, i) for i in range(4)]


def ffn_blocks(own, out_rows, width, blocks):
    spots = [(1, 0, out_rows, slice(None))]
    return spots + [(0, out_rows + i * own, own, slice(i * width, (i + 1) * width)) for i in range(blocks)]


def self_forward_kernel(own, count_ref, place_ref, x_ref, *refs):
    act_ref, query_ref, key_ref, value_ref, mixed_ref, lse_ref, out_ref = refs[2:9]
    if own:
        w_ref, table_ref, bias, mixed_t, turned = refs[9:]

        @pl.when(pl.program_id(0) == 0)
        def _():
            place_weights(place_ref, refs[0], refs[1], attn_blocks(own), (w_ref,), turned, table_ref)
    else:
        w_ref, table_ref = refs[:2]
        bias, mixed_t = refs[9:]
    bias[...] = self_bias(bias.shape[0], count_ref[pl.program_id(0)])
    x = x_ref[0].astype(F32)
    hat, _ = normalize(x)
    act = (hat * (1.0 + table_ref[0:1]) + table_ref[1:2]).astype(LOW)
    act_ref[0] = act
    query = (dot_nn(act, w_ref[0]) + table_ref[6:7]).astype(LOW)
    key = dot_nn(act, w_ref[1]).astype(LOW)
    value = (dot_nn(act, w_ref[2]) + table_ref[7:8]).astype(LOW)
    query_ref[0], key_ref[0], value_ref[0] = query, key, value
    attend(query, key, value, bias, mixed_t, lse_ref)
    mixed = mixed_t[...].T.astype(LOW)
    mixed_ref[0] = mixed
    out_ref[0] = x + dot_nn(mixed, w_ref[3]) + table_ref[8:9]


def cross_forward_kernel(own, count_ref, place_ref, x_ref, mem_ref, table_ref, *refs):
    start = 2 if own else 1
    act_ref, query_ref, key_ref, value_ref, mixed_ref, lse_ref, out_ref = refs[start : start + 7]
    if own:
        w_ref, bias, mixed_t = refs[9:]

        @pl.when(pl.program_id(0) == 0)
        def _():
            place_weights(place_ref, refs[0], refs[1], attn_blocks(own), (w_ref,))
    else:
        w_ref = refs[0]
        bias, mixed_t = refs[8:]
    bias[...] = cross_bias(*bias.shape, count_ref[pl.program_id(0)])
    x = x_ref[0]
    hat, _ = normalize(x)
    act = (hat * (1.0 + table_ref[2:3]) + table_ref[3:4]).astype(LOW)
    act_ref[0] = act
    query = (dot_nn(act, w_ref[0]) + table_ref[9:10]).astype(LOW)
    key = dot_nn(mem_ref[0], w_ref[1]).astype(LOW)
    value = (dot_nn(mem_ref[0], w_ref[2]) + table_ref[10:11]).astype(LOW)
    query_ref[0], key_ref[0], value_ref[0] = query, key, value
    attend(query, key, value, bias, mixed_t, lse_ref)
    mixed = mixed_t[...].T.astype(LOW)
    mixed_ref[0] = mixed
    out_ref[0] = x + dot_nn(mixed, w_ref[3]) + table_ref[11:12]


def emit(place_ref, rows_ref, keep_ref, send_ref, row, own):
    planes, depths = keep_ref.shape[:2]
    for plane in range(planes):
        for depth in range(depths):
            base = ((depth ^ place_ref[0]) * planes + (plane ^ place_ref[1])) * 2
            for ref, core in ((keep_ref, place_ref[2]), (send_ref, 1 - place_ref[2])):
                first = pl.multiple_of((base + core) * own, own)
                ref[plane, depth, row : row + own] = rows_ref[pl.ds(first, own)].astype(ref.dtype)


def ffn_kernel(own, count_ref, place_ref, x_ref, cot_ref, table_ref, bias_ref, *refs):
    step = pl.program_id(0)
    seqs, length, width = x_ref.shape
    out_ref, grad_ref, first_ref, second_ref, small_ref = refs[2:7]
    act, gf, hidden, gpre, back = refs[7:12]
    chunk = hidden.shape[2]
    if own:
        rows, whole_in, whole_out = refs[12:]
        count = first_ref.shape[2]
        w_in_ref = whole_in.at[step]
        w_out_ref = whole_out.at[pl.ds(pl.multiple_of(step * chunk, chunk), chunk)]
    else:
        w_in_ref, w_out_ref = refs[:2]

    def valid(seq):
        row = lax.broadcasted_iota(jnp.int32, (length, 1), 0)
        return (row < count_ref[seq]).astype(F32)

    @pl.when(step == 0)
    def _():
        if own:
            out_rows = count // 2
            spots = [(1, 0, out_rows, slice(None))]
            spots += [(0, out_rows + i * own, own, i) for i in range(whole_in.shape[0])]
            place_weights(place_ref, refs[0], refs[1], spots, (whole_in, whole_out))
        small_ref[...] = jnp.zeros_like(small_ref)
        for seq in range(seqs):
            x = x_ref[seq]
            hat, _ = normalize(x)
            act[seq] = (hat * (1.0 + table_ref[4:5]) + table_ref[5:6]).astype(LOW)
            grad = (cot_ref[seq].astype(F32) * valid(seq)).astype(LOW)
            gf[seq] = grad
            small_ref[2:3] += column_sum(grad)
            out_ref[seq] = x + table_ref[12:13]
            back[seq] = jnp.zeros_like(back[seq])

    sums = jnp.zeros((1, chunk), F32)
    for seq in range(seqs):
        pre = dot_nn(act[seq], w_in_ref[...]) + bias_ref[...]
        cdf = 0.5 + 0.5 * lax.erf(pre * 0.5**0.5)
        slope = cdf + pre * (jnp.exp(pre * pre * -0.5) * 0.3989422804014327)
        unit = (pre * cdf).astype(LOW)
        hidden[seq] = unit
        grad_pre = (dot_nt(gf[seq], w_out_ref[...]) * slope).astype(LOW)
        gpre[seq] = grad_pre
        sums += column_sum(grad_pre)
        out_ref[seq] += dot_nn(unit, w_out_ref[...])
        back[seq] += dot_nt(grad_pre, w_in_ref[...])
    small_ref[pl.ds(8 + step, 1)] = sums
    tokens = seqs * length
    hidden_all, gf_all = hidden[...].reshape(tokens, -1), gf[...].reshape(tokens, -1)
    act_all, gpre_all = act[...].reshape(tokens, -1), gpre[...].reshape(tokens, -1)
    if own:
        planes = first_ref.shape[0]
        rows[...] = dot_tn(act_all, gpre_all)
        for spot in range(4):

            @pl.when(step == spot)
            def _():
                emit(place_ref, rows, first_ref, second_ref, count // 2 + spot * own, own)

        rows[...] = dot_tn(hidden_all, gf_all)
        depth = step ^ place_ref[0]
        for plane in range(planes):
            base = (plane ^ place_ref[1]) * 2
            for ref, core in ((first_ref, place_ref[2]), (second_ref, 1 - place_ref[2])):
                begin = pl.multiple_of((base + core) * (count // 2), count // 2)
                ref[plane, depth, : count // 2] = rows[pl.ds(begin, count // 2)].astype(ref.dtype)
    else:
        first_ref[...] = dot_tn(act_all, gpre_all)
        second_ref[...] = dot_tn(hidden_all, gf_all)

    @pl.when(step == pl.num_programs(0) - 1)
    def _():
        for seq in range(seqs):
            hat, inverse = normalize(x_ref[seq])
            grad = back[seq]
            small_ref[0:1] += column_sum(grad * hat)
            small_ref[1:2] += column_sum(grad)
            grad_ref[seq] = cot_ref[seq].astype(F32) * valid(seq) + normalize_back(
                grad, hat, inverse, table_ref[4:5]
            )


def begin_sums(*refs):
    @pl.when(pl.program_id(0) == 0)
    def _():
        for ref in refs:
            ref[...] = jnp.zeros_like(ref)


def end_sums(own, place_ref, gw, keep_ref, send_ref):
    @pl.when(pl.program_id(0) == pl.num_programs(0) - 1)
    def _():
        for index in range(4):
            emit(place_ref, gw.at[index], keep_ref, send_ref, index * own, own)


def cross_back_kernel(
    own, count_ref, place_ref, grad_ref, x_ref, act_ref, mem_ref, query_ref, key_ref,
    value_ref, mixed_ref, lse_ref, w_ref, table_ref, *refs,
):
    out_ref, gk_ref, gv_ref, small_ref = refs[:4]
    if own:
        keep_ref, send_ref, bias, gq_t, gw = refs[4:]
    else:
        gw, bias, gq_t = refs[4:]
    begin_sums(gw, small_ref)
    bias[...] = cross_bias(*bias.shape, count_ref[pl.program_id(0)])
    grad = grad_ref[0]
    low = grad.astype(LOW)
    gw[3] += dot_tn(mixed_ref[0], low)
    small_ref[4:5] += column_sum(low)
    grad_mixed = dot_nt(low, w_ref[3]).astype(LOW)
    attend_back(query_ref, key_ref, value_ref, grad_mixed, bias, lse_ref, gq_t, gk_ref, gv_ref)
    gq = (gq_t[...] * SCALE).T.astype(LOW)
    small_ref[2:3] += column_sum(gq)
    small_ref[3:4] += column_sum(gv_ref[0])
    gw[0] += dot_tn(act_ref[0], gq)
    gw[1] += dot_tn(mem_ref[0], gk_ref[0])
    gw[2] += dot_tn(mem_ref[0], gv_ref[0])
    back = dot_nt(gq, w_ref[0])
    hat, inverse = normalize(x_ref[0])
    small_ref[0:1] += column_sum(back * hat)
    small_ref[1:2] += column_sum(back)
    out_ref[0] = grad + normalize_back(back, hat, inverse, table_ref[2:3])
    if own:
        end_sums(own, place_ref, gw, keep_ref, send_ref)


def self_back_kernel(
    own, count_ref, place_ref, grad_ref, act_ref, query_ref, key_ref, value_ref, mixed_ref,
    lse_ref, w_ref, *refs,
):
    gq_ref, gk_ref, gv_ref, small_ref = refs[:4]
    if own:
        keep_ref, send_ref, bias, gq_t, gw = refs[4:]
    else:
        gw, bias, gq_t = refs[4:]
    begin_sums(gw, small_ref)
    bias[...] = self_bias(bias.shape[0], count_ref[pl.program_id(0)])
    low = grad_ref[0].astype(LOW)
    gw[3] += dot_tn(mixed_ref[0], low)
    small_ref[4:5] += column_sum(low)
    grad_mixed = dot_nt(low, w_ref[3]).astype(LOW)
    attend_back(query_ref, key_ref, value_ref, grad_mixed, bias, lse_ref, gq_t, gk_ref, gv_ref)
    gq = (gq_t[...] * SCALE).T.astype(LOW)
    gq_ref[0] = gq
    small_ref[2:3] += column_sum(gq)
    small_ref[3:4] += column_sum(gv_ref[0])
    gw[0] += dot_tn(act_ref[0], gq)
    gw[1] += dot_tn(act_ref[0], gk_ref[0])
    gw[2] += dot_tn(act_ref[0], gv_ref[0])
    if own:
        end_sums(own, place_ref, gw, keep_ref, send_ref)


def memory_kernel(gk_ref, gv_ref, w_ref, out_ref):
    out_ref[0] = dot_nt(gk_ref[0], w_ref[1]) + dot_nt(gv_ref[0], w_ref[2])


def input_kernel(own, place_ref, grad_ref, x_ref, gq_ref, gk_ref, gv_ref, w_ref, table_ref, *refs):
    out_ref, small_ref = refs[-4:-2] if own else refs[-2:]
    begin_sums(small_ref)
    back = dot_nt(gq_ref[0], w_ref[0]) + dot_nt(gk_ref[0], w_ref[1]) + dot_nt(gv_ref[0], w_ref[2])
    hat, inverse = normalize(x_ref[0].astype(F32))
    small_ref[0:1] += column_sum(back * hat)
    small_ref[1:2] += column_sum(back)
    out_ref[0] = grad_ref[0] + normalize_back(back, hat, inverse, table_ref[0:1])

    @pl.when(pl.program_id(0) == pl.num_programs(0) - 1)
    def _():
        one_ref, two_ref, three_ref = refs[:3]
        small_ref[2:4] = two_ref[0:2]
        small_ref[4:6] = three_ref[0:2]
        small_ref[6:9] = one_ref[2:5]
        small_ref[9:12] = two_ref[2:5]
        small_ref[12:13] = three_ref[2:3]
        small_ref[13:17] = three_ref[8:12]
        if own:
            parts_ref, turned = refs[-2:]
            wide = jnp.concatenate([small_ref[...], jnp.zeros((128 - small_ref.shape[0], small_ref.shape[1]), F32)], 0)
            turned[...] = wide.T
            _, planes, depths = parts_ref.shape[:3]
            for core in range(2):
                for plane in range(planes):
                    for depth in range(depths):
                        base = ((depth ^ place_ref[0]) * planes + (plane ^ place_ref[1])) * 2
                        first = pl.multiple_of((base + (core ^ place_ref[2])) * 16, 16)
                        for half in range(2):
                            rows = turned[pl.ds(pl.multiple_of(first + 8 * half, 8), 8)]
                            parts_ref[core, plane, depth, :, 128 * half : 128 * (half + 1)] = rows


def by_seq(*tail):
    return pl.BlockSpec((1,) + tail, lambda seq, *_: (seq,) + (0,) * len(tail))


def fixed(*shape):
    return pl.BlockSpec(shape, lambda *_: (0,) * len(shape))


def shape_of(shape, dtype):
    return jax.ShapeDtypeStruct(shape, dtype)


def call(kernel, name, work, grid, scalars, args, in_specs, outs, out_specs, scratch):
    return pl.pallas_call(
        kernel,
        out_shape=[shape_of(*out) for out in outs],
        grid_spec=pltpu.PrefetchScalarGridSpec(
            num_scalar_prefetch=len(scalars),
            grid=grid,
            in_specs=in_specs,
            out_specs=out_specs,
            scratch_shapes=scratch,
        ),
        compiler_params=pltpu.CompilerParams(vmem_limit_bytes=LIMIT),
        cost_estimate=pl.CostEstimate(flops=int(work * 1.1e9), bytes_accessed=1 << 20, transcendentals=0),
        name=name,
    )(*scalars, *args)


def self_forward(lengths, grid, x, weights):
    seqs, length, width = x.shape
    shape = x.shape
    block = by_seq(length, width)
    outs = [(shape, LOW)] * 5 + [((seqs, HEADS, length), F32), (shape, F32)]
    out_specs = [block] * 5 + [by_seq(HEADS, length), block]
    scratch = [pltpu.VMEM((length, length), F32), pltpu.VMEM((width, length), F32)]
    if grid.own:
        outs += [((4, width, width), LOW), ((24, width), F32)]
        out_specs += [fixed(4, width, width), fixed(24, width)]
        scratch += [pltpu.VMEM((width, 128), F32)]
    results = call(
        partial(self_forward_kernel, grid.own), "self_forward", 18, (seqs,), (lengths, grid.spot), (x, *weights),
        [block] + [fixed(*part.shape) for part in weights], outs, out_specs, scratch,
    )
    return results if grid.own else (*results, *weights)


def cross_forward(mem_lengths, grid, x, memory, table, weights):
    seqs, length, width = x.shape
    mem_len = memory.shape[1]
    block, mem_block = by_seq(length, width), by_seq(mem_len, width)
    shape, mem_shape = x.shape, memory.shape
    outs = [(shape, LOW), (shape, LOW), (mem_shape, LOW), (mem_shape, LOW), (shape, LOW)]
    outs += [((seqs, HEADS, length), F32), (shape, F32)]
    out_specs = [block, block, mem_block, mem_block, block, by_seq(HEADS, length), block]
    if grid.own:
        outs += [((4, width, width), LOW)]
        out_specs += [fixed(4, width, width)]
    results = call(
        partial(cross_forward_kernel, grid.own), "cross_forward", 24, (seqs,), (mem_lengths, grid.spot),
        (x, memory, table, *weights),
        [block, mem_block, fixed(*table.shape)] + [fixed(*part.shape) for part in weights], outs, out_specs,
        [pltpu.VMEM((mem_len, length), F32), pltpu.VMEM((width, length), F32)],
    )
    return results if grid.own else (*results, *weights)


def ffn(lengths, grid, x, cotangent, table, weights):
    seqs, length, width = x.shape
    blocks = 4
    chunk = grid.hidden // blocks
    bias = table[13:17].reshape(1, grid.hidden)
    act = pltpu.VMEM((seqs, length, width), LOW)
    wide = pltpu.VMEM((seqs, length, chunk), LOW)
    flat = pl.BlockSpec((1, chunk), lambda i, *_: (0, i))
    scratch = [act, act, wide, wide, pltpu.VMEM((seqs, length, width), F32)]
    if grid.own:
        parts = grid.sizes[1::-1] + (8 * grid.own, width)
        grads, grad_specs = [(parts, LOW), (parts, LOW)], [fixed(*parts), fixed(*parts)]
        specs = [fixed(*part.shape) for part in weights]
        scratch += [pltpu.VMEM((width, chunk), F32), pltpu.VMEM((blocks, width, chunk), LOW)]
        scratch += [pltpu.VMEM((grid.hidden, width), LOW)]
    else:
        cols = pl.BlockSpec((width, chunk), lambda i, *_: (0, i))
        rows = pl.BlockSpec((chunk, width), lambda i, *_: (i, 0))
        grads, grad_specs = [(part.shape, F32) for part in weights], [cols, rows]
        specs = [cols, rows]
    return call(
        partial(ffn_kernel, grid.own), "ffn", 24, (blocks,), (lengths, grid.spot),
        (x, cotangent, table, bias, *weights),
        [fixed(*x.shape), fixed(*x.shape), fixed(*table.shape), flat] + specs,
        [(x.shape, F32), (x.shape, F32)] + grads + [((16, width), F32)],
        [fixed(*x.shape), fixed(*x.shape)] + grad_specs + [fixed(16, width)],
        scratch,
    )


def back_call(kernel, name, work, counts, grid, args, in_specs, outs, out_specs, scratch):
    seqs, _, width = args[0].shape
    gw, small = (4, width, width), (8, width)
    outs, out_specs = outs + [(small, F32)], out_specs + [fixed(*small)]
    if grid.own:
        parts = grid.sizes[1::-1] + (4 * grid.own, width)
        outs, out_specs = outs + [(parts, LOW)] * 2, out_specs + [fixed(*parts)] * 2
        scratch = scratch + [pltpu.VMEM(gw, F32)]
    else:
        outs, out_specs = outs + [(gw, F32)], out_specs + [fixed(*gw)]
    return call(
        partial(kernel, grid.own), name, work, (seqs,), (counts, grid.spot), args, in_specs, outs, out_specs, scratch
    )


def cross_back(mem_lengths, grid, grad, x, act, memory, query, key, value, mixed, lse, weights, table):
    seqs, length, width = x.shape
    mem_len = key.shape[1]
    block, mem_block = by_seq(length, width), by_seq(mem_len, width)
    return back_call(
        cross_back_kernel, "cross_back", 30, mem_lengths, grid,
        (grad, x, act, memory, query, key, value, mixed, lse, weights, table),
        [block, block, block, mem_block, block, mem_block, mem_block, block, by_seq(HEADS, length),
         fixed(4, width, width), fixed(*table.shape)],
        [(x.shape, F32), (key.shape, LOW), (key.shape, LOW)],
        [block, mem_block, mem_block],
        [pltpu.VMEM((mem_len, length), F32), pltpu.VMEM((width, length), F32)],
    )


def self_back(lengths, grid, grad, act, query, key, value, mixed, lse, weights):
    seqs, length, width = query.shape
    block = by_seq(length, width)
    return back_call(
        self_back_kernel, "self_back", 22, lengths, grid,
        (grad, act, query, key, value, mixed, lse, weights),
        [block] * 6 + [by_seq(HEADS, length), fixed(4, width, width)],
        [(query.shape, LOW)] * 3, [block] * 3,
        [pltpu.VMEM((length, length), F32), pltpu.VMEM((width, length), F32)],
    )


def memory_grad(gk, gv, weights):
    seqs, mem_len, width = gk.shape
    block = by_seq(mem_len, width)
    return call(
        memory_kernel, "memory_grad", 4, (seqs,), (), (gk, gv, weights),
        [block, block, fixed(4, width, width)], [(gk.shape, F32)], [block], [],
    )[0]


def input_grad(grid, grad, x, gq, gk, gv, weights, table, smalls):
    seqs, length, width = x.shape
    block = by_seq(length, width)
    outs, out_specs, scratch = [(x.shape, F32), ((24, width), F32)], [block, fixed(24, width)], []
    if grid.own:
        parts = (2,) + grid.sizes[1::-1] + (8, 256)
        outs, out_specs, scratch = outs + [(parts, F32)], out_specs + [fixed(*parts)], [pltpu.VMEM((width, 128), F32)]
    return call(
        partial(input_kernel, grid.own), "input_grad", 5, (seqs,), (grid.spot,),
        (grad, x, gq, gk, gv, weights, table, *smalls),
        [block] * 5 + [fixed(4, width, width), fixed(*table.shape)] + [fixed(*small.shape) for small in smalls],
        outs, out_specs, scratch,
    )


def tie(value, *others):
    return lax.optimization_barrier((value, others))[0]


def add_all(parts):
    return sum(part.astype(F32) for part in parts)


class Grid:
    def __init__(self, dp, fsdp, own, hidden):
        self.sizes = (dp, fsdp // 2, 2)
        self.strides = (fsdp, 2, 1)
        self.devices = dp * fsdp
        self.hidden = hidden
        self.own = own if own % 16 == 0 and dp == 4 else 0
        index = lax.axis_index("fsdp")
        self.place = (lax.axis_index("dp"), index >> 1, index & 1)
        self.spot = jnp.stack(self.place).astype(jnp.int32)

    def swap(self, values, stage, step):
        stride = self.strides[stage]
        pairs = [(i, i ^ (step * stride)) for i in range(self.devices)]
        return lax.ppermute(values, AXES, pairs)

    def spread(self, values, stage):
        return jnp.stack(self.send(values, stage))

    def send(self, values, stage):
        return [values] + [self.swap(values, stage, step) for step in range(1, self.sizes[stage])]

    def fetch(self, parts, stage):
        return [parts[0]] + [self.swap(parts[step].astype(LOW), stage, step) for step in range(1, self.sizes[stage])]

    def absolute(self, mine, other):
        depths, planes, _ = self.sizes
        both = jnp.stack([mine, other], 2)
        for axis, stage in ((0, 1), (1, 0), (2, 2)):
            order = jnp.arange(self.sizes[stage]) ^ self.place[stage]
            both = jnp.take(both, order, axis)
        both = jnp.swapaxes(both, 0, 1)
        return both.reshape((self.devices,) + both.shape[3:])

    def relative(self, parts):
        depths, planes, _ = self.sizes
        both = jnp.swapaxes(parts.reshape(self.sizes + parts.shape[1:]), 0, 1)
        for axis, stage in ((0, 1), (1, 0), (2, 2)):
            order = jnp.arange(self.sizes[stage]) ^ self.place[stage]
            both = jnp.take(both, order, axis)
        return both[:, :, 0], both[:, :, 1].astype(LOW)


def adam_update(weight, grad, first, second, clip_scale, step, rate):
    clipped = grad * clip_scale
    first_new = 0.5 * first + 0.5 * clipped
    second_new = 0.55 * second + 0.45 * clipped * clipped
    fix_first = 1.0 - jnp.power(0.5, step)
    fix_second = 1.0 - jnp.power(0.55, step)
    weight_new = weight - rate * (
        first_new / fix_first / (jnp.sqrt(second_new / fix_second) + 1e-08) + 0.01 * weight
    )
    return (weight_new, first_new, second_new)


def local(
    dp,
    fsdp,
    inputs,
    memory,
    cotangent,
    lengths,
    mem_lengths,
    attn_weights,
    ffn_in,
    ffn_out,
    vectors,
    attn_first,
    attn_second,
    ffn_in_first,
    ffn_in_second,
    ffn_out_first,
    ffn_out_second,
    vector_first,
    vector_second,
):
    seqs, length, width = inputs.shape
    own = attn_weights.shape[1]
    hidden = ffn_in.shape[1]
    grid = Grid(dp, fsdp, own, hidden)
    blocks = hidden // width
    out_rows = ffn_out.shape[0]
    count = vectors.shape[0]

    self_low = attn_weights[:4].astype(LOW).reshape(4 * own, width)
    if grid.own:
        turned = jnp.pad(vectors.astype(LOW).T, ((0, 0), (0, 128 - count)))
        turned = jnp.concatenate([turned[:8], turned[8:]], 1)
        extra = jnp.pad(turned, ((0, 0), (0, width - 256)))
    else:
        extra = jnp.pad(vectors.astype(LOW).reshape(1, count * own), ((0, 7), (0, width - count * own)))
    self_chunk = jnp.concatenate([self_low, extra], 0)
    cross_chunk = attn_weights[4:].astype(LOW).reshape(4 * own, width)
    in_blocks = jnp.swapaxes(ffn_in.astype(LOW).reshape(own, blocks, width), 0, 1)
    ffn_chunk = jnp.concatenate([ffn_out.astype(LOW), in_blocks.reshape(blocks * own, width)], 0)

    def attn_whole(mine, other):
        if grid.own:
            return (mine, other)
        full = grid.absolute(mine, other)
        weights = jnp.swapaxes(full[:, : 4 * own].reshape(-1, 4, own, width), 0, 1).reshape(4, width, width)
        table = full[:, 4 * own :].reshape(grid.devices, -1)[:, : count * own]
        if table.size == 0:
            return (weights,)
        table = jnp.swapaxes(table.reshape(-1, count, own), 0, 1).reshape(count, width)
        return (weights, table.astype(F32))

    def ffn_whole(mine, other):
        if grid.own:
            return (mine, other)
        full = grid.absolute(mine, other)
        w_in = full[:, out_rows:].reshape(-1, blocks, own, width)
        return jnp.swapaxes(w_in, 1, 2).reshape(width, hidden), full[:, :out_rows].reshape(hidden, width)

    self_depth = grid.spread(self_chunk, 0)
    late_depth = grid.spread(tie(jnp.concatenate([cross_chunk, ffn_chunk], 0), self_depth), 0)
    self_plane = grid.spread(self_depth, 1)
    self_plane, late_depth = lax.optimization_barrier((self_plane, late_depth))
    cross_parts = grid.send(late_depth[:, : 4 * own], 1)
    first = self_forward(lengths, grid, inputs, attn_whole(self_plane, grid.swap(self_plane, 2, 1)))
    first, cross_parts = lax.optimization_barrier((first, cross_parts))
    act_one, query_one, key_one, value_one, mixed_one, lse_one, resid_one, w_self, table = first
    ffn_parts = grid.send(tie(late_depth[:, 4 * own :], cross_parts), 1)
    cross_plane = jnp.stack(cross_parts)
    second = cross_forward(
        mem_lengths, grid, resid_one, memory, table, attn_whole(cross_plane, grid.swap(cross_plane, 2, 1))
    )
    second, ffn_parts = lax.optimization_barrier((second, ffn_parts))
    act_two, query_two, key_two, value_two, mixed_two, lse_two, resid_two, w_cross = second
    ffn_plane = jnp.stack(ffn_parts)
    output, grad_two, ffn_keep, ffn_send, small_three = ffn(
        lengths, grid, resid_two, cotangent, table, ffn_whole(ffn_plane, grid.swap(ffn_plane, 2, 1))
    )
    if not grid.own:
        parts = jnp.swapaxes(ffn_keep.reshape(grid.devices, own, blocks, width), 1, 2)
        parts = jnp.concatenate(
            [ffn_send.reshape(grid.devices, out_rows, width), parts.reshape(grid.devices, blocks * own, width)], 1
        )
        ffn_keep, ffn_send = grid.relative(parts)

    def attn_parts(grads):
        if grid.own:
            return grads
        parts = jnp.swapaxes(grads[0].reshape(4, grid.devices, own, width), 0, 1)
        return grid.relative(parts.reshape(grid.devices, 4 * own, width))

    def meet(keep, send):
        return keep.astype(F32) + grid.swap(send, 2, 1).astype(F32)

    ffn_sum = meet(ffn_keep, ffn_send)
    grad_two, ffn_sum = lax.optimization_barrier((grad_two, ffn_sum))
    ffn_got = grid.fetch(ffn_sum, 1)
    cross = cross_back(
        mem_lengths, grid, grad_two, resid_one, act_two, memory, query_two, key_two, value_two, mixed_two,
        lse_two, w_cross, table,
    )
    cross, ffn_got = lax.optimization_barrier((cross, ffn_got))
    grad_one, gk_two, gv_two, small_two, *cross_grads = cross
    cross_sum = meet(*attn_parts(cross_grads))
    ffn_sum = add_all(ffn_got)
    grad_one, cross_sum, ffn_sum = lax.optimization_barrier((grad_one, cross_sum, ffn_sum))
    cross_got = grid.fetch(cross_sum, 1)
    state = self_back(
        lengths, grid, grad_one, act_one, query_one, key_one, value_one, mixed_one, lse_one, w_self
    )
    state, cross_got = lax.optimization_barrier((state, cross_got))
    gq_one, gk_one, gv_one, small_one, *self_grads = state
    self_keep, self_send = attn_parts(self_grads)
    late_got = grid.fetch(jnp.concatenate([add_all(cross_got), ffn_sum], 1), 0)
    self_got = grid.swap(self_send, 2, 1)
    grad_one_late = tie(grad_one, self_keep)
    smalls = (small_one, small_two, small_three)
    grad_input, grad_table, *table_parts = input_grad(
        grid, grad_one_late, inputs, gq_one, gk_one, gv_one, w_self, table, smalls
    )
    if grid.own:
        table_keep, table_send = table_parts[0][0], table_parts[0][1]
    else:
        parts = jnp.swapaxes(grad_table[:count].reshape(count, grid.devices, own), 0, 1)
        parts = jnp.pad(parts.reshape(grid.devices, count * own), ((0, 0), (0, -count * own % 256)))
        parts = jnp.pad(parts.reshape(grid.devices, -1, 256), ((0, 0), (0, 7), (0, 0)))[:, :8]
        table_keep, table_send = grid.relative(parts)
    table_sum = table_keep + grid.swap(table_send.astype(LOW), 2, 1).astype(F32)
    self_sum = self_keep.astype(F32) + self_got.astype(F32)
    table_sum = jnp.pad(table_sum, ((0, 0), (0, 0), (0, 0), (0, width - 256)))
    self_sum = jnp.concatenate([self_sum, table_sum], 2)
    last_got = grid.fetch(self_sum, 1)
    last_got, late_got = lax.optimization_barrier((last_got, late_got))
    last_share = add_all(grid.fetch(add_all(last_got), 0))
    late_share = add_all(late_got)
    cross_share, ffn_share = late_share[: 4 * own], late_share[4 * own :]
    self_share = last_share[: 4 * own]
    table_share = last_share[4 * own :, :256]
    if grid.own:
        table_share = jnp.swapaxes(table_share.reshape(8, 2, 128), 0, 1).reshape(own, 128)[:, :count].T
    else:
        table_share = table_share.reshape(-1)[: count * own].reshape(count, own)
    gk_late = tie(gk_two, last_share)
    grad_memory = memory_grad(gk_late, gv_two, w_cross)

    squares = sum(jnp.sum(share * share) for share in (ffn_share, cross_share, self_share, table_share))
    spread = jnp.broadcast_to(squares, (grid.devices, 8, 128))
    total_squares = jnp.sum(lax.all_to_all(spread, AXES, 0, 0)[:, 0, 0])
    grad_norm = jnp.sqrt(total_squares)
    clip_scale = jnp.minimum(1.0, 1.0 / (grad_norm + 1e-06))
    step = jnp.float32(STEP)
    attn_share = jnp.concatenate([self_share, cross_share], 0).reshape(8, own, width)
    in_share = jnp.swapaxes(ffn_share[out_rows:].reshape(blocks, own, width), 0, 1).reshape(own, hidden)
    out_share = ffn_share[:out_rows]
    attn_new = adam_update(attn_weights, attn_share, attn_first, attn_second, clip_scale, step, 0.04)
    first_new = adam_update(ffn_in, in_share, ffn_in_first, ffn_in_second, clip_scale, step, 0.04)
    second_new = adam_update(ffn_out, out_share, ffn_out_first, ffn_out_second, clip_scale, step, 0.04)
    table_new = adam_update(vectors, table_share, vector_first, vector_second, clip_scale, step, 0.25)
    return (
        output,
        grad_input,
        grad_memory,
        grad_norm.reshape(1),
        *attn_new,
        *first_new,
        *second_new,
        *table_new,
    )


def solution(mesh):
    both = ("dp", "fsdp")
    rows = P(both, None, None)
    attn, flat, vec = P(None, both, None), P(both, None), P(None, both)
    return jax.shard_map(
        partial(local, mesh.shape["dp"], mesh.shape["fsdp"]),
        mesh=mesh,
        in_specs=(rows, rows, rows, P(both), P(both), attn, flat, flat, vec)
        + (attn, attn, flat, flat, flat, flat, vec, vec),
        out_specs=(rows, rows, rows, P(), attn, attn, attn) + (flat,) * 6 + (vec,) * 3,
        check_vma=False,
    )
```

time: 342 us -> 265 us (0.77); the launches traced: 337 us -> 264 us
  waiting for transfers between devices: 77 us -> 37.2 us
  local copies, waits for them, and re-layouts: 43.7 us -> 10.5 us
  Pallas kernels: 120 us -> 136 us
  starting transfers between devices: 62.8 us -> 54.6 us
  other arithmetic: 27 us -> 19.4 us
    ppermute x42 -> x37, waiting for transfers between devices: 69 us -> 36 us  [swap(): return lax.ppermute(values, AXES, pairs)]
    pallas_call x5 -> x7, Pallas kernels: 120 us -> 136 us  [call(): pl.pallas_call(kernel, out_shape=[shape_of(*out) for out in outs], grid_s...]
    ppermute x42 -> x37, starting transfers between devices: 58.8 us -> 50 us  [swap(): return lax.ppermute(values, AXES, pairs)]
    reshape x8 -> x2, local copies, waits for them, and re-layouts: 8.72 us -> 0.01 us  [the longest x1 0.01 us: local(): ffn_in.astype(LOW).reshape(own, blocks, width)]
    all_to_all x1, waiting for transfers between devices: 7.96 us -> 1.17 us  [local(): total_squares = jnp.sum(lax.all_to_all(spread, AXES, 0, 0)[:, 0, 0])]
    dynamic_update_slice x23 -> x0, local copies, waits for them, and re-layouts: 5.05 us -> none  [gather(): lax.dynamic_update_index_in_dim(whole, parts[step], place ^ step, stage)]
    concatenate x10 -> x0, local copies, waits for them, and re-layouts: 4.53 us -> none  [the longest x1 3.27 us: local(): jnp.concatenate([grad_ffn_out.reshape(grid.devices, -1, width), grad_ffn_...]
    transpose x3 -> x0, local copies, waits for them, and re-layouts: 4.15 us -> none  [the longest x2 3.07 us: attn_unfold(): jnp.moveaxis(full.reshape(grid.devices, -1, own, width), 1, 0)]
  transfers between devices with their start and end apart: 43 -> 38, of which waited for: 19 -> 12; matrix products, arithmetic and copies ran while one was open for 13% -> 4% of each run, Pallas kernels for 13% -> 41%
where the time goes in v3:
time: 265 us; the launch traced here: 264 us
  Pallas kernels  136 us (51%)
  starting transfers between devices  54.6 us (21%)
  waiting for transfers between devices  37.2 us (14%)
  other arithmetic  19.4 us (7%)
  local copies, waits for them, and re-layouts  10.5 us (4%)
  between operations  5.84 us (2%)
    pallas_call x7, Pallas kernels, call(): pl.pallas_call(kernel, out_shape=[shape_of(*out) for out in outs], grid_s...  136 us
    ppermute x37, starting transfers between devices, swap(): return lax.ppermute(values, AXES, pairs)  50 us
    ppermute x37, waiting for transfers between devices, swap(): return lax.ppermute(values, AXES, pairs)  36 us
    unnamed x48, local copies, waits for them, and re-layouts  6.19 us
  transfers between devices with their start and end apart: 38, of which 12 were waited for; matrix products, arithmetic and copies ran while one was open for 4% of the time, Pallas kernels for 41%

profile of v3, /device:TPU:0, one launch (start us, length us, event | category | flops | bytes accessed | tf_op | source)
XLA Modules:
  0.0 263.9 jit_solution(4968029614345892030)
XLA Ops:
  0.6 0.7 convert_bitcast_fusion
  1.4 1.0 convert.32
  2.4 4.1 %collective-permute-start.1 = (bf16[72,512]{1,0:T(8,128)(2,1)S(1)}, bf16[72,512]{1,0:T(8,128)(2,1)S(1)}, u32[]{:S(2)}, u32[]{:S(2)}) collective-permute-start(bf16[72,512]{1,0:T(8,128)(2,1)S(1)} %get-tuple-element.254), channel_id=1, source_target_pairs={{0,16},{1,17},{2,18},{3,19},{4,20},{5,21},{6,22},{7,23},{8,24},{9,... | collective-permute-start | bytes 221192 | tf_op jit(solution)/shard_map/ppermute | solution.py:582
  6.5 1.6 collective-permute-start
  8.1 0.9 convert_element_type.149
  9.0 0.9 convert_element_type.148
  9.9 0.9 collective-permute-done
  10.8 3.4 %collective-permute-done.2 = bf16[72,512]{1,0:T(8,128)(2,1)S(1)} collective-permute-done((bf16[72,512]{1,0:T(8,128)(2,1)S(1)}, bf16[72,512]{1,0:T(8,128)(2,1)S(1)}, u32[]{:S(2)}, u32[]{:S(2)}) %collective-permute-start.2) | collective-permute-done | bytes 73760 | tf_op jit(solution)/shard_map/ppermute | solution.py:582
  14.3 1.7 collective-permute-start.8
  16.3 2.4 collective-permute-start.6
  18.7 2.4 collective-permute-start.5
  21.7 2.2 collective-permute-done.8
  23.8 1.5 collective-permute-start.3
  25.3 8.4 %collective-permute-done.7 = bf16[192,512]{1,0:T(8,128)(2,1)S(1)} collective-permute-done((bf16[192,512]{1,0:T(8,128)(2,1)S(1)}, bf16[192,512]{1,0:T(8,128)(2,1)S(1)}, u32[]{:S(2)}, u32[]{:S(2)}) %collective-permute-start.7) | collective-permute-done | bytes 196640 | tf_op jit(solution)/shard_map/ppermute | solution.py:582
  34.1 0.7 pad_add_fusion.place_ref
  34.9 2.5 collective-permute-start.12
  38.4 19.0 %self_forward.1 = (bf16[4,256,512]{2,1,0:T(8,128)(2,1)}, bf16[4,256,512]{2,1,0:T(8,128)(2,1)}, bf16[4,256,512]{2,1,0:T(8,128)(2,1)}, bf16[4,256,512]{2,1,0:T(8,1...) custom-call(s32[4]{0:T(128)} %count_ref.9, ...), custom_call_target="tpu_custom_call" | custom-call | flops 19800000512 | bytes 1048576 | tf_op jit(solution)/shard_map/self_forward/pallas_call | solution.py:410
  57.5 0.7 copy-done.12
  58.2 1.1 pad_maximum_fusion.3.refs_0_
  59.4 2.5 collective-permute-start.16
  62.9 24.9 %cross_forward.1 = (bf16[4,256,512]{2,1,0:T(8,128)(2,1)}, bf16[4,256,512]{2,1,0:T(8,128)(2,1)}, bf16[4,512,512]{2,1,0:T(8,128)(2,1)}, bf16[4,512,512]{2,1,0:T(8,...) custom-call(s32[4]{0:T(128)} %count_ref.8, ...), custom_call_target="tpu_custom_call" | custom-call | flops 26400000000 | bytes 1048576 | tf_op jit(solution)/shard_map/cross_forward/pallas_call | solution.py:410
  87.9 0.8 copy-done.9
  88.7 1.6 pad_maximum_fusion.refs_0_
  90.4 0.8 slice_bitcast_fusion.20
  91.2 0.6 copy.43
  91.8 2.7 %collective-permute-done.17.refs_1_ = bf16[4,4,128,512]{3,2,1,0:T(8,128)(2,1)S(1)} collective-permute-done((bf16[4,4,128,512]{3,2,1,0:T(8,128)(2,1)S(1)}, bf16[4,4,128,512]{3,2,1,0:T(8,128)(2,1)S(1)}, u32[]{:S(2)}, u32[]{:S(2)}) %collective-permute-start.17) | collective-permute-done | bytes 2097184 | tf_op jit(solution)/shard_map/ppermute | solution.py:582
  94.6 1.4 copy-done.21
  95.9 27.6 %ffn.1 = (f32[4,256,512]{2,1,0:T(8,128)}, f32[4,256,512]{2,1,0:T(8,128)}, bf16[4,4,128,512]{3,2,1,0:T(8,128)(2,1)}, bf16[4,4,128,512]{3,2,1,0:T(8,128)(2,1)}, f32[16,512]{1,0:T(8,128)}) custom-call(s32[4]{0:T(128)} %count_ref.9, s32[3]{0:T(128)} %pad_add_fusion.place_ref, f32[4,256,512]{2,1,0:T(8,128)} %get-tuple-element.143.x_ref, ...), custom_call_target="tpu_custom_call" | custom-call | flops 26400000000 | bytes 1048576 | tf_op jit(solution)/shard_map/ffn/pallas_call | solution.py:410
  123.7 4.2 %collective-permute-done.18 = bf16[4,4,128,512]{3,2,1,0:T(8,128)(2,1)S(1)} collective-permute-done((bf16[4,4,128,512]{3,2,1,0:T(8,128)(2,1)}, bf16[4,4,128,512]{3,2,1,0:T(8,128)(2,1)S(1)}, u32[]{:S(2)}, u32[]{:S(2)}) %collective-permute-start.18) | collective-permute-done | bytes 2097184 | tf_op jit(solution)/shard_map/ppermute | solution.py:582
  128.0 2.2 convert_add_fusion
  130.5 1.7 copy-done
  132.4 2.5 collective-permute-start.21
  136.0 29.3 %cross_back.1 = (f32[4,256,512]{2,1,0:T(8,128)}, bf16[4,512,512]{2,1,0:T(8,128)(2,1)}, bf16[4,512,512]{2,1,0:T(8,128)(2,1)}, f32[8,512]{1,0:T(8,128)}, bf16[4,4,...) custom-call(s32[4]{0:T(128)} %count_ref.8, s32[3]{0:T(128)} %pad_add_fusion.place_ref, ...), custom_call_target="tpu_custom_call" | custom-call | flops 32999999488 | bytes 1048576 | tf_op jit(solution)/shard_map/cross_back/pallas_call | solution.py:410
  165.3 1.4 slice_bitcast_fusion
  167.1 2.3 collective-permute-done.22
  169.9 0.9 slice_bitcast_fusion.9
  170.8 2.5 collective-permute-start.25
  174.3 20.5 %self_back.1 = (bf16[4,256,512]{2,1,0:T(8,128)(2,1)}, bf16[4,256,512]{2,1,0:T(8,128)(2,1)}, bf16[4,256,512]{2,1,0:T(8,128)(2,1)}, f32[8,512]{1,0:T(8,128)}, bf16...) custom-call(s32[4]{0:T(128)} %count_ref.9, s32[3]{0:T(128)} %pad_add_fusion.place_ref, ...), custom_call_target="tpu_custom_call" | custom-call | flops 24199999488 | bytes 1048576 | tf_op jit(solution)/shard_map/self_back/pallas_call | solution.py:410
  195.0 8.1 %input_grad.1 = (f32[4,256,512]{2,1,0:T(8,128)}, f32[24,512]{1,0:T(8,128)}, f32[2,4,4,8,256]{4,3,2,1,0:T(8,128)}) custom-call(s32[3]{0:T(128)} %pad_add_fusion.place_ref, f32[4,256,512]{2,1,0:T(8,128)} %get-tuple-element.190.grad_ref, bf16[4,256,512]{2,1,0:T(8,128)(2,1)} %x_ref.3, bf16[4,256,512]{2,1,0:T(8,128)(2,1)} %get-tuple-element.191.gq_ref, ...), custom_call_target="tpu_custom_call" | custom-call | flops 5500000256 | bytes 1048576 | tf_op jit(solution)/shard_map/input_grad/pallas_call | solution.py:410
  203.1 0.9 fusion.10
  204.5 1.2 convert_add_fusion.5
  205.9 2.5 collective-permute-start.33
  208.4 4.1 %collective-permute-start.32 = (bf16[192,512]{1,0:T(8,128)(2,1)S(1)}, bf16[192,512]{1,0:T(8,128)(2,1)S(1)}, u32[]{:S(2)}, u32[]{:S(2)}) collective-permute-start(bf16[192,512]{1,0:T(8,128)(2,1)S(1)} %get-tuple-element.240), channel_id=1, source_target_pairs={{0,16},{1,17},{2,18},{3,19},{4,20},{5,21},{6,22},{7,23},{8,24},{9,... | collective-permute-start | bytes 589832 | tf_op jit(solution)/shard_map/ppermute | solution.py:582
  213.1 2.5 collective-permute-start.30
  217.0 6.7 %collective-permute-start.31 = (bf16[192,512]{1,0:T(8,128)(2,1)S(1)}, bf16[192,512]{1,0:T(8,128)(2,1)S(1)}, u32[]{:S(2)}, u32[]{:S(2)}) collective-permute-start(bf16[192,512]{1,0:T(8,128)(2,1)S(1)} %get-tuple-element.241), channel_id=1, source_target_pairs={{0,8},{1,9},{2,10},{3,11},{4,12},{5,13},{6,14},{7,15},{8,0},{9,1},... | collective-permute-start | bytes 589832 | tf_op jit(solution)/shard_map/ppermute | solution.py:582
  223.7 3.6 %collective-permute-done.32 = bf16[192,512]{1,0:T(8,128)(2,1)S(1)} collective-permute-done((bf16[192,512]{1,0:T(8,128)(2,1)S(1)}, bf16[192,512]{1,0:T(8,128)(2,1)S(1)}, u32[]{:S(2)}, u32[]{:S(2)}) %collective-permute-start.32) | collective-permute-done | bytes 196640 | tf_op jit(solution)/shard_map/ppermute | solution.py:582
  227.3 4.1 %collective-permute-done.31 = bf16[192,512]{1,0:T(8,128)(2,1)S(1)} collective-permute-done((bf16[192,512]{1,0:T(8,128)(2,1)S(1)}, bf16[192,512]{1,0:T(8,128)(2,1)S(1)}, u32[]{:S(2)}, u32[]{:S(2)}) %collective-permute-start.31) | collective-permute-done | bytes 196640 | tf_op jit(solution)/shard_map/ppermute | solution.py:582
  231.8 2.5 collective-permute-start.36
  234.2 1.0 collective-permute-start.35
  235.3 0.7 fusion.4
  236.0 0.6 multiply_reduce_fusion.1
  237.9 0.8 collective-permute-done.36
  238.8 3.2 %collective-permute-done.35 = bf16[72,512]{1,0:T(8,128)(2,1)S(1)} collective-permute-done((bf16[72,512]{1,0:T(8,128)(2,1)S(1)}, bf16[72,512]{1,0:T(8,128)(2,1)S(1)}, u32[]{:S(2)}, u32[]{:S(2)}) %collective-permute-start.35) | collective-permute-done | bytes 73760 | tf_op jit(solution)/shard_map/ppermute | solution.py:582
  242.1 0.6 fusion.25
  242.7 0.6 multiply_reduce_fusion.2
  244.6 0.7 broadcast_in_dim.3
  245.3 4.6 %all-to-all-start = ((f32[32,8,128]{2,1,0:T(8,128)}), f32[32,8,128]{2,1,0:T(8,128)S(1)}, u32[]{:S(2)}, u32[]{:S(2)}) async-start(f32[32,8,128]{2,1,0:T(8,128)} %broadcast_in_dim.3), calls=%async_computation | async-start | bytes 262144 | tf_op jit(solution)/shard_map/all_to_all | solution.py:770
  249.9 6.9 %memory_grad.1 = f32[4,512,512]{2,1,0:T(8,128)} custom-call(bf16[4,512,512]{2,1,0:T(8,128)(2,1)} %get-tuple-element.210.gk_ref, bf16[4,512,512]{2,1,0:T(8,128)(2,1)} %get-tuple-element.211.gv_ref, bf16[4,512,512]{2,1,0:T(8,128)(2,1)} %get-tuple-element.159.w_ref), custom_call_target="tpu_custom_call" | custom-call | flops 4400000000 | bytes 1048576 | tf_op jit(solution)/shard_map/memory_grad/pallas_call | solution.py:410
  256.9 1.2 all-to-all-done
  258.1 0.6 slice_reduce_fusion
  259.5 0.8 multiply_subtract_fusion.1
  260.3 0.6 multiply_subtract_fusion.3
  261.0 0.8 multiply_subtract_fusion.2
  261.8 1.0 multiply_subtract_fusion
  (122 shorter events, 10.5 us)
Async XLA Ops:
  2.4 7.5 %collective-permute-start.1 = (bf16[72,512]{1,0:T(8,128)(2,1)S(1)}, bf16[72,512]{1,0:T(8,128)(2,1)S(1)}, u32[]{:S(2)}, u32[]{:S(2)}) collective-permute-start(bf16[72,512]{1,0:T(8,128)(2,1)S(1)} %get-tuple-element.254), channel_id=1, source_target_pairs={{0,16},{1,17},{2,18},{3,19},{4,20},{5,21},{6,22},{7,23},{8,24},{9,... | collective-permute-start | bytes 221192 | tf_op jit(solution)/shard_map/ppermute | solution.py:582
  6.5 4.4 %collective-permute-start = (bf16[72,512]{1,0:T(8,128)(2,1)S(1)}, bf16[72,512]{1,0:T(8,128)(2,1)S(1)}, u32[]{:S(2)}, u32[]{:S(2)}) collective-permute-start(bf16[72,512]{1,0:T(8,128)(2,1)S(1)} %get-tuple-element.254), channel_id=1, source_target_pairs={{0,8},{1,9},{2,10},{3,11},{4,12},{5,13},{6,14},{7,15},{8,0},{9,1},... | collective-permute-start | bytes 221192 | tf_op jit(solution)/shard_map/ppermute | solution.py:582
  8.1 6.2 %collective-permute-start.2 = (bf16[72,512]{1,0:T(8,128)(2,1)S(1)}, bf16[72,512]{1,0:T(8,128)(2,1)S(1)}, u32[]{:S(2)}, u32[]{:S(2)}) collective-permute-start(bf16[72,512]{1,0:T(8,128)(2,1)S(1)} %get-tuple-element.254), channel_id=1, source_target_pairs={{0,24},{1,25},{2,26},{3,27},{4,28},{5,29},{6,30},{7,31},{8,16},{9,... | collective-permute-start | bytes 221192 | tf_op jit(solution)/shard_map/ppermute | solution.py:582
  14.3 9.6 %collective-permute-start.8 = (bf16[192,512]{1,0:T(8,128)(2,1)S(1)}, bf16[192,512]{1,0:T(8,128)(2,1)S(1)}, u32[]{:S(2)}, u32[]{:S(2)}) collective-permute-start(bf16[192,512]{1,0:T(8,128)(2,1)S(1)} %pad_maximum_fusion.6), channel_id=1, source_target_pairs={{0,24},{1,25},{2,26},{3,27},{4,28},{5,29},{6,30},{7,31},{8,16},{9,... | collective-permute-start | bytes 589832 | tf_op jit(solution)/shard_map/ppermute | solution.py:582
  16.0 17.8 %collective-permute-start.7 = (bf16[192,512]{1,0:T(8,128)(2,1)S(1)}, bf16[192,512]{1,0:T(8,128)(2,1)S(1)}, u32[]{:S(2)}, u32[]{:S(2)}) collective-permute-start(bf16[192,512]{1,0:T(8,128)(2,1)S(1)} %pad_maximum_fusion.6), channel_id=1, source_target_pairs={{0,16},{1,17},{2,18},{3,19},{4,20},{5,21},{6,22},{7,23},{8,24},{9,... | collective-permute-start | bytes 589832 | tf_op jit(solution)/shard_map/ppermute | solution.py:582
  16.3 17.4 %collective-permute-start.6 = (bf16[192,512]{1,0:T(8,128)(2,1)S(1)}, bf16[192,512]{1,0:T(8,128)(2,1)S(1)}, u32[]{:S(2)}, u32[]{:S(2)}) collective-permute-start(bf16[192,512]{1,0:T(8,128)(2,1)S(1)} %pad_maximum_fusion.6), channel_id=1, source_target_pairs={{0,8},{1,9},{2,10},{3,11},{4,12},{5,13},{6,14},{7,15},{8,0},{9,1},... | collective-permute-start | bytes 589832 | tf_op jit(solution)/shard_map/ppermute | solution.py:582
  18.7 15.1 %collective-permute-start.5 = (bf16[4,72,512]{2,1,0:T(8,128)(2,1)S(1)}, bf16[4,72,512]{2,1,0:T(8,128)(2,1)S(1)}, u32[]{:S(2)}, u32[]{:S(2)}) collective-permute-start(bf16[4,72,512]{2,1,0:T(8,128)(2,1)S(1)} %get-tuple-element.248), channel_id=1, source_target_pairs={{0,6},{1,7},{2,4},{3,5},{4,2},{5,3},{6,0},{7,1},{8,14},{9,15},{10,... | collective-permute-start | bytes 884744 | tf_op jit(solution)/shard_map/ppermute | solution.py:582
  21.2 12.7 %collective-permute-start.4 = (bf16[4,72,512]{2,1,0:T(8,128)(2,1)S(1)}, bf16[4,72,512]{2,1,0:T(8,128)(2,1)S(1)}, u32[]{:S(2)}, u32[]{:S(2)}) collective-permute-start(bf16[4,72,512]{2,1,0:T(8,128)(2,1)S(1)} %get-tuple-element.248), channel_id=1, source_target_pairs={{0,4},{1,5},{2,6},{3,7},{4,0},{5,1},{6,2},{7,3},{8,12},{9,13},{10,... | collective-permute-start | bytes 884744 | tf_op jit(solution)/shard_map/ppermute | solution.py:582
  23.8 10.0 %collective-permute-start.3 = (bf16[4,72,512]{2,1,0:T(8,128)(2,1)S(1)}, bf16[4,72,512]{2,1,0:T(8,128)(2,1)S(1)}, u32[]{:S(2)}, u32[]{:S(2)}) collective-permute-start(bf16[4,72,512]{2,1,0:T(8,128)(2,1)S(1)} %get-tuple-element.248), channel_id=1, source_target_pairs={{0,2},{1,3},{2,0},{3,1},{4,6},{5,7},{6,4},{7,5},{8,10},{9,11},{10,... | collective-permute-start | bytes 884744 | tf_op jit(solution)/shard_map/ppermute | solution.py:582
  34.0 4.4 %copy-start.2 = (bf16[4,4,72,512]{3,2,1,0:T(8,128)(2,1)}, bf16[4,4,72,512]{3,2,1,0:T(8,128)(2,1)S(1)}, u32[]{:S(2)}) copy-start(bf16[4,4,72,512]{3,2,1,0:T(8,128)(2,1)S(1)} %pad_maximum_fusion.2.refs_0_) | copy-start | bytes 3538948
  34.0 4.4 %collective-permute-start.9 = (bf16[4,4,72,512]{3,2,1,0:T(8,128)(2,1)S(1)}, bf16[4,4,72,512]{3,2,1,0:T(8,128)(2,1)}, u32[]{:S(2)}, u32[]{:S(2)}) collective-permute-start(bf16[4,4,72,512]{3,2,1,0:T(8,128)(2,1)S(1)} %pad_maximum_fusion.2.refs_0_), channel_id=1, source_target_pairs={{0,1},{1,0},{2,3},{3,2},{4,5},{5,4},{6,7},{7,6},{8,9},{9,8},{10,11... | collective-permute-start | bytes 3538952 | tf_op jit(solution)/shard_map/ppermute | solution.py:582
  34.9 22.6 %collective-permute-start.12 = (bf16[4,64,512]{2,1,0:T(8,128)(2,1)S(1)}, bf16[4,64,512]{2,1,0:T(8,128)(2,1)S(1)}, u32[]{:S(2)}, u32[]{:S(2)}) collective-permute-start(bf16[4,64,512]{2,1,0:T(8,128)(2,1)S(1)} %slice.135), channel_id=1, source_target_pairs={{0,6},{1,7},{2,4},{3,5},{4,2},{5,3},{6,0},{7,1},{8,14},{9,15},{10,... | collective-permute-start | bytes 786440 | tf_op jit(solution)/shard_map/ppermute | solution.py:582
  37.4 20.0 %collective-permute-start.11 = (bf16[4,64,512]{2,1,0:T(8,128)(2,1)S(1)}, bf16[4,64,512]{2,1,0:T(8,128)(2,1)S(1)}, u32[]{:S(2)}, u32[]{:S(2)}) collective-permute-start(bf16[4,64,512]{2,1,0:T(8,128)(2,1)S(1)} %slice.135), channel_id=1, source_target_pairs={{0,4},{1,5},{2,6},{3,7},{4,0},{5,1},{6,2},{7,3},{8,12},{9,13},{10,... | collective-permute-start | bytes 786440 | tf_op jit(solution)/shard_map/ppermute | solution.py:582
  37.9 19.6 %collective-permute-start.10 = (bf16[4,64,512]{2,1,0:T(8,128)(2,1)S(1)}, bf16[4,64,512]{2,1,0:T(8,128)(2,1)S(1)}, u32[]{:S(2)}, u32[]{:S(2)}) collective-permute-start(bf16[4,64,512]{2,1,0:T(8,128)(2,1)S(1)} %slice.135), channel_id=1, source_target_pairs={{0,2},{1,3},{2,0},{3,1},{4,6},{5,7},{6,4},{7,5},{8,10},{9,11},{10,... | collective-permute-start | bytes 786440 | tf_op jit(solution)/shard_map/ppermute | solution.py:582
  57.5 0.7 copy-start.12
  59.2 3.7 %copy-start.4 = (bf16[4,4,64,512]{3,2,1,0:T(8,128)(2,1)}, bf16[4,4,64,512]{3,2,1,0:T(8,128)(2,1)S(1)}, u32[]{:S(2)}) copy-start(bf16[4,4,64,512]{3,2,1,0:T(8,128)(2,1)S(1)} %pad_maximum_fusion.3.refs_0_) | copy-start | bytes 3145732
  59.3 3.7 %collective-permute-start.13 = (bf16[4,4,64,512]{3,2,1,0:T(8,128)(2,1)S(1)}, bf16[4,4,64,512]{3,2,1,0:T(8,128)(2,1)}, u32[]{:S(2)}, u32[]{:S(2)}) collective-permute-start(bf16[4,4,64,512]{3,2,1,0:T(8,128)(2,1)S(1)} %pad_maximum_fusion.3.refs_0_), channel_id=1, source_target_pairs={{0,1},{1,0},{2,3},{3,2},{4,5},{5,4},{6,7},{7,6},{8,9},{9,8},{10,11... | collective-permute-start | bytes 3145736 | tf_op jit(solution)/shard_map/ppermute | solution.py:582
  59.4 28.5 %collective-permute-start.16 = (bf16[4,128,512]{2,1,0:T(8,128)(2,1)S(1)}, bf16[4,128,512]{2,1,0:T(8,128)(2,1)}, u32[]{:S(2)}, u32[]{:S(2)}) collective-permute-start(bf16[4,128,512]{2,1,0:T(8,128)(2,1)S(1)} %slice.136), channel_id=1, source_target_pairs={{0,6},{1,7},{2,4},{3,5},{4,2},{5,3},{6,0},{7,1},{8,14},{9,15},{10,... | collective-permute-start | bytes 1572872 | tf_op jit(solution)/shard_map/ppermute | solution.py:582
  61.9 26.0 %collective-permute-start.15 = (bf16[4,128,512]{2,1,0:T(8,128)(2,1)S(1)}, bf16[4,128,512]{2,1,0:T(8,128)(2,1)}, u32[]{:S(2)}, u32[]{:S(2)}) collective-permute-start(bf16[4,128,512]{2,1,0:T(8,128)(2,1)S(1)} %slice.136), channel_id=1, source_target_pairs={{0,4},{1,5},{2,6},{3,7},{4,0},{5,1},{6,2},{7,3},{8,12},{9,13},{10,... | collective-permute-start | bytes 1572872 | tf_op jit(solution)/shard_map/ppermute | solution.py:582
  62.4 25.5 %collective-permute-start.14 = (bf16[4,128,512]{2,1,0:T(8,128)(2,1)S(1)}, bf16[4,128,512]{2,1,0:T(8,128)(2,1)S(1)}, u32[]{:S(2)}, u32[]{:S(2)}) collective-permute-start(bf16[4,128,512]{2,1,0:T(8,128)(2,1)S(1)} %slice.136), channel_id=1, source_target_pairs={{0,2},{1,3},{2,0},{3,1},{4,6},{5,7},{6,4},{7,5},{8,10},{9,11},{10,... | collective-permute-start | bytes 1572872 | tf_op jit(solution)/shard_map/ppermute | solution.py:582
  87.9 0.8 copy-start.9
  90.3 5.6 %copy-start.1 = (bf16[4,4,128,512]{3,2,1,0:T(8,128)(2,1)}, bf16[4,4,128,512]{3,2,1,0:T(8,128)(2,1)S(1)}, u32[]{:S(2)}) copy-start(bf16[4,4,128,512]{3,2,1,0:T(8,128)(2,1)S(1)} %pad_maximum_fusion.refs_0_) | copy-start | bytes 6291460
  90.3 4.2 %collective-permute-start.17 = (bf16[4,4,128,512]{3,2,1,0:T(8,128)(2,1)S(1)}, bf16[4,4,128,512]{3,2,1,0:T(8,128)(2,1)S(1)}, u32[]{:S(2)}, u32[]{:S(2)}) collective-permute-start(bf16[4,4,128,512]{3,2,1,0:T(8,128)(2,1)S(1)} %pad_maximum_fusion.refs_0_), channel_id=1, source_target_pairs={{0,1},{1,0},{2,3},{3,2},{4,5},{5,4},{6,7},{7,6},{8,9},{9,8},{10,11... | collective-permute-start | bytes 6291464 | tf_op jit(solution)/shard_map/ppermute | solution.py:582
  94.6 1.4 copy-start.21
  123.6 4.4 %collective-permute-start.18 = (bf16[4,4,128,512]{3,2,1,0:T(8,128)(2,1)}, bf16[4,4,128,512]{3,2,1,0:T(8,128)(2,1)S(1)}, u32[]{:S(2)}, u32[]{:S(2)}) collective-permute-start(bf16[4,4,128,512]{3,2,1,0:T(8,128)(2,1)} %get-tuple-element.151), channel_id=1, source_target_pairs={{0,1},{1,0},{2,3},{3,2},{4,5},{5,4},{6,7},{7,6},{8,9},{9,8},{10,11... | collective-permute-start | bytes 6291464 | tf_op jit(solution)/shard_map/ppermute | solution.py:582
  130.2 2.0 copy-start
  132.4 34.3 %collective-permute-start.21 = (bf16[4,128,512]{2,1,0:T(8,128)(2,1)S(1)}, bf16[4,128,512]{2,1,0:T(8,128)(2,1)S(1)}, u32[]{:S(2)}, u32[]{:S(2)}) collective-permute-start(bf16[4,128,512]{2,1,0:T(8,128)(2,1)S(1)} %get-tuple-element.230), channel_id=1, source_target_pairs={{0,6},{1,7},{2,4},{3,5},{4,2},{5,3},{6,0},{7,1},{8,14},{9,15},{10,... | collective-permute-start | bytes 1572872 | tf_op jit(solution)/shard_map/ppermute | solution.py:582
  134.9 31.8 %collective-permute-start.20 = (bf16[4,128,512]{2,1,0:T(8,128)(2,1)S(1)}, bf16[4,128,512]{2,1,0:T(8,128)(2,1)S(1)}, u32[]{:S(2)}, u32[]{:S(2)}) collective-permute-start(bf16[4,128,512]{2,1,0:T(8,128)(2,1)S(1)} %get-tuple-element.231), channel_id=1, source_target_pairs={{0,4},{1,5},{2,6},{3,7},{4,0},{5,1},{6,2},{7,3},{8,12},{9,13},{10,... | collective-permute-start | bytes 1572872 | tf_op jit(solution)/shard_map/ppermute | solution.py:582
  135.4 31.3 %collective-permute-start.19 = (bf16[4,128,512]{2,1,0:T(8,128)(2,1)S(1)}, bf16[4,128,512]{2,1,0:T(8,128)(2,1)S(1)}, u32[]{:S(2)}, u32[]{:S(2)}) collective-permute-start(bf16[4,128,512]{2,1,0:T(8,128)(2,1)S(1)} %get-tuple-element.232), channel_id=1, source_target_pairs={{0,2},{1,3},{2,0},{3,1},{4,6},{5,7},{6,4},{7,5},{8,10},{9,11},{10,... | collective-permute-start | bytes 1572872 | tf_op jit(solution)/shard_map/ppermute | solution.py:582
  165.2 1.5 copy-start.22
  166.6 2.8 %copy-start.6 = (bf16[4,4,64,512]{3,2,1,0:T(8,128)(2,1)S(1)}, bf16[4,4,64,512]{3,2,1,0:T(8,128)(2,1)}, u32[]{:S(2)}) copy-start(bf16[4,4,64,512]{3,2,1,0:T(8,128)(2,1)} %get-tuple-element.168) | copy-start | bytes 3145732
  166.8 2.7 %collective-permute-start.22 = (bf16[4,4,64,512]{3,2,1,0:T(8,128)(2,1)S(1)}, bf16[4,4,64,512]{3,2,1,0:T(8,128)(2,1)S(1)}, u32[]{:S(2)}, u32[]{:S(2)}) collective-permute-start(bf16[4,4,64,512]{3,2,1,0:T(8,128)(2,1)S(1)} %copy-done.22), channel_id=1, source_target_pairs={{0,1},{1,0},{2,3},{3,2},{4,5},{5,4},{6,7},{7,6},{8,9},{9,8},{10,11... | collective-permute-start | bytes 3145736 | tf_op jit(solution)/shard_map/ppermute | solution.py:582
  170.8 24.1 %collective-permute-start.25 = (bf16[4,64,512]{2,1,0:T(8,128)(2,1)}, bf16[4,64,512]{2,1,0:T(8,128)(2,1)S(1)}, u32[]{:S(2)}, u32[]{:S(2)}) collective-permute-start(bf16[4,64,512]{2,1,0:T(8,128)(2,1)} %get-tuple-element.236), channel_id=1, source_target_pairs={{0,6},{1,7},{2,4},{3,5},{4,2},{5,3},{6,0},{7,1},{8,14},{9,15},{10,... | collective-permute-start | bytes 786440 | tf_op jit(solution)/shard_map/ppermute | solution.py:582
  173.3 21.6 %collective-permute-start.24 = (bf16[4,64,512]{2,1,0:T(8,128)(2,1)}, bf16[4,64,512]{2,1,0:T(8,128)(2,1)}, u32[]{:S(2)}, u32[]{:S(2)}) collective-permute-start(bf16[4,64,512]{2,1,0:T(8,128)(2,1)} %get-tuple-element.237), channel_id=1, source_target_pairs={{0,4},{1,5},{2,6},{3,7},{4,0},{5,1},{6,2},{7,3},{8,12},{9,13},{10,... | collective-permute-start | bytes 786440 | tf_op jit(solution)/shard_map/ppermute | solution.py:582
  173.8 21.1 %collective-permute-start.23 = (bf16[4,64,512]{2,1,0:T(8,128)(2,1)}, bf16[4,64,512]{2,1,0:T(8,128)(2,1)}, u32[]{:S(2)}, u32[]{:S(2)}) collective-permute-start(bf16[4,64,512]{2,1,0:T(8,128)(2,1)} %get-tuple-element.238), channel_id=1, source_target_pairs={{0,2},{1,3},{2,0},{3,1},{4,6},{5,7},{6,4},{7,5},{8,10},{9,11},{10,... | collective-permute-start | bytes 786440 | tf_op jit(solution)/shard_map/ppermute | solution.py:582
  194.9 17.6 %collective-permute-start.26 = (bf16[4,4,64,512]{3,2,1,0:T(8,128)(2,1)}, bf16[4,4,64,512]{3,2,1,0:T(8,128)(2,1)S(1)}, u32[]{:S(2)}, u32[]{:S(2)}) collective-permute-start(bf16[4,4,64,512]{3,2,1,0:T(8,128)(2,1)} %get-tuple-element.199), channel_id=1, source_target_pairs={{0,1},{1,0},{2,3},{3,2},{4,5},{5,4},{6,7},{7,6},{8,9},{9,8},{10,11... | collective-permute-start | bytes 3145736 | tf_op jit(solution)/shard_map/ppermute | solution.py:582
  204.0 8.5 %collective-permute-start.27 = (bf16[4,4,8,256]{3,2,1,0:T(8,128)(2,1)S(1)}, bf16[4,4,8,256]{3,2,1,0:T(8,128)(2,1)S(1)}, u32[]{:S(2)}, u32[]{:S(2)}) collective-permute-start(bf16[4,4,8,256]{3,2,1,0:T(8,128)(2,1)S(1)} %fusion.10), channel_id=1, source_target_pairs={{0,1},{1,0},{2,3},{3,2},{4,5},{5,4},{6,7},{7,6},{8,9},{9,8},{10,11... | collective-permute-start | bytes 196616 | tf_op jit(solution)/shard_map/ppermute | solution.py:582
  205.8 6.7 %copy-start.13 = (f32[2,4,4,8,256]{4,3,2,1,0:T(8,128)S(1)}, f32[2,4,4,8,256]{4,3,2,1,0:T(8,128)}, u32[]{:S(2)}) copy-start(f32[2,4,4,8,256]{4,3,2,1,0:T(8,128)} %get-tuple-element.200) | copy-start | bytes 786436
  205.8 6.7 %copy-start.5 = (bf16[4,4,64,512]{3,2,1,0:T(8,128)(2,1)S(1)}, bf16[4,4,64,512]{3,2,1,0:T(8,128)(2,1)}, u32[]{:S(2)}) copy-start(bf16[4,4,64,512]{3,2,1,0:T(8,128)(2,1)} %get-tuple-element.189) | copy-start | bytes 3145732
  205.9 11.1 %collective-permute-start.33 = (bf16[192,512]{1,0:T(8,128)(2,1)S(1)}, bf16[192,512]{1,0:T(8,128)(2,1)S(1)}, u32[]{:S(2)}, u32[]{:S(2)}) collective-permute-start(bf16[192,512]{1,0:T(8,128)(2,1)S(1)} %get-tuple-element.239), channel_id=1, source_target_pairs={{0,24},{1,25},{2,26},{3,27},{4,28},{5,29},{6,30},{7,31},{8,16},{9,... | collective-permute-start | bytes 589832 | tf_op jit(solution)/shard_map/ppermute | solution.py:582
  208.4 19.0 %collective-permute-start.32 = (bf16[192,512]{1,0:T(8,128)(2,1)S(1)}, bf16[192,512]{1,0:T(8,128)(2,1)S(1)}, u32[]{:S(2)}, u32[]{:S(2)}) collective-permute-start(bf16[192,512]{1,0:T(8,128)(2,1)S(1)} %get-tuple-element.240), channel_id=1, source_target_pairs={{0,16},{1,17},{2,18},{3,19},{4,20},{5,21},{6,22},{7,23},{8,24},{9,... | collective-permute-start | bytes 589832 | tf_op jit(solution)/shard_map/ppermute | solution.py:582
  213.1 18.3 %collective-permute-start.30 = (bf16[4,72,512]{2,1,0:T(8,128)(2,1)S(1)}, bf16[4,72,512]{2,1,0:T(8,128)(2,1)S(1)}, u32[]{:S(2)}, u32[]{:S(2)}) collective-permute-start(bf16[4,72,512]{2,1,0:T(8,128)(2,1)S(1)} %get-tuple-element.233), channel_id=1, source_target_pairs={{0,6},{1,7},{2,4},{3,5},{4,2},{5,3},{6,0},{7,1},{8,14},{9,15},{10,... | collective-permute-start | bytes 884744 | tf_op jit(solution)/shard_map/ppermute | solution.py:582
  215.7 15.8 %collective-permute-start.29 = (bf16[4,72,512]{2,1,0:T(8,128)(2,1)S(1)}, bf16[4,72,512]{2,1,0:T(8,128)(2,1)S(1)}, u32[]{:S(2)}, u32[]{:S(2)}) collective-permute-start(bf16[4,72,512]{2,1,0:T(8,128)(2,1)S(1)} %get-tuple-element.234), channel_id=1, source_target_pairs={{0,4},{1,5},{2,6},{3,7},{4,0},{5,1},{6,2},{7,3},{8,12},{9,13},{10,... | collective-permute-start | bytes 884744 | tf_op jit(solution)/shard_map/ppermute | solution.py:582
  216.2 15.3 %collective-permute-start.28 = (bf16[4,72,512]{2,1,0:T(8,128)(2,1)S(1)}, bf16[4,72,512]{2,1,0:T(8,128)(2,1)S(1)}, u32[]{:S(2)}, u32[]{:S(2)}) collective-permute-start(bf16[4,72,512]{2,1,0:T(8,128)(2,1)S(1)} %get-tuple-element.235), channel_id=1, source_target_pairs={{0,2},{1,3},{2,0},{3,1},{4,6},{5,7},{6,4},{7,5},{8,10},{9,11},{10,... | collective-permute-start | bytes 884744 | tf_op jit(solution)/shard_map/ppermute | solution.py:582
  217.0 14.5 %collective-permute-start.31 = (bf16[192,512]{1,0:T(8,128)(2,1)S(1)}, bf16[192,512]{1,0:T(8,128)(2,1)S(1)}, u32[]{:S(2)}, u32[]{:S(2)}) collective-permute-start(bf16[192,512]{1,0:T(8,128)(2,1)S(1)} %get-tuple-element.241), channel_id=1, source_target_pairs={{0,8},{1,9},{2,10},{3,11},{4,12},{5,13},{6,14},{7,15},{8,0},{9,1},... | collective-permute-start | bytes 589832 | tf_op jit(solution)/shard_map/ppermute | solution.py:582
  231.7 6.3 %collective-permute-start.34 = (bf16[72,512]{1,0:T(8,128)(2,1)S(1)}, bf16[72,512]{1,0:T(8,128)(2,1)S(1)}, u32[]{:S(2)}, u32[]{:S(2)}) collective-permute-start(bf16[72,512]{1,0:T(8,128)(2,1)S(1)} %get-tuple-element.244), channel_id=1, source_target_pairs={{0,8},{1,9},{2,10},{3,11},{4,12},{5,13},{6,14},{7,15},{8,0},{9,1},... | collective-permute-start | bytes 221192 | tf_op jit(solution)/shard_map/ppermute | solution.py:582
  231.8 7.0 %collective-permute-start.36 = (bf16[72,512]{1,0:T(8,128)(2,1)S(1)}, bf16[72,512]{1,0:T(8,128)(2,1)S(1)}, u32[]{:S(2)}, u32[]{:S(2)}) collective-permute-start(bf16[72,512]{1,0:T(8,128)(2,1)S(1)} %get-tuple-element.245), channel_id=1, source_target_pairs={{0,24},{1,25},{2,26},{3,27},{4,28},{5,29},{6,30},{7,31},{8,16},{9,... | collective-permute-start | bytes 221192 | tf_op jit(solution)/shard_map/ppermute | solution.py:582
  234.2 7.8 %collective-permute-start.35 = (bf16[72,512]{1,0:T(8,128)(2,1)S(1)}, bf16[72,512]{1,0:T(8,128)(2,1)S(1)}, u32[]{:S(2)}, u32[]{:S(2)}) collective-permute-start(bf16[72,512]{1,0:T(8,128)(2,1)S(1)} %get-tuple-element.246), channel_id=1, source_target_pairs={{0,16},{1,17},{2,18},{3,19},{4,20},{5,21},{6,22},{7,23},{8,24},{9,... | collective-permute-start | bytes 221192 | tf_op jit(solution)/shard_map/ppermute | solution.py:582
  245.3 12.8 %all-to-all-start = ((f32[32,8,128]{2,1,0:T(8,128)}), f32[32,8,128]{2,1,0:T(8,128)S(1)}, u32[]{:S(2)}, u32[]{:S(2)}) async-start(f32[32,8,128]{2,1,0:T(8,128)} %broadcast_in_dim.3), calls=%async_computation | async-start | bytes 262144 | tf_op jit(solution)/shard_map/all_to_all | solution.py:770
  249.8 9.6 %copy-start.8 = (f32[64,512]{1,0:T(8,128)S(1)}, f32[64,512]{1,0:T(8,128)}, u32[]{:S(2)}) copy-start(f32[64,512]{1,0:T(8,128)} %param.24) | copy-start | bytes 393220
  249.9 9.6 %copy-start.16 = (f32[64,512]{1,0:T(8,128)S(1)}, f32[64,512]{1,0:T(8,128)}, u32[]{:S(2)}) copy-start(f32[64,512]{1,0:T(8,128)} %param.31) | copy-start | bytes 393220
  249.9 9.6 %copy-start.17 = (f32[64,512]{1,0:T(8,128)S(1)}, f32[64,512]{1,0:T(8,128)}, u32[]{:S(2)}) copy-start(f32[64,512]{1,0:T(8,128)} %param.30) | copy-start | bytes 393220
  249.9 10.4 %copy-start.18 = (f32[17,16]{0,1:T(8,128)S(1)}, f32[17,16]{0,1:T(8,128)}, u32[]{:S(2)}) copy-start(f32[17,16]{0,1:T(8,128)} %param.25) | copy-start | bytes 3268
  249.9 10.4 %copy-start.19 = (f32[17,16]{0,1:T(8,128)S(1)}, f32[17,16]{0,1:T(8,128)}, u32[]{:S(2)}) copy-start(f32[17,16]{0,1:T(8,128)} %param.33) | copy-start | bytes 3268
  249.9 10.4 %copy-start.20 = (f32[17,16]{0,1:T(8,128)S(1)}, f32[17,16]{0,1:T(8,128)}, u32[]{:S(2)}) copy-start(f32[17,16]{0,1:T(8,128)} %param.32) | copy-start | bytes 3268
  256.8 4.1 %copy-start.7 = (f32[16,2048]{1,0:T(8,128)S(1)}, f32[16,2048]{1,0:T(8,128)}, u32[]{:S(2)}) copy-start(f32[16,2048]{1,0:T(8,128)} %param.23) | copy-start | bytes 393220
  256.8 4.1 %copy-start.14 = (f32[16,2048]{1,0:T(8,128)S(1)}, f32[16,2048]{1,0:T(8,128)}, u32[]{:S(2)}) copy-start(f32[16,2048]{1,0:T(8,128)} %param.29) | copy-start | bytes 393220
  256.9 4.1 %copy-start.15 = (f32[16,2048]{1,0:T(8,128)S(1)}, f32[16,2048]{1,0:T(8,128)}, u32[]{:S(2)}) copy-start(f32[16,2048]{1,0:T(8,128)} %param.28) | copy-start | bytes 393220
  256.9 4.9 %copy-start.3 = (f32[8,16,512]{2,1,0:T(8,128)S(1)}, f32[8,16,512]{2,1,0:T(8,128)}, u32[]{:S(2)}) copy-start(f32[8,16,512]{2,1,0:T(8,128)} %param.22) | copy-start | bytes 786436
  256.9 4.9 %copy-start.10 = (f32[8,16,512]{2,1,0:T(8,128)S(1)}, f32[8,16,512]{2,1,0:T(8,128)}, u32[]{:S(2)}) copy-start(f32[8,16,512]{2,1,0:T(8,128)} %param.27) | copy-start | bytes 786436
  256.9 4.9 %copy-start.11 = (f32[8,16,512]{2,1,0:T(8,128)S(1)}, f32[8,16,512]{2,1,0:T(8,128)}, u32[]{:S(2)}) copy-start(f32[8,16,512]{2,1,0:T(8,128)} %param.26) | copy-start | bytes 786436

commit v4 on v3

--- a/solution.py
+++ b/solution.py
@@ -8,6 +8,10 @@
 from jax.sharding import PartitionSpec as P
 
 HEADS = 8
+TILE = 256
+FFN_AHEAD = 1
+LATE = 1
+AHEAD = 2
 HEAD_DIM = 64
 STEP = 5
 AXES = ("dp", "fsdp")
@@ -47,62 +51,127 @@
     return jnp.sum(values.astype(F32), 0, keepdims=True)
 
 
-def half_of(pair, odd):
-    lane = lax.broadcasted_iota(jnp.int32, pair.shape, 1)
-    keep = lane >= HEAD_DIM if odd else lane < HEAD_DIM
-    return jnp.where(keep, pair, jnp.zeros_like(pair))
-
-
-def self_bias(size, count):
+def own_half(shape, odd):
+    lane = lax.broadcasted_iota(jnp.int32, shape, 1)
+    return lane >= HEAD_DIM if odd else lane < HEAD_DIM
+
+
+def half_of(pair, odd, other=0.0):
+    return jnp.where(own_half(pair.shape, odd), pair, jnp.asarray(other, pair.dtype))
+
+
+def spare_column(keys, odd, index, values):
+    lane = lax.broadcasted_iota(jnp.int32, (keys, PAIR), 1)
+    return jnp.where(lane == index + (0 if odd else HEAD_DIM), values, 0.0)
+
+
+def key_bias(keys, count):
+    key = lax.broadcasted_iota(jnp.int32, (keys, PAIR), 0)
+    return jnp.where(key < count, 0.0, -1e30)
+
+
+def causal_bias(size):
     key = lax.broadcasted_iota(jnp.int32, (size, size), 0)
     query = lax.broadcasted_iota(jnp.int32, (size, size), 1)
-    return jnp.where((key <= query) & (key < count), 0.0, -1e30)
-
-
-def cross_bias(keys, queries, count):
-    key = lax.broadcasted_iota(jnp.int32, (keys, queries), 0)
-    return jnp.where(key < count, 0.0, -1e30)
-
-
-def attend(query, key, value, bias_ref, mixed_ref, lse_ref):
+    return jnp.where(key <= query, 0.0, -1e30)
+
+
+def three_parts(row):
+    high = row.astype(LOW).astype(F32)
+    mid = (row - high).astype(LOW).astype(F32)
+    index = lax.broadcasted_iota(jnp.int32, (16, row.shape[1]), 0)
+    block = jnp.where(index == 0, high, jnp.where(index == 1, mid, jnp.where(index == 2, row - high - mid, 0.0)))
+    return jnp.where(index == 3, 1.0, block).astype(LOW)
+
+
+def spare_rows(rows, odd, extra):
+    zeros = jnp.zeros((HEAD_DIM - 16, rows.shape[1]), rows.dtype)
+    return jnp.concatenate([extra, zeros, rows] if odd else [rows, extra, zeros], 0)
+
+
+def attend(query, key, value, count, causal_ref, mixed_ref, lse_ref):
     value_t = value.T
-    for pair in range(HEADS // 2):
+    keys = key.shape[0]
+    bias = key_bias(keys, count)
+    patterns = [spare_column(keys, odd, 3, bias).astype(LOW) for odd in range(2)]
+
+    def score(head):
+        pair, odd = head // 2, head % 2
         cols = slice(pair * PAIR, (pair + 1) * PAIR)
-        query_pair, key_pair = query[:, cols] * SCALE, key[:, cols]
-        for odd in range(2):
-            head = 2 * pair + odd
-            rows = slice(head * HEAD_DIM, (head + 1) * HEAD_DIM)
-            scores = dot_nt(half_of(key_pair, odd), query_pair) + bias_ref[...]
-            top = jnp.max(scores, 0, keepdims=True)
-            expo = jnp.exp(scores - top)
-            total = jnp.sum(expo, 0, keepdims=True)
-            probs = (expo * (1.0 / total)).astype(LOW)
-            mixed_ref[rows] = dot_nn(value_t[rows], probs)
-            lse_ref[0, head : head + 1] = top + jnp.log(total)
-
-
-def attend_back(query_ref, key_ref, value_ref, grad, bias_ref, lse_ref, gq_ref, gk_ref, gv_ref):
-    key_t = key_ref[0].T
-    for pair in range(HEADS // 2):
+        left = jnp.where(own_half((keys, PAIR), odd), key[:, cols], patterns[odd])
+        scores = dot_nt(left, half_of(query[:, cols] * SCALE, odd, 1.0))
+        return scores if causal_ref is None else scores + causal_ref[...]
+
+    def finish(rows, probs):
+        mixed_ref[rows] = dot_nn(value_t[rows], probs)
+
+    ahead, late = [score(head) for head in range(AHEAD)], []
+    for head in range(HEADS):
+        scores = ahead.pop(0)
+        if head + AHEAD < HEADS:
+            ahead.append(score(head + AHEAD))
+        rows = slice(head * HEAD_DIM, (head + 1) * HEAD_DIM)
+        top = jnp.max(scores, 0, keepdims=True)
+        expo = jnp.exp(scores - top)
+        total = jnp.sum(expo, 0, keepdims=True)
+        lse_ref[0, head : head + 1] = top + jnp.log(total)
+        late.append((rows, (expo * (1.0 / total)).astype(LOW)))
+        if len(late) > LATE:
+            finish(*late.pop(0))
+    for item in late:
+        finish(*item)
+
+
+def attend_back(query_ref, key_ref, value_ref, mixed_ref, grad, count, causal_ref, lse_ref, gq_ref, gk_ref, gv_ref):
+    key_t, query_t, grad_t = key_ref[0].T, (query_ref[0] * SCALE).T, grad.T
+    keys = key_ref.shape[1]
+    bias = key_bias(keys, count)
+    lane = lax.broadcasted_iota(jnp.int32, (keys, PAIR), 1)
+    patterns = []
+    for odd in range(2):
+        start = 0 if odd else HEAD_DIM
+        ones = jnp.where((lane >= start) & (lane < start + 3), 1.0, 0.0)
+        patterns.append((ones + spare_column(keys, odd, 3, bias)).astype(LOW))
+
+    def begin(head):
+        pair, odd = head // 2, head % 2
         cols = slice(pair * PAIR, (pair + 1) * PAIR)
-        query_pair = query_ref[0, :, cols] * SCALE
-        key_pair, value_pair, grad_pair = key_ref[0, :, cols], value_ref[0, :, cols], grad[:, cols]
-        grad_key = grad_value = None
-        for odd in range(2):
-            head = 2 * pair + odd
-            rows = slice(head * HEAD_DIM, (head + 1) * HEAD_DIM)
-            scores = dot_nt(half_of(key_pair, odd), query_pair) + bias_ref[...]
-            probs = jnp.exp(scores - lse_ref[0, head : head + 1])
-            grad_probs = dot_nt(half_of(value_pair, odd), grad_pair)
-            inner = jnp.sum(probs * grad_probs, 0, keepdims=True)
-            grad_scores = (probs * (grad_probs - inner)).astype(LOW)
-            to_value = dot_nn(probs.astype(LOW), half_of(grad_pair, odd))
-            to_key = dot_nn(grad_scores, half_of(query_pair, odd))
-            grad_value = to_value if grad_value is None else grad_value + to_value
-            grad_key = to_key if grad_key is None else grad_key + to_key
-            gq_ref[rows] = dot_nn(key_t[rows], grad_scores)
-        gk_ref[0, :, cols] = grad_key.astype(LOW)
-        gv_ref[0, :, cols] = grad_value.astype(LOW)
+        rows = slice(head * HEAD_DIM, (head + 1) * HEAD_DIM)
+        scores = dot_nn(
+            jnp.where(own_half((keys, PAIR), odd), key_ref[0, :, cols], patterns[odd]),
+            spare_rows(query_t[rows], odd, three_parts(-lse_ref[0, head : head + 1])),
+        )
+        slopes = dot_nn(half_of(value_ref[0, :, cols], odd), grad_t[cols])
+        return scores if causal_ref is None else scores + causal_ref[...], slopes
+
+    sums = []
+
+    def finish(head, probs, grad_scores):
+        pair, odd = head // 2, head % 2
+        cols = slice(pair * PAIR, (pair + 1) * PAIR)
+        rows = slice(head * HEAD_DIM, (head + 1) * HEAD_DIM)
+        sums.append(
+            (dot_nn(probs, half_of(grad[:, cols], odd)),
+             dot_nn(grad_scores, half_of(query_ref[0, :, cols] * SCALE, odd)))
+        )
+        gq_ref[rows] = dot_nn(key_t[rows], grad_scores)
+        if odd:
+            gv_ref[0, :, cols] = (sums[-2][0] + sums[-1][0]).astype(LOW)
+            gk_ref[0, :, cols] = (sums[-2][1] + sums[-1][1]).astype(LOW)
+
+    ahead, late = [begin(head) for head in range(AHEAD)], []
+    for head in range(HEADS):
+        scores, slopes = ahead.pop(0)
+        if head + AHEAD < HEADS:
+            ahead.append(begin(head + AHEAD))
+        probs = jnp.exp(scores)
+        inner = jnp.sum(probs * slopes, 0, keepdims=True)
+        grad_scores = (probs * (slopes - inner)).astype(LOW)
+        late.append((head, probs.astype(LOW), grad_scores))
+        if len(late) > LATE:
+            finish(*late.pop(0))
+    for item in late:
+        finish(*item)
 
 
 def place_weights(place_ref, mine_ref, other_ref, blocks, outs, turned=None, table_ref=None):
@@ -148,7 +217,8 @@
     else:
         w_ref, table_ref = refs[:2]
         bias, mixed_t = refs[9:]
-    bias[...] = self_bias(bias.shape[0], count_ref[pl.program_id(0)])
+    count = count_ref[pl.program_id(0)]
+    bias[...] = causal_bias(bias.shape[0])
     x = x_ref[0].astype(F32)
     hat, _ = normalize(x)
     act = (hat * (1.0 + table_ref[0:1]) + table_ref[1:2]).astype(LOW)
@@ -157,7 +227,7 @@
     key = dot_nn(act, w_ref[1]).astype(LOW)
     value = (dot_nn(act, w_ref[2]) + table_ref[7:8]).astype(LOW)
     query_ref[0], key_ref[0], value_ref[0] = query, key, value
-    attend(query, key, value, bias, mixed_t, lse_ref)
+    attend(query, key, value, count, bias, mixed_t, lse_ref)
     mixed = mixed_t[...].T.astype(LOW)
     mixed_ref[0] = mixed
     out_ref[0] = x + dot_nn(mixed, w_ref[3]) + table_ref[8:9]
@@ -167,15 +237,15 @@
     start = 2 if own else 1
     act_ref, query_ref, key_ref, value_ref, mixed_ref, lse_ref, out_ref = refs[start : start + 7]
     if own:
-        w_ref, bias, mixed_t = refs[9:]
+        w_ref, mixed_t = refs[9:]
 
         @pl.when(pl.program_id(0) == 0)
         def _():
             place_weights(place_ref, refs[0], refs[1], attn_blocks(own), (w_ref,))
     else:
         w_ref = refs[0]
-        bias, mixed_t = refs[8:]
-    bias[...] = cross_bias(*bias.shape, count_ref[pl.program_id(0)])
+        (mixed_t,) = refs[8:]
+    count = count_ref[pl.program_id(0)]
     x = x_ref[0]
     hat, _ = normalize(x)
     act = (hat * (1.0 + table_ref[2:3]) + table_ref[3:4]).astype(LOW)
@@ -184,7 +254,7 @@
     key = dot_nn(mem_ref[0], w_ref[1]).astype(LOW)
     value = (dot_nn(mem_ref[0], w_ref[2]) + table_ref[10:11]).astype(LOW)
     query_ref[0], key_ref[0], value_ref[0] = query, key, value
-    attend(query, key, value, bias, mixed_t, lse_ref)
+    attend(query, key, value, count, None, mixed_t, lse_ref)
     mixed = mixed_t[...].T.astype(LOW)
     mixed_ref[0] = mixed
     out_ref[0] = x + dot_nn(mixed, w_ref[3]) + table_ref[11:12]
@@ -203,28 +273,32 @@
 def ffn_kernel(own, count_ref, place_ref, x_ref, cot_ref, table_ref, bias_ref, *refs):
     step = pl.program_id(0)
     seqs, length, width = x_ref.shape
-    out_ref, grad_ref, first_ref, second_ref, small_ref = refs[2:7]
-    act, gf, hidden, gpre, back = refs[7:12]
+    skip = 4 if own else 2
+    out_hbm, grad_hbm, small_ref = refs[skip : skip + 3]
+    grad_refs = refs[skip + 3 : 2 * skip + 3]
+    act, gf, hidden, gpre, back, out, sems = refs[2 * skip + 3 : 2 * skip + 10]
     chunk = hidden.shape[2]
-    if own:
-        rows, whole_in, whole_out = refs[12:]
-        count = first_ref.shape[2]
-        w_in_ref = whole_in.at[step]
-        w_out_ref = whole_out.at[pl.ds(pl.multiple_of(step * chunk, chunk), chunk)]
-    else:
-        w_in_ref, w_out_ref = refs[:2]
 
     def valid(seq):
         row = lax.broadcasted_iota(jnp.int32, (length, 1), 0)
         return (row < count_ref[seq]).astype(F32)
 
+    if own:
+        w_in_ref, w_out_ref, rows_in, rows_out = refs[2 * skip + 10 :]
+        in_mine, in_other, out_mine, out_other = refs[:4]
+        out_rows = out_mine.shape[2]
+        planes = out_mine.shape[0]
+        place_weights(place_ref, in_mine, in_other, [(0, 0, own, slice(None))], (w_in_ref,))
+        for plane in range(planes):
+            base = (plane ^ place_ref[1]) * 2
+            for ref, core in ((out_mine, place_ref[2]), (out_other, 1 - place_ref[2])):
+                first = pl.multiple_of((base + core) * out_rows, out_rows)
+                w_out_ref[pl.ds(first, out_rows)] = ref[plane, 0]
+    else:
+        w_in_ref, w_out_ref = refs[:2]
+
     @pl.when(step == 0)
     def _():
-        if own:
-            out_rows = count // 2
-            spots = [(1, 0, out_rows, slice(None))]
-            spots += [(0, out_rows + i * own, own, i) for i in range(whole_in.shape[0])]
-            place_weights(place_ref, refs[0], refs[1], spots, (whole_in, whole_out))
         small_ref[...] = jnp.zeros_like(small_ref)
         for seq in range(seqs):
             x = x_ref[seq]
@@ -233,55 +307,77 @@
             grad = (cot_ref[seq].astype(F32) * valid(seq)).astype(LOW)
             gf[seq] = grad
             small_ref[2:3] += column_sum(grad)
-            out_ref[seq] = x + table_ref[12:13]
+            out[seq] = x + table_ref[12:13]
             back[seq] = jnp.zeros_like(back[seq])
 
+    tiles = [(seq, first) for seq in range(seqs) for first in range(0, length, TILE)]
+
+    def begin(tile):
+        seq, first = tile
+        rows = slice(first, first + TILE)
+        pre = dot_nn(act[seq, rows], w_in_ref[...]) + bias_ref[...]
+        return tile, pre, dot_nt(gf[seq, rows], w_out_ref[...])
+
+    def finish(tile, unit, grad_pre):
+        seq, first = tile
+        rows = slice(first, first + TILE)
+        out[seq, rows] += dot_nn(unit, w_out_ref[...])
+        back[seq, rows] += dot_nt(grad_pre, w_in_ref[...])
+
+    ahead, late = [begin(tile) for tile in tiles[:FFN_AHEAD]], []
     sums = jnp.zeros((1, chunk), F32)
-    for seq in range(seqs):
-        pre = dot_nn(act[seq], w_in_ref[...]) + bias_ref[...]
+    for index in range(len(tiles)):
+        (seq, first), pre, grad_unit = ahead.pop(0)
+        if index + FFN_AHEAD < len(tiles):
+            ahead.append(begin(tiles[index + FFN_AHEAD]))
         cdf = 0.5 + 0.5 * lax.erf(pre * 0.5**0.5)
         slope = cdf + pre * (jnp.exp(pre * pre * -0.5) * 0.3989422804014327)
         unit = (pre * cdf).astype(LOW)
-        hidden[seq] = unit
-        grad_pre = (dot_nt(gf[seq], w_out_ref[...]) * slope).astype(LOW)
-        gpre[seq] = grad_pre
+        grad_pre = (grad_unit * slope).astype(LOW)
+        hidden[seq, first : first + TILE] = unit
+        gpre[seq, first : first + TILE] = grad_pre
         sums += column_sum(grad_pre)
-        out_ref[seq] += dot_nn(unit, w_out_ref[...])
-        back[seq] += dot_nt(grad_pre, w_in_ref[...])
+        late.append(((seq, first), unit, grad_pre))
+        if len(late) > LATE:
+            finish(*late.pop(0))
+    for item in late:
+        finish(*item)
     small_ref[pl.ds(8 + step, 1)] = sums
     tokens = seqs * length
     hidden_all, gf_all = hidden[...].reshape(tokens, -1), gf[...].reshape(tokens, -1)
     act_all, gpre_all = act[...].reshape(tokens, -1), gpre[...].reshape(tokens, -1)
     if own:
-        planes = first_ref.shape[0]
-        rows[...] = dot_tn(act_all, gpre_all)
-        for spot in range(4):
-
-            @pl.when(step == spot)
-            def _():
-                emit(place_ref, rows, first_ref, second_ref, count // 2 + spot * own, own)
-
-        rows[...] = dot_tn(hidden_all, gf_all)
-        depth = step ^ place_ref[0]
+        in_keep, in_send, out_keep, out_send = grad_refs
+        rows_in[...] = dot_tn(act_all, gpre_all)
+        rows_out[...] = dot_tn(hidden_all, gf_all)
+        emit(place_ref, rows_in, in_keep, in_send, 0, own)
         for plane in range(planes):
             base = (plane ^ place_ref[1]) * 2
-            for ref, core in ((first_ref, place_ref[2]), (second_ref, 1 - place_ref[2])):
-                begin = pl.multiple_of((base + core) * (count // 2), count // 2)
-                ref[plane, depth, : count // 2] = rows[pl.ds(begin, count // 2)].astype(ref.dtype)
-    else:
-        first_ref[...] = dot_tn(act_all, gpre_all)
-        second_ref[...] = dot_tn(hidden_all, gf_all)
+            for ref, core in ((out_keep, place_ref[2]), (out_send, 1 - place_ref[2])):
+                first = pl.multiple_of((base + core) * out_rows, out_rows)
+                ref[plane, 0] = rows_out[pl.ds(first, out_rows)].astype(ref.dtype)
+    else:
+        grad_refs[0][...] = dot_tn(act_all, gpre_all)
+        grad_refs[1][...] = dot_tn(hidden_all, gf_all)
 
     @pl.when(step == pl.num_programs(0) - 1)
     def _():
+        copies = []
+        for seq in range(seqs):
+            copies.append(pltpu.make_async_copy(out.at[seq], out_hbm.at[seq], sems.at[0, seq]))
+            copies[-1].start()
         for seq in range(seqs):
             hat, inverse = normalize(x_ref[seq])
             grad = back[seq]
             small_ref[0:1] += column_sum(grad * hat)
             small_ref[1:2] += column_sum(grad)
-            grad_ref[seq] = cot_ref[seq].astype(F32) * valid(seq) + normalize_back(
+            back[seq] = cot_ref[seq].astype(F32) * valid(seq) + normalize_back(
                 grad, hat, inverse, table_ref[4:5]
             )
+            copies.append(pltpu.make_async_copy(back.at[seq], grad_hbm.at[seq], sems.at[1, seq]))
+            copies[-1].start()
+        for copy in copies:
+            copy.wait()
 
 
 def begin_sums(*refs):
@@ -304,17 +400,17 @@
 ):
     out_ref, gk_ref, gv_ref, small_ref = refs[:4]
     if own:
-        keep_ref, send_ref, bias, gq_t, gw = refs[4:]
-    else:
-        gw, bias, gq_t = refs[4:]
+        keep_ref, send_ref, gq_t, gw = refs[4:]
+    else:
+        gw, gq_t = refs[4:]
     begin_sums(gw, small_ref)
-    bias[...] = cross_bias(*bias.shape, count_ref[pl.program_id(0)])
+    count = count_ref[pl.program_id(0)]
     grad = grad_ref[0]
     low = grad.astype(LOW)
     gw[3] += dot_tn(mixed_ref[0], low)
     small_ref[4:5] += column_sum(low)
     grad_mixed = dot_nt(low, w_ref[3]).astype(LOW)
-    attend_back(query_ref, key_ref, value_ref, grad_mixed, bias, lse_ref, gq_t, gk_ref, gv_ref)
+    attend_back(query_ref, key_ref, value_ref, mixed_ref, grad_mixed, count, None, lse_ref, gq_t, gk_ref, gv_ref)
     gq = (gq_t[...] * SCALE).T.astype(LOW)
     small_ref[2:3] += column_sum(gq)
     small_ref[3:4] += column_sum(gv_ref[0])
@@ -340,12 +436,13 @@
     else:
         gw, bias, gq_t = refs[4:]
     begin_sums(gw, small_ref)
-    bias[...] = self_bias(bias.shape[0], count_ref[pl.program_id(0)])
+    count = count_ref[pl.program_id(0)]
+    bias[...] = causal_bias(bias.shape[0])
     low = grad_ref[0].astype(LOW)
     gw[3] += dot_tn(mixed_ref[0], low)
     small_ref[4:5] += column_sum(low)
     grad_mixed = dot_nt(low, w_ref[3]).astype(LOW)
-    attend_back(query_ref, key_ref, value_ref, grad_mixed, bias, lse_ref, gq_t, gk_ref, gv_ref)
+    attend_back(query_ref, key_ref, value_ref, mixed_ref, grad_mixed, count, bias, lse_ref, gq_t, gk_ref, gv_ref)
     gq = (gq_t[...] * SCALE).T.astype(LOW)
     gq_ref[0] = gq
     small_ref[2:3] += column_sum(gq)
@@ -406,6 +503,9 @@
     return jax.ShapeDtypeStruct(shape, dtype)
 
 
+LIMITS = {'self_forward': 20, 'cross_forward': 20, 'ffn': 28, 'cross_back': 26, 'self_back': 20, 'input_grad': 16, 'memory_grad': 16}
+
+
 def call(kernel, name, work, grid, scalars, args, in_specs, outs, out_specs, scratch):
     return pl.pallas_call(
         kernel,
@@ -417,7 +517,7 @@
             out_specs=out_specs,
             scratch_shapes=scratch,
         ),
-        compiler_params=pltpu.CompilerParams(vmem_limit_bytes=LIMIT),
+        compiler_params=pltpu.CompilerParams(vmem_limit_bytes=LIMITS[name] << 20),
         cost_estimate=pl.CostEstimate(flops=int(work * 1.1e9), bytes_accessed=1 << 20, transcendentals=0),
         name=name,
     )(*scalars, *args)
@@ -456,7 +556,7 @@
         partial(cross_forward_kernel, grid.own), "cross_forward", 24, (seqs,), (mem_lengths, grid.spot),
         (x, memory, table, *weights),
         [block, mem_block, fixed(*table.shape)] + [fixed(*part.shape) for part in weights], outs, out_specs,
-        [pltpu.VMEM((mem_len, length), F32), pltpu.VMEM((width, length), F32)],
+        [pltpu.VMEM((width, length), F32)],
     )
     return results if grid.own else (*results, *weights)
 
@@ -468,14 +568,25 @@
     bias = table[13:17].reshape(1, grid.hidden)
     act = pltpu.VMEM((seqs, length, width), LOW)
     wide = pltpu.VMEM((seqs, length, chunk), LOW)
+    total = pltpu.VMEM((seqs, length, width), F32)
     flat = pl.BlockSpec((1, chunk), lambda i, *_: (0, i))
-    scratch = [act, act, wide, wide, pltpu.VMEM((seqs, length, width), F32)]
+    anywhere = pl.BlockSpec(memory_space=pl.ANY)
+    scratch = [act, act, wide, wide, total, total, pltpu.SemaphoreType.DMA((2, seqs))]
     if grid.own:
-        parts = grid.sizes[1::-1] + (8 * grid.own, width)
-        grads, grad_specs = [(parts, LOW), (parts, LOW)], [fixed(*parts), fixed(*parts)]
-        specs = [fixed(*part.shape) for part in weights]
-        scratch += [pltpu.VMEM((width, chunk), F32), pltpu.VMEM((blocks, width, chunk), LOW)]
-        scratch += [pltpu.VMEM((grid.hidden, width), LOW)]
+        depths, planes = grid.sizes[:2]
+        own, out_rows = grid.own, grid.hidden // grid.devices
+        in_parts, out_parts = (planes, depths, blocks * own, width), (planes, depths, out_rows, width)
+
+        def rows_spec(first):
+            return pl.BlockSpec((planes, depths, own, width), lambda i, *_: (0, 0, first + i, 0))
+
+        depth_spec = pl.BlockSpec((planes, 1, out_rows, width), lambda i, counts, place: (0, i ^ place[0], 0, 0))
+        specs = [rows_spec(out_rows // own)] * 2 + [depth_spec] * 2
+        weights = (*weights, *weights)
+        grads = [(in_parts, LOW)] * 2 + [(out_parts, LOW)] * 2
+        grad_specs = [rows_spec(0)] * 2 + [depth_spec] * 2
+        scratch += [pltpu.VMEM((width, chunk), LOW), pltpu.VMEM((chunk, width), LOW)]
+        scratch += [pltpu.VMEM((width, chunk), F32), pltpu.VMEM((chunk, width), F32)]
     else:
         cols = pl.BlockSpec((width, chunk), lambda i, *_: (0, i))
         rows = pl.BlockSpec((chunk, width), lambda i, *_: (i, 0))
@@ -485,8 +596,8 @@
         partial(ffn_kernel, grid.own), "ffn", 24, (blocks,), (lengths, grid.spot),
         (x, cotangent, table, bias, *weights),
         [fixed(*x.shape), fixed(*x.shape), fixed(*table.shape), flat] + specs,
-        [(x.shape, F32), (x.shape, F32)] + grads + [((16, width), F32)],
-        [fixed(*x.shape), fixed(*x.shape)] + grad_specs + [fixed(16, width)],
+        [(x.shape, F32), (x.shape, F32), ((16, width), F32)] + grads,
+        [anywhere, anywhere, fixed(16, width)] + grad_specs,
         scratch,
     )
 
@@ -517,7 +628,7 @@
          fixed(4, width, width), fixed(*table.shape)],
         [(x.shape, F32), (key.shape, LOW), (key.shape, LOW)],
         [block, mem_block, mem_block],
-        [pltpu.VMEM((mem_len, length), F32), pltpu.VMEM((width, length), F32)],
+        [pltpu.VMEM((width, length), F32)],
     )
 
 
@@ -695,15 +806,13 @@
     second, ffn_parts = lax.optimization_barrier((second, ffn_parts))
     act_two, query_two, key_two, value_two, mixed_two, lse_two, resid_two, w_cross = second
     ffn_plane = jnp.stack(ffn_parts)
-    output, grad_two, ffn_keep, ffn_send, small_three = ffn(
+    output, grad_two, small_three, *ffn_grads = ffn(
         lengths, grid, resid_two, cotangent, table, ffn_whole(ffn_plane, grid.swap(ffn_plane, 2, 1))
     )
     if not grid.own:
-        parts = jnp.swapaxes(ffn_keep.reshape(grid.devices, own, blocks, width), 1, 2)
-        parts = jnp.concatenate(
-            [ffn_send.reshape(grid.devices, out_rows, width), parts.reshape(grid.devices, blocks * own, width)], 1
-        )
-        ffn_keep, ffn_send = grid.relative(parts)
+        parts = jnp.swapaxes(ffn_grads[0].reshape(grid.devices, own, blocks, width), 1, 2)
+        in_parts = grid.relative(parts.reshape(grid.devices, blocks * own, width))
+        ffn_grads = (*in_parts, *grid.relative(ffn_grads[1].reshape(grid.devices, out_rows, width)))
 
     def attn_parts(grads):
         if grid.own:
@@ -714,7 +823,7 @@
     def meet(keep, send):
         return keep.astype(F32) + grid.swap(send, 2, 1).astype(F32)
 
-    ffn_sum = meet(ffn_keep, ffn_send)
+    ffn_sum = jnp.concatenate([meet(*ffn_grads[2:]), meet(*ffn_grads[:2])], 2)
     grad_two, ffn_sum = lax.optimization_barrier((grad_two, ffn_sum))
     ffn_got = grid.fetch(ffn_sum, 1)
     cross = cross_back(

time: 265 us -> 218 us (0.82)
  Pallas kernels: 136 us -> 82.1 us
  waiting for transfers between devices: 37.2 us -> 51.8 us
  other arithmetic: 19.4 us -> 15.3 us
  local copies, waits for them, and re-layouts: 10.5 us -> 7.52 us
    pallas_call x7, Pallas kernels: 136 us -> 82.1 us  [call(): pl.pallas_call(kernel, out_shape=[shape_of(*out) for out in outs], grid_s...]
    ppermute x37 -> x38, waiting for transfers between devices: 36 us -> 51 us  [swap(): return lax.ppermute(values, AXES, pairs)]
    unnamed x48 -> x74, local copies, waits for them, and re-layouts: 6.19 us -> 5.31 us
    ppermute x37 -> x38, starting transfers between devices: 50 us -> 50.6 us  [swap(): return lax.ppermute(values, AXES, pairs)]
  transfers between devices with their start and end apart: 38 -> 39, of which waited for: 12 -> 17; matrix products, arithmetic and copies ran while one was open for 4% -> 3% of each run, Pallas kernels for 41% -> 28%
where the time goes in v4:
time: 218 us; the launch traced here: 217 us
  Pallas kernels  82.1 us (38%)
  starting transfers between devices  54.4 us (25%)
  waiting for transfers between devices  51.8 us (24%)
  other arithmetic  15.3 us (7%)
  local copies, waits for them, and re-layouts  7.52 us (3%)
  between operations  5.9 us (3%)
    pallas_call x7, Pallas kernels, call(): pl.pallas_call(kernel, out_shape=[shape_of(*out) for out in outs], grid_s...  82.1 us
    ppermute x38, waiting for transfers between devices, swap(): return lax.ppermute(values, AXES, pairs)  51 us
    ppermute x38, starting transfers between devices, swap(): return lax.ppermute(values, AXES, pairs)  50.6 us
    unnamed x74, local copies, waits for them, and re-layouts  5.31 us
  transfers between devices with their start and end apart: 39, of which 17 were waited for; matrix products, arithmetic and copies ran while one was open for 3% of the time, Pallas kernels for 28%

profile of v4, /device:TPU:0, one launch (start us, length us, event | category | flops | bytes accessed | tf_op | source)
XLA Modules:
  0.0 217.1 jit_solution(13846209413462460231)
XLA Ops:
  0.6 0.7 convert_bitcast_fusion
  1.4 1.0 convert.32
  2.4 4.1 %collective-permute-start.1 = (bf16[72,512]{1,0:T(8,128)(2,1)S(1)}, bf16[72,512]{1,0:T(8,128)(2,1)S(1)}, u32[]{:S(2)}, u32[]{:S(2)}) collective-permute-start(bf16[72,512]{1,0:T(8,128)(2,1)S(1)} %get-tuple-element.258), channel_id=1, source_target_pairs={{0,16},{1,17},{2,18},{3,19},{4,20},{5,21},{6,22},{7,23},{8,24},{9,... | collective-permute-start | bytes 221192 | tf_op jit(solution)/shard_map/ppermute | solution.py:693
  6.5 1.6 collective-permute-start
  8.1 0.9 convert_element_type.155
  9.0 0.9 convert_element_type.154
  9.9 0.9 collective-permute-done
  10.8 3.4 %collective-permute-done.2 = bf16[72,512]{1,0:T(8,128)(2,1)S(1)} collective-permute-done((bf16[72,512]{1,0:T(8,128)(2,1)S(1)}, bf16[72,512]{1,0:T(8,128)(2,1)S(1)}, u32[]{:S(2)}, u32[]{:S(2)}) %collective-permute-start.2) | collective-permute-done | bytes 73760 | tf_op jit(solution)/shard_map/ppermute | solution.py:693
  14.3 1.7 collective-permute-start.8
  16.3 2.4 %collective-permute-start.6 = (bf16[192,512]{1,0:T(8,128)(2,1)S(1)}, bf16[192,512]{1,0:T(8,128)(2,1)S(1)}, u32[]{:S(2)}, u32[]{:S(2)}) collective-permute-start(bf16[192,512]{1,0:T(8,128)(2,1)S(1)} %pad_maximum_fusion.7), channel_id=1, source_target_pairs={{0,8},{1,9},{2,10},{3,11},{4,12},{5,13},{6,14},{7,15},{8,0},{9,1},... | collective-permute-start | bytes 589832 | tf_op jit(solution)/shard_map/ppermute | solution.py:693
  18.7 2.4 %collective-permute-start.5 = (bf16[4,72,512]{2,1,0:T(8,128)(2,1)S(1)}, bf16[4,72,512]{2,1,0:T(8,128)(2,1)S(1)}, u32[]{:S(2)}, u32[]{:S(2)}) collective-permute-start(bf16[4,72,512]{2,1,0:T(8,128)(2,1)S(1)} %get-tuple-element.252), channel_id=1, source_target_pairs={{0,6},{1,7},{2,4},{3,5},{4,2},{5,3},{6,0},{7,1},{8,14},{9,15},{10,... | collective-permute-start | bytes 884744 | tf_op jit(solution)/shard_map/ppermute | solution.py:693
  21.7 2.2 collective-permute-done.8
  23.8 1.5 collective-permute-start.3
  25.3 8.4 %collective-permute-done.7 = bf16[192,512]{1,0:T(8,128)(2,1)S(1)} collective-permute-done((bf16[192,512]{1,0:T(8,128)(2,1)S(1)}, bf16[192,512]{1,0:T(8,128)(2,1)S(1)}, u32[]{:S(2)}, u32[]{:S(2)}) %collective-permute-start.7) | collective-permute-done | bytes 196640 | tf_op jit(solution)/shard_map/ppermute | solution.py:693
  33.7 1.0 pad_maximum_fusion.5
  35.0 1.0 slice.135
  36.0 2.5 %collective-permute-start.12 = (bf16[4,64,512]{2,1,0:T(8,128)(2,1)S(1)}, bf16[4,64,512]{2,1,0:T(8,128)(2,1)S(1)}, u32[]{:S(2)}, u32[]{:S(2)}) collective-permute-start(bf16[4,64,512]{2,1,0:T(8,128)(2,1)S(1)} %slice.135), channel_id=1, source_target_pairs={{0,6},{1,7},{2,4},{3,5},{4,2},{5,3},{6,0},{7,1},{8,14},{9,15},{10,... | collective-permute-start | bytes 786440 | tf_op jit(solution)/shard_map/ppermute | solution.py:693
  39.6 9.1 %self_forward.1 = (bf16[4,256,512]{2,1,0:T(8,128)(2,1)S(1)}, bf16[4,256,512]{2,1,0:T(8,128)(2,1)S(1)}, bf16[4,256,512]{2,1,0:T(8,128)(2,1)S(1)}, bf16[4,256,512]...) custom-call(s32[4]{0:T(128)S(1)} %copy-done.4, ...), custom_call_target="tpu_custom_call" | custom-call | flops 19800000512 | bytes 1048576 | tf_op jit(solution)/shard_map/self_forward/pallas_call | solution.py:510
  48.7 1.0 copy-done.9
  49.7 1.0 copy-done.11
  50.6 0.6 collective-permute-done.11
  51.7 1.8 collective-permute-start.16
  53.5 1.2 collective-permute-start.15
  55.2 12.2 %cross_forward.1 = (bf16[4,256,512]{2,1,0:T(8,128)(2,1)S(1)}, bf16[4,256,512]{2,1,0:T(8,128)(2,1)S(1)}, bf16[4,512,512]{2,1,0:T(8,128)(2,1)S(1)}, bf16[4,512,512...) custom-call(s32[4]{0:T(128)S(1)} %copy-done.3, ...), custom_call_target="tpu_custom_call" | custom-call | flops 26400000000 | bytes 1048576 | tf_op jit(solution)/shard_map/cross_forward/pallas_call | solution.py:510
  67.5 10.6 %collective-permute-done.15 = bf16[4,128,512]{2,1,0:T(8,128)(2,1)S(1)} collective-permute-done((bf16[4,128,512]{2,1,0:T(8,128)(2,1)S(1)}, bf16[4,128,512]{2,1,0:T(8,128)(2,1)S(1)}, u32[]{:S(2)}, u32[]{:S(2)}) %collective-permute-start.15) | collective-permute-done | bytes 524320 | tf_op jit(solution)/shard_map/ppermute | solution.py:693
  78.6 4.1 %collective-permute-done.17.refs_1_.refs_3_ = bf16[4,4,128,512]{3,2,1,0:T(8,128)(2,1)S(1)} collective-permute-done((bf16[4,4,128,512]{3,2,1,0:T(8,128)(2,1)S(1)}, bf16[4,4,128,512]{3,2,1,0:T(8,128)(2,1)S(1)}, u32[]{:S(2)}, u32[]{:S(2)}) %collective-permute-start.17) | collective-permute-done | bytes 2097184 | tf_op jit(solution)/shard_map/ppermute | solution.py:693
  82.7 21.2 %ffn.1 = (f32[4,256,512]{2,1,0:T(8,128)}, f32[4,256,512]{2,1,0:T(8,128)S(1)}, f32[16,512]{1,0:T(8,128)S(1)}, bf16[4,4,64,512]{3,2,1,0:T(8,128)(2,1)S(1)}, bf16[4...) custom-call(s32[4]{0:T(128)S(1)} %copy-done.4, ...), custom_call_target="tpu_custom_call" | custom-call | flops 26400000000 | bytes 1048576 | tf_op jit(solution)/shard_map/ffn/pallas_call | solution.py:510
  104.5 2.1 collective-permute-done.18
  107.0 1.2 collective-permute-done.19
  109.6 1.8 collective-permute-start.22
  111.3 1.2 collective-permute-start.21
  113.1 19.2 %cross_back.1 = (f32[4,256,512]{2,1,0:T(8,128)S(1)}, bf16[4,512,512]{2,1,0:T(8,128)(2,1)S(1)}, bf16[4,512,512]{2,1,0:T(8,128)(2,1)S(1)}, f32[8,512]{1,0:T(8,128)...) custom-call(s32[4]{0:T(128)S(1)} %copy-done.3, s32[3]{0:T(128)S(1)} %pad_add_fusion.place_ref, ...), custom_call_target="tpu_custom_call" | custom-call | flops 32999999488 | bytes 1048576 | tf_op jit(solution)/shard_map/cross_back/pallas_call | solution.py:510
  132.5 3.3 %collective-permute-done.21 = bf16[4,128,512]{2,1,0:T(8,128)(2,1)S(1)} collective-permute-done((bf16[4,128,512]{2,1,0:T(8,128)(2,1)S(1)}, bf16[4,128,512]{2,1,0:T(8,128)(2,1)S(1)}, u32[]{:S(2)}, u32[]{:S(2)}) %collective-permute-start.21) | collective-permute-done | bytes 524320 | tf_op jit(solution)/shard_map/ppermute | solution.py:693
  136.1 2.3 %collective-permute-done.23 = bf16[4,4,64,512]{3,2,1,0:T(8,128)(2,1)S(1)} collective-permute-done((bf16[4,4,64,512]{3,2,1,0:T(8,128)(2,1)S(1)}, bf16[4,4,64,512]{3,2,1,0:T(8,128)(2,1)S(1)}, u32[]{:S(2)}, u32[]{:S(2)}) %collective-permute-start.23) | collective-permute-done | bytes 1048608 | tf_op jit(solution)/shard_map/ppermute | solution.py:693
  139.0 1.8 collective-permute-start.26
  140.7 1.2 collective-permute-start.25
  142.5 11.5 %self_back.1 = (bf16[4,256,512]{2,1,0:T(8,128)(2,1)S(1)}, bf16[4,256,512]{2,1,0:T(8,128)(2,1)S(1)}, bf16[4,256,512]{2,1,0:T(8,128)(2,1)S(1)}, f32[8,512]{1,0:T(8...) custom-call(s32[4]{0:T(128)S(1)} %copy-done.4, s32[3]{0:T(128)S(1)} %pad_add_fusion.place_ref, ...), custom_call_target="tpu_custom_call" | custom-call | flops 24199999488 | bytes 1048576 | tf_op jit(solution)/shard_map/self_back/pallas_call | solution.py:510
  154.2 4.8 %input_grad.1 = (f32[4,256,512]{2,1,0:T(8,128)}, f32[24,512]{1,0:T(8,128)}, f32[2,4,4,8,256]{4,3,2,1,0:T(8,128)S(1)}) custom-call(s32[3]{0:T(128)S(1)} %pad_add_fusion.place_ref, f32[4,256,512]{2,1,0:T(8,128)S(1)} %get-tuple-element.194.grad_ref, bf16[4,256,512]{2,1,0:T(8,128)(2,1)S(1)} %copy-done.2, bf16[4,256,512]{2,1,0:T(8,128)(2,1)S(1)} %get-tuple-element.195.gq_ref, ...), custom_call_target="tpu_custom_call" | custom-call | flops 5500000256 | bytes 1048576 | tf_op jit(solution)/shard_map/input_grad/pallas_call | solution.py:510
  159.8 2.5 %collective-permute-start.34 = (bf16[192,512]{1,0:T(8,128)(2,1)S(1)}, bf16[192,512]{1,0:T(8,128)(2,1)S(1)}, u32[]{:S(2)}, u32[]{:S(2)}) collective-permute-start(bf16[192,512]{1,0:T(8,128)(2,1)S(1)} %get-tuple-element.243), channel_id=1, source_target_pairs={{0,24},{1,25},{2,26},{3,27},{4,28},{5,29},{6,30},{7,31},{8,16},{9,... | collective-permute-start | bytes 589832 | tf_op jit(solution)/shard_map/ppermute | solution.py:693
  162.3 3.2 %collective-permute-start.33 = (bf16[192,512]{1,0:T(8,128)(2,1)S(1)}, bf16[192,512]{1,0:T(8,128)(2,1)S(1)}, u32[]{:S(2)}, u32[]{:S(2)}) collective-permute-start(bf16[192,512]{1,0:T(8,128)(2,1)S(1)} %get-tuple-element.244), channel_id=1, source_target_pairs={{0,16},{1,17},{2,18},{3,19},{4,20},{5,21},{6,22},{7,23},{8,24},{9,... | collective-permute-start | bytes 589832 | tf_op jit(solution)/shard_map/ppermute | solution.py:693
  166.2 1.8 collective-permute-start.31
  168.0 1.2 collective-permute-start.30
  170.1 7.5 %collective-permute-start.32 = (bf16[192,512]{1,0:T(8,128)(2,1)S(1)}, bf16[192,512]{1,0:T(8,128)(2,1)S(1)}, u32[]{:S(2)}, u32[]{:S(2)}) collective-permute-start(bf16[192,512]{1,0:T(8,128)(2,1)S(1)} %get-tuple-element.245), channel_id=1, source_target_pairs={{0,8},{1,9},{2,10},{3,11},{4,12},{5,13},{6,14},{7,15},{8,0},{9,1},... | collective-permute-start | bytes 589832 | tf_op jit(solution)/shard_map/ppermute | solution.py:693
  177.6 3.6 %collective-permute-done.33 = bf16[192,512]{1,0:T(8,128)(2,1)S(1)} collective-permute-done((bf16[192,512]{1,0:T(8,128)(2,1)S(1)}, bf16[192,512]{1,0:T(8,128)(2,1)S(1)}, u32[]{:S(2)}, u32[]{:S(2)}) %collective-permute-start.33) | collective-permute-done | bytes 196640 | tf_op jit(solution)/shard_map/ppermute | solution.py:693
  181.3 4.1 %collective-permute-done.32 = bf16[192,512]{1,0:T(8,128)(2,1)S(1)} collective-permute-done((bf16[192,512]{1,0:T(8,128)(2,1)S(1)}, bf16[192,512]{1,0:T(8,128)(2,1)S(1)}, u32[]{:S(2)}, u32[]{:S(2)}) %collective-permute-start.32) | collective-permute-done | bytes 196640 | tf_op jit(solution)/shard_map/ppermute | solution.py:693
  185.7 2.5 %collective-permute-start.37 = (bf16[72,512]{1,0:T(8,128)(2,1)S(1)}, bf16[72,512]{1,0:T(8,128)(2,1)S(1)}, u32[]{:S(2)}, u32[]{:S(2)}) collective-permute-start(bf16[72,512]{1,0:T(8,128)(2,1)S(1)} %get-tuple-element.249), channel_id=1, source_target_pairs={{0,24},{1,25},{2,26},{3,27},{4,28},{5,29},{6,30},{7,31},{8,16},{9,... | collective-permute-start | bytes 221192 | tf_op jit(solution)/shard_map/ppermute | solution.py:693
  188.2 1.0 collective-permute-start.36
  189.3 0.7 fusion.4
  189.9 0.6 multiply_reduce_fusion.1
  191.9 0.8 collective-permute-done.37
  192.7 3.3 %collective-permute-done.36 = bf16[72,512]{1,0:T(8,128)(2,1)S(1)} collective-permute-done((bf16[72,512]{1,0:T(8,128)(2,1)S(1)}, bf16[72,512]{1,0:T(8,128)(2,1)S(1)}, u32[]{:S(2)}, u32[]{:S(2)}) %collective-permute-start.36) | collective-permute-done | bytes 73760 | tf_op jit(solution)/shard_map/ppermute | solution.py:693
  196.0 0.6 fusion.25
  196.6 0.6 multiply_reduce_fusion.2
  198.5 0.7 broadcast_in_dim.3
  199.2 3.8 %all-to-all-start = ((f32[32,8,128]{2,1,0:T(8,128)}), f32[32,8,128]{2,1,0:T(8,128)S(1)}, u32[]{:S(2)}, u32[]{:S(2)}) async-start(f32[32,8,128]{2,1,0:T(8,128)} %broadcast_in_dim.3), calls=%async_computation | async-start | bytes 262144 | tf_op jit(solution)/shard_map/all_to_all | solution.py:879
  203.0 1.6 copy-done.6
  204.6 1.6 copy-done.8
  206.2 4.2 %memory_grad.1 = f32[4,512,512]{2,1,0:T(8,128)} custom-call(bf16[4,512,512]{2,1,0:T(8,128)(2,1)S(1)} %copy-done.6, bf16[4,512,512]{2,1,0:T(8,128)(2,1)S(1)} %copy-done.8, bf16[4,512,512]{2,1,0:T(8,128)(2,1)S(1)} %get-tuple-element.163.w_ref), custom_call_target="tpu_custom_call" | custom-call | flops 4400000000 | bytes 1048576 | tf_op jit(solution)/shard_map/memory_grad/pallas_call | solution.py:510
  210.5 0.8 all-to-all-done
  211.2 0.6 slice_reduce_fusion
  212.6 0.8 multiply_subtract_fusion.1
  213.5 0.6 multiply_subtract_fusion.3
  214.2 0.8 multiply_subtract_fusion.2
  215.0 1.0 multiply_subtract_fusion
  (152 shorter events, 10.9 us)
Async XLA Ops:
  2.4 7.5 %collective-permute-start.1 = (bf16[72,512]{1,0:T(8,128)(2,1)S(1)}, bf16[72,512]{1,0:T(8,128)(2,1)S(1)}, u32[]{:S(2)}, u32[]{:S(2)}) collective-permute-start(bf16[72,512]{1,0:T(8,128)(2,1)S(1)} %get-tuple-element.258), channel_id=1, source_target_pairs={{0,16},{1,17},{2,18},{3,19},{4,20},{5,21},{6,22},{7,23},{8,24},{9,... | collective-permute-start | bytes 221192 | tf_op jit(solution)/shard_map/ppermute | solution.py:693
  6.5 4.4 %collective-permute-start = (bf16[72,512]{1,0:T(8,128)(2,1)S(1)}, bf16[72,512]{1,0:T(8,128)(2,1)S(1)}, u32[]{:S(2)}, u32[]{:S(2)}) collective-permute-start(bf16[72,512]{1,0:T(8,128)(2,1)S(1)} %get-tuple-element.258), channel_id=1, source_target_pairs={{0,8},{1,9},{2,10},{3,11},{4,12},{5,13},{6,14},{7,15},{8,0},{9,1},... | collective-permute-start | bytes 221192 | tf_op jit(solution)/shard_map/ppermute | solution.py:693
  8.1 6.2 %collective-permute-start.2 = (bf16[72,512]{1,0:T(8,128)(2,1)S(1)}, bf16[72,512]{1,0:T(8,128)(2,1)S(1)}, u32[]{:S(2)}, u32[]{:S(2)}) collective-permute-start(bf16[72,512]{1,0:T(8,128)(2,1)S(1)} %get-tuple-element.258), channel_id=1, source_target_pairs={{0,24},{1,25},{2,26},{3,27},{4,28},{5,29},{6,30},{7,31},{8,16},{9,... | collective-permute-start | bytes 221192 | tf_op jit(solution)/shard_map/ppermute | solution.py:693
  14.3 9.6 %collective-permute-start.8 = (bf16[192,512]{1,0:T(8,128)(2,1)S(1)}, bf16[192,512]{1,0:T(8,128)(2,1)S(1)}, u32[]{:S(2)}, u32[]{:S(2)}) collective-permute-start(bf16[192,512]{1,0:T(8,128)(2,1)S(1)} %pad_maximum_fusion.7), channel_id=1, source_target_pairs={{0,24},{1,25},{2,26},{3,27},{4,28},{5,29},{6,30},{7,31},{8,16},{9,... | collective-permute-start | bytes 589832 | tf_op jit(solution)/shard_map/ppermute | solution.py:693
  16.0 17.8 %collective-permute-start.7 = (bf16[192,512]{1,0:T(8,128)(2,1)S(1)}, bf16[192,512]{1,0:T(8,128)(2,1)S(1)}, u32[]{:S(2)}, u32[]{:S(2)}) collective-permute-start(bf16[192,512]{1,0:T(8,128)(2,1)S(1)} %pad_maximum_fusion.7), channel_id=1, source_target_pairs={{0,16},{1,17},{2,18},{3,19},{4,20},{5,21},{6,22},{7,23},{8,24},{9,... | collective-permute-start | bytes 589832 | tf_op jit(solution)/shard_map/ppermute | solution.py:693
  16.3 17.4 %collective-permute-start.6 = (bf16[192,512]{1,0:T(8,128)(2,1)S(1)}, bf16[192,512]{1,0:T(8,128)(2,1)S(1)}, u32[]{:S(2)}, u32[]{:S(2)}) collective-permute-start(bf16[192,512]{1,0:T(8,128)(2,1)S(1)} %pad_maximum_fusion.7), channel_id=1, source_target_pairs={{0,8},{1,9},{2,10},{3,11},{4,12},{5,13},{6,14},{7,15},{8,0},{9,1},... | collective-permute-start | bytes 589832 | tf_op jit(solution)/shard_map/ppermute | solution.py:693
  18.7 16.0 %collective-permute-start.5 = (bf16[4,72,512]{2,1,0:T(8,128)(2,1)S(1)}, bf16[4,72,512]{2,1,0:T(8,128)(2,1)S(1)}, u32[]{:S(2)}, u32[]{:S(2)}) collective-permute-start(bf16[4,72,512]{2,1,0:T(8,128)(2,1)S(1)} %get-tuple-element.252), channel_id=1, source_target_pairs={{0,6},{1,7},{2,4},{3,5},{4,2},{5,3},{6,0},{7,1},{8,14},{9,15},{10,... | collective-permute-start | bytes 884744 | tf_op jit(solution)/shard_map/ppermute | solution.py:693
  21.2 13.6 %collective-permute-start.4 = (bf16[4,72,512]{2,1,0:T(8,128)(2,1)S(1)}, bf16[4,72,512]{2,1,0:T(8,128)(2,1)S(1)}, u32[]{:S(2)}, u32[]{:S(2)}) collective-permute-start(bf16[4,72,512]{2,1,0:T(8,128)(2,1)S(1)} %get-tuple-element.252), channel_id=1, source_target_pairs={{0,4},{1,5},{2,6},{3,7},{4,0},{5,1},{6,2},{7,3},{8,12},{9,13},{10,... | collective-permute-start | bytes 884744 | tf_op jit(solution)/shard_map/ppermute | solution.py:693
  23.8 10.9 %collective-permute-start.3 = (bf16[4,72,512]{2,1,0:T(8,128)(2,1)S(1)}, bf16[4,72,512]{2,1,0:T(8,128)(2,1)S(1)}, u32[]{:S(2)}, u32[]{:S(2)}) collective-permute-start(bf16[4,72,512]{2,1,0:T(8,128)(2,1)S(1)} %get-tuple-element.252), channel_id=1, source_target_pairs={{0,2},{1,3},{2,0},{3,1},{4,6},{5,7},{6,4},{7,5},{8,10},{9,11},{10,... | collective-permute-start | bytes 884744 | tf_op jit(solution)/shard_map/ppermute | solution.py:693
  33.7 5.9 %copy-start.2 = (bf16[4,256,512]{2,1,0:T(8,128)(2,1)S(1)}, bf16[4,256,512]{2,1,0:T(8,128)(2,1)}, u32[]{:S(2)}) copy-start(bf16[4,256,512]{2,1,0:T(8,128)(2,1)} %x_ref.3) | copy-start | bytes 3145732
  33.7 5.9 %copy-start.4 = (s32[4]{0:T(128)S(1)}, s32[4]{0:T(128)}, u32[]{:S(2)}) copy-start(s32[4]{0:T(128)} %count_ref.9) | copy-start | bytes 52
  34.9 4.7 %collective-permute-start.9 = (bf16[4,4,72,512]{3,2,1,0:T(8,128)(2,1)S(1)}, bf16[4,4,72,512]{3,2,1,0:T(8,128)(2,1)S(1)}, u32[]{:S(2)}, u32[]{:S(2)}) collective-permute-start(bf16[4,4,72,512]{3,2,1,0:T(8,128)(2,1)S(1)} %pad_maximum_fusion.3.refs_0_), channel_id=1, source_target_pairs={{0,1},{1,0},{2,3},{3,2},{4,5},{5,4},{6,7},{7,6},{8,9},{9,8},{10,11... | collective-permute-start | bytes 3538952 | tf_op jit(solution)/shard_map/ppermute | solution.py:693
  36.0 14.6 %collective-permute-start.12 = (bf16[4,64,512]{2,1,0:T(8,128)(2,1)S(1)}, bf16[4,64,512]{2,1,0:T(8,128)(2,1)S(1)}, u32[]{:S(2)}, u32[]{:S(2)}) collective-permute-start(bf16[4,64,512]{2,1,0:T(8,128)(2,1)S(1)} %slice.135), channel_id=1, source_target_pairs={{0,6},{1,7},{2,4},{3,5},{4,2},{5,3},{6,0},{7,1},{8,14},{9,15},{10,... | collective-permute-start | bytes 786440 | tf_op jit(solution)/shard_map/ppermute | solution.py:693
  38.5 12.8 %collective-permute-start.11 = (bf16[4,64,512]{2,1,0:T(8,128)(2,1)S(1)}, bf16[4,64,512]{2,1,0:T(8,128)(2,1)S(1)}, u32[]{:S(2)}, u32[]{:S(2)}) collective-permute-start(bf16[4,64,512]{2,1,0:T(8,128)(2,1)S(1)} %slice.135), channel_id=1, source_target_pairs={{0,4},{1,5},{2,6},{3,7},{4,0},{5,1},{6,2},{7,3},{8,12},{9,13},{10,... | collective-permute-start | bytes 786440 | tf_op jit(solution)/shard_map/ppermute | solution.py:693
  39.0 12.4 %collective-permute-start.10 = (bf16[4,64,512]{2,1,0:T(8,128)(2,1)S(1)}, bf16[4,64,512]{2,1,0:T(8,128)(2,1)S(1)}, u32[]{:S(2)}, u32[]{:S(2)}) collective-permute-start(bf16[4,64,512]{2,1,0:T(8,128)(2,1)S(1)} %slice.135), channel_id=1, source_target_pairs={{0,2},{1,3},{2,0},{3,1},{4,6},{5,7},{6,4},{7,5},{8,10},{9,11},{10,... | collective-permute-start | bytes 786440 | tf_op jit(solution)/shard_map/ppermute | solution.py:693
  39.6 12.0 %copy-start.23 = (bf16[4,192,512]{2,1,0:T(8,128)(2,1)S(1)}, bf16[4,192,512]{2,1,0:T(8,128)(2,1)}, u32[]{:S(2)}) copy-start(bf16[4,192,512]{2,1,0:T(8,128)(2,1)} %pad_maximum_fusion.5) | copy-start | bytes 2359300
  50.6 16.9 %copy-start.13 = (bf16[4,256,512]{2,1,0:T(8,128)(2,1)}, bf16[4,256,512]{2,1,0:T(8,128)(2,1)S(1)}, u32[]{:S(2)}) copy-start(bf16[4,256,512]{2,1,0:T(8,128)(2,1)S(1)} %get-tuple-element.182.value_ref) | copy-start | bytes 3145732
  50.6 16.9 %copy-start.15 = (bf16[4,256,512]{2,1,0:T(8,128)(2,1)}, bf16[4,256,512]{2,1,0:T(8,128)(2,1)S(1)}, u32[]{:S(2)}) copy-start(bf16[4,256,512]{2,1,0:T(8,128)(2,1)S(1)} %get-tuple-element.183.mixed_ref) | copy-start | bytes 3145732
  50.6 4.6 %copy-start = (bf16[4,512,512]{2,1,0:T(8,128)(2,1)S(1)}, bf16[4,512,512]{2,1,0:T(8,128)(2,1)}, u32[]{:S(2)}) copy-start(bf16[4,512,512]{2,1,0:T(8,128)(2,1)} %mem_ref.3) | copy-start | bytes 6291460
  50.6 4.6 %copy-start.3 = (s32[4]{0:T(128)S(1)}, s32[4]{0:T(128)}, u32[]{:S(2)}) copy-start(s32[4]{0:T(128)} %count_ref.8) | copy-start | bytes 52
  51.5 3.7 %collective-permute-start.13 = (bf16[4,4,64,512]{3,2,1,0:T(8,128)(2,1)S(1)}, bf16[4,4,64,512]{3,2,1,0:T(8,128)(2,1)S(1)}, u32[]{:S(2)}, u32[]{:S(2)}) collective-permute-start(bf16[4,4,64,512]{3,2,1,0:T(8,128)(2,1)S(1)} %pad_maximum_fusion.4.refs_0_), channel_id=1, source_target_pairs={{0,1},{1,0},{2,3},{3,2},{4,5},{5,4},{6,7},{7,6},{8,9},{9,8},{10,11... | collective-permute-start | bytes 3145736 | tf_op jit(solution)/shard_map/ppermute | solution.py:693
  51.7 15.9 %collective-permute-start.16 = (bf16[4,128,512]{2,1,0:T(8,128)(2,1)S(1)}, bf16[4,128,512]{2,1,0:T(8,128)(2,1)S(1)}, u32[]{:S(2)}, u32[]{:S(2)}) collective-permute-start(bf16[4,128,512]{2,1,0:T(8,128)(2,1)S(1)} %slice.136), channel_id=1, source_target_pairs={{0,6},{1,7},{2,4},{3,5},{4,2},{5,3},{6,0},{7,1},{8,14},{9,15},{10,... | collective-permute-start | bytes 1572872 | tf_op jit(solution)/shard_map/ppermute | solution.py:693
  53.5 24.7 %collective-permute-start.15 = (bf16[4,128,512]{2,1,0:T(8,128)(2,1)S(1)}, bf16[4,128,512]{2,1,0:T(8,128)(2,1)S(1)}, u32[]{:S(2)}, u32[]{:S(2)}) collective-permute-start(bf16[4,128,512]{2,1,0:T(8,128)(2,1)S(1)} %slice.136), channel_id=1, source_target_pairs={{0,4},{1,5},{2,6},{3,7},{4,0},{5,1},{6,2},{7,3},{8,12},{9,13},{10,... | collective-permute-start | bytes 1572872 | tf_op jit(solution)/shard_map/ppermute | solution.py:693
  54.7 23.5 %collective-permute-start.14 = (bf16[4,128,512]{2,1,0:T(8,128)(2,1)S(1)}, bf16[4,128,512]{2,1,0:T(8,128)(2,1)S(1)}, u32[]{:S(2)}, u32[]{:S(2)}) collective-permute-start(bf16[4,128,512]{2,1,0:T(8,128)(2,1)S(1)} %slice.136), channel_id=1, source_target_pairs={{0,2},{1,3},{2,0},{3,1},{4,6},{5,7},{6,4},{7,5},{8,10},{9,11},{10,... | collective-permute-start | bytes 1572872 | tf_op jit(solution)/shard_map/ppermute | solution.py:693
  67.5 11.0 %copy-start.17 = (bf16[4,256,512]{2,1,0:T(8,128)(2,1)}, bf16[4,256,512]{2,1,0:T(8,128)(2,1)S(1)}, u32[]{:S(2)}) copy-start(bf16[4,256,512]{2,1,0:T(8,128)(2,1)S(1)} %get-tuple-element.157.act_ref) | copy-start | bytes 3145732
  67.5 10.9 %copy-start.19 = (bf16[4,256,512]{2,1,0:T(8,128)(2,1)}, bf16[4,256,512]{2,1,0:T(8,128)(2,1)S(1)}, u32[]{:S(2)}) copy-start(bf16[4,256,512]{2,1,0:T(8,128)(2,1)S(1)} %get-tuple-element.158.query_ref) | copy-start | bytes 3145732
  67.5 10.9 %copy-start.21 = (bf16[4,256,512]{2,1,0:T(8,128)(2,1)}, bf16[4,256,512]{2,1,0:T(8,128)(2,1)S(1)}, u32[]{:S(2)}) copy-start(bf16[4,256,512]{2,1,0:T(8,128)(2,1)S(1)} %get-tuple-element.161.mixed_ref) | copy-start | bytes 3145732
  78.2 4.5 %copy-start.1 = (bf16[4,256,512]{2,1,0:T(8,128)(2,1)S(1)}, bf16[4,256,512]{2,1,0:T(8,128)(2,1)}, u32[]{:S(2)}) copy-start(bf16[4,256,512]{2,1,0:T(8,128)(2,1)} %cot_ref.1) | copy-start | bytes 3145732
  78.5 4.2 %collective-permute-start.17 = (bf16[4,4,128,512]{3,2,1,0:T(8,128)(2,1)S(1)}, bf16[4,4,128,512]{3,2,1,0:T(8,128)(2,1)S(1)}, u32[]{:S(2)}, u32[]{:S(2)}) collective-permute-start(bf16[4,4,128,512]{3,2,1,0:T(8,128)(2,1)S(1)} %pad_maximum_fusion.1.refs_0_.refs_2_), channel_id=1, source_target_pairs={{0,1},{1,0},{2,3},{3,2},{4,5},{5,4},{6,7},{7,6},{8,9},{9,8},{10,11... | collective-permute-start | bytes 6291464 | tf_op jit(solution)/shard_map/ppermute | solution.py:693
  103.9 2.7 %collective-permute-start.18 = (bf16[4,4,64,512]{3,2,1,0:T(8,128)(2,1)S(1)}, bf16[4,4,64,512]{3,2,1,0:T(8,128)(2,1)S(1)}, u32[]{:S(2)}, u32[]{:S(2)}) collective-permute-start(bf16[4,4,64,512]{3,2,1,0:T(8,128)(2,1)S(1)} %get-tuple-element.153), channel_id=1, source_target_pairs={{0,1},{1,0},{2,3},{3,2},{4,5},{5,4},{6,7},{7,6},{8,9},{9,8},{10,11... | collective-permute-start | bytes 3145736 | tf_op jit(solution)/shard_map/ppermute | solution.py:693
  104.1 4.0 %collective-permute-start.19 = (bf16[4,4,64,512]{3,2,1,0:T(8,128)(2,1)S(1)}, bf16[4,4,64,512]{3,2,1,0:T(8,128)(2,1)S(1)}, u32[]{:S(2)}, u32[]{:S(2)}) collective-permute-start(bf16[4,4,64,512]{3,2,1,0:T(8,128)(2,1)S(1)} %get-tuple-element.155), channel_id=1, source_target_pairs={{0,1},{1,0},{2,3},{3,2},{4,5},{5,4},{6,7},{7,6},{8,9},{9,8},{10,11... | collective-permute-start | bytes 3145736 | tf_op jit(solution)/shard_map/ppermute | solution.py:693
  109.3 3.8 %copy-start.18 = (bf16[4,256,512]{2,1,0:T(8,128)(2,1)S(1)}, bf16[4,256,512]{2,1,0:T(8,128)(2,1)}, u32[]{:S(2)}) copy-start(bf16[4,256,512]{2,1,0:T(8,128)(2,1)} %copy-done.17) | copy-start | bytes 3145732
  109.6 22.9 %collective-permute-start.22 = (bf16[4,128,512]{2,1,0:T(8,128)(2,1)S(1)}, bf16[4,128,512]{2,1,0:T(8,128)(2,1)S(1)}, u32[]{:S(2)}, u32[]{:S(2)}) collective-permute-start(bf16[4,128,512]{2,1,0:T(8,128)(2,1)S(1)} %get-tuple-element.234), channel_id=1, source_target_pairs={{0,6},{1,7},{2,4},{3,5},{4,2},{5,3},{6,0},{7,1},{8,14},{9,15},{10,... | collective-permute-start | bytes 1572872 | tf_op jit(solution)/shard_map/ppermute | solution.py:693
  111.3 24.4 %collective-permute-start.21 = (bf16[4,128,512]{2,1,0:T(8,128)(2,1)S(1)}, bf16[4,128,512]{2,1,0:T(8,128)(2,1)S(1)}, u32[]{:S(2)}, u32[]{:S(2)}) collective-permute-start(bf16[4,128,512]{2,1,0:T(8,128)(2,1)S(1)} %get-tuple-element.235), channel_id=1, source_target_pairs={{0,4},{1,5},{2,6},{3,7},{4,0},{5,1},{6,2},{7,3},{8,12},{9,13},{10,... | collective-permute-start | bytes 1572872 | tf_op jit(solution)/shard_map/ppermute | solution.py:693
  112.6 23.2 %collective-permute-start.20 = (bf16[4,128,512]{2,1,0:T(8,128)(2,1)S(1)}, bf16[4,128,512]{2,1,0:T(8,128)(2,1)S(1)}, u32[]{:S(2)}, u32[]{:S(2)}) collective-permute-start(bf16[4,128,512]{2,1,0:T(8,128)(2,1)S(1)} %get-tuple-element.236), channel_id=1, source_target_pairs={{0,2},{1,3},{2,0},{3,1},{4,6},{5,7},{6,4},{7,5},{8,10},{9,11},{10,... | collective-permute-start | bytes 1572872 | tf_op jit(solution)/shard_map/ppermute | solution.py:693
  135.7 2.7 %collective-permute-start.23 = (bf16[4,4,64,512]{3,2,1,0:T(8,128)(2,1)S(1)}, bf16[4,4,64,512]{3,2,1,0:T(8,128)(2,1)S(1)}, u32[]{:S(2)}, u32[]{:S(2)}) collective-permute-start(bf16[4,4,64,512]{3,2,1,0:T(8,128)(2,1)S(1)} %get-tuple-element.173), channel_id=1, source_target_pairs={{0,1},{1,0},{2,3},{3,2},{4,5},{5,4},{6,7},{7,6},{8,9},{9,8},{10,11... | collective-permute-start | bytes 3145736 | tf_op jit(solution)/shard_map/ppermute | solution.py:693
  138.7 3.8 %copy-start.10 = (bf16[4,256,512]{2,1,0:T(8,128)(2,1)S(1)}, bf16[4,256,512]{2,1,0:T(8,128)(2,1)}, u32[]{:S(2)}) copy-start(bf16[4,256,512]{2,1,0:T(8,128)(2,1)} %copy-done.9) | copy-start | bytes 3145732
  138.7 3.8 %copy-start.12 = (bf16[4,256,512]{2,1,0:T(8,128)(2,1)S(1)}, bf16[4,256,512]{2,1,0:T(8,128)(2,1)}, u32[]{:S(2)}) copy-start(bf16[4,256,512]{2,1,0:T(8,128)(2,1)} %copy-done.11) | copy-start | bytes 3145732
  138.7 3.8 %copy-start.14 = (bf16[4,256,512]{2,1,0:T(8,128)(2,1)S(1)}, bf16[4,256,512]{2,1,0:T(8,128)(2,1)}, u32[]{:S(2)}) copy-start(bf16[4,256,512]{2,1,0:T(8,128)(2,1)} %copy-done.13) | copy-start | bytes 3145732
  138.7 3.8 %copy-start.16 = (bf16[4,256,512]{2,1,0:T(8,128)(2,1)S(1)}, bf16[4,256,512]{2,1,0:T(8,128)(2,1)}, u32[]{:S(2)}) copy-start(bf16[4,256,512]{2,1,0:T(8,128)(2,1)} %copy-done.15) | copy-start | bytes 3145732
  139.0 15.1 %collective-permute-start.26 = (bf16[4,64,512]{2,1,0:T(8,128)(2,1)S(1)}, bf16[4,64,512]{2,1,0:T(8,128)(2,1)S(1)}, u32[]{:S(2)}, u32[]{:S(2)}) collective-permute-start(bf16[4,64,512]{2,1,0:T(8,128)(2,1)S(1)} %get-tuple-element.240), channel_id=1, source_target_pairs={{0,6},{1,7},{2,4},{3,5},{4,2},{5,3},{6,0},{7,1},{8,14},{9,15},{10,... | collective-permute-start | bytes 786440 | tf_op jit(solution)/shard_map/ppermute | solution.py:693
  140.7 13.3 %collective-permute-start.25 = (bf16[4,64,512]{2,1,0:T(8,128)(2,1)S(1)}, bf16[4,64,512]{2,1,0:T(8,128)(2,1)S(1)}, u32[]{:S(2)}, u32[]{:S(2)}) collective-permute-start(bf16[4,64,512]{2,1,0:T(8,128)(2,1)S(1)} %get-tuple-element.241), channel_id=1, source_target_pairs={{0,4},{1,5},{2,6},{3,7},{4,0},{5,1},{6,2},{7,3},{8,12},{9,13},{10,... | collective-permute-start | bytes 786440 | tf_op jit(solution)/shard_map/ppermute | solution.py:693
  142.0 12.1 %collective-permute-start.24 = (bf16[4,64,512]{2,1,0:T(8,128)(2,1)S(1)}, bf16[4,64,512]{2,1,0:T(8,128)(2,1)S(1)}, u32[]{:S(2)}, u32[]{:S(2)}) collective-permute-start(bf16[4,64,512]{2,1,0:T(8,128)(2,1)S(1)} %get-tuple-element.242), channel_id=1, source_target_pairs={{0,2},{1,3},{2,0},{3,1},{4,6},{5,7},{6,4},{7,5},{8,10},{9,11},{10,... | collective-permute-start | bytes 786440 | tf_op jit(solution)/shard_map/ppermute | solution.py:693
  154.1 11.5 %collective-permute-start.27 = (bf16[4,4,64,512]{3,2,1,0:T(8,128)(2,1)S(1)}, bf16[4,4,64,512]{3,2,1,0:T(8,128)(2,1)S(1)}, u32[]{:S(2)}, u32[]{:S(2)}) collective-permute-start(bf16[4,4,64,512]{3,2,1,0:T(8,128)(2,1)S(1)} %get-tuple-element.203), channel_id=1, source_target_pairs={{0,1},{1,0},{2,3},{3,2},{4,5},{5,4},{6,7},{7,6},{8,9},{9,8},{10,11... | collective-permute-start | bytes 3145736 | tf_op jit(solution)/shard_map/ppermute | solution.py:693
  159.0 6.6 %collective-permute-start.28 = (bf16[4,4,8,256]{3,2,1,0:T(8,128)(2,1)S(1)}, bf16[4,4,8,256]{3,2,1,0:T(8,128)(2,1)S(1)}, u32[]{:S(2)}, u32[]{:S(2)}) collective-permute-start(bf16[4,4,8,256]{3,2,1,0:T(8,128)(2,1)S(1)} %fusion.10), channel_id=1, source_target_pairs={{0,1},{1,0},{2,3},{3,2},{4,5},{5,4},{6,7},{7,6},{8,9},{9,8},{10,11... | collective-permute-start | bytes 196616 | tf_op jit(solution)/shard_map/ppermute | solution.py:693
  159.8 10.2 %collective-permute-start.34 = (bf16[192,512]{1,0:T(8,128)(2,1)S(1)}, bf16[192,512]{1,0:T(8,128)(2,1)S(1)}, u32[]{:S(2)}, u32[]{:S(2)}) collective-permute-start(bf16[192,512]{1,0:T(8,128)(2,1)S(1)} %get-tuple-element.243), channel_id=1, source_target_pairs={{0,24},{1,25},{2,26},{3,27},{4,28},{5,29},{6,30},{7,31},{8,16},{9,... | collective-permute-start | bytes 589832 | tf_op jit(solution)/shard_map/ppermute | solution.py:693
  162.3 19.0 %collective-permute-start.33 = (bf16[192,512]{1,0:T(8,128)(2,1)S(1)}, bf16[192,512]{1,0:T(8,128)(2,1)S(1)}, u32[]{:S(2)}, u32[]{:S(2)}) collective-permute-start(bf16[192,512]{1,0:T(8,128)(2,1)S(1)} %get-tuple-element.244), channel_id=1, source_target_pairs={{0,16},{1,17},{2,18},{3,19},{4,20},{5,21},{6,22},{7,23},{8,24},{9,... | collective-permute-start | bytes 589832 | tf_op jit(solution)/shard_map/ppermute | solution.py:693
  166.2 19.2 %collective-permute-start.31 = (bf16[4,72,512]{2,1,0:T(8,128)(2,1)S(1)}, bf16[4,72,512]{2,1,0:T(8,128)(2,1)S(1)}, u32[]{:S(2)}, u32[]{:S(2)}) collective-permute-start(bf16[4,72,512]{2,1,0:T(8,128)(2,1)S(1)} %get-tuple-element.237), channel_id=1, source_target_pairs={{0,6},{1,7},{2,4},{3,5},{4,2},{5,3},{6,0},{7,1},{8,14},{9,15},{10,... | collective-permute-start | bytes 884744 | tf_op jit(solution)/shard_map/ppermute | solution.py:693
  168.0 17.4 %collective-permute-start.30 = (bf16[4,72,512]{2,1,0:T(8,128)(2,1)S(1)}, bf16[4,72,512]{2,1,0:T(8,128)(2,1)S(1)}, u32[]{:S(2)}, u32[]{:S(2)}) collective-permute-start(bf16[4,72,512]{2,1,0:T(8,128)(2,1)S(1)} %get-tuple-element.238), channel_id=1, source_target_pairs={{0,4},{1,5},{2,6},{3,7},{4,0},{5,1},{6,2},{7,3},{8,12},{9,13},{10,... | collective-permute-start | bytes 884744 | tf_op jit(solution)/shard_map/ppermute | solution.py:693
  169.2 16.2 %collective-permute-start.29 = (bf16[4,72,512]{2,1,0:T(8,128)(2,1)S(1)}, bf16[4,72,512]{2,1,0:T(8,128)(2,1)S(1)}, u32[]{:S(2)}, u32[]{:S(2)}) collective-permute-start(bf16[4,72,512]{2,1,0:T(8,128)(2,1)S(1)} %get-tuple-element.239), channel_id=1, source_target_pairs={{0,2},{1,3},{2,0},{3,1},{4,6},{5,7},{6,4},{7,5},{8,10},{9,11},{10,... | collective-permute-start | bytes 884744 | tf_op jit(solution)/shard_map/ppermute | solution.py:693
  170.1 15.3 %collective-permute-start.32 = (bf16[192,512]{1,0:T(8,128)(2,1)S(1)}, bf16[192,512]{1,0:T(8,128)(2,1)S(1)}, u32[]{:S(2)}, u32[]{:S(2)}) collective-permute-start(bf16[192,512]{1,0:T(8,128)(2,1)S(1)} %get-tuple-element.245), channel_id=1, source_target_pairs={{0,8},{1,9},{2,10},{3,11},{4,12},{5,13},{6,14},{7,15},{8,0},{9,1},... | collective-permute-start | bytes 589832 | tf_op jit(solution)/shard_map/ppermute | solution.py:693
  185.6 6.3 %collective-permute-start.35 = (bf16[72,512]{1,0:T(8,128)(2,1)S(1)}, bf16[72,512]{1,0:T(8,128)(2,1)S(1)}, u32[]{:S(2)}, u32[]{:S(2)}) collective-permute-start(bf16[72,512]{1,0:T(8,128)(2,1)S(1)} %get-tuple-element.248), channel_id=1, source_target_pairs={{0,8},{1,9},{2,10},{3,11},{4,12},{5,13},{6,14},{7,15},{8,0},{9,1},... | collective-permute-start | bytes 221192 | tf_op jit(solution)/shard_map/ppermute | solution.py:693
  185.7 7.0 %collective-permute-start.37 = (bf16[72,512]{1,0:T(8,128)(2,1)S(1)}, bf16[72,512]{1,0:T(8,128)(2,1)S(1)}, u32[]{:S(2)}, u32[]{:S(2)}) collective-permute-start(bf16[72,512]{1,0:T(8,128)(2,1)S(1)} %get-tuple-element.249), channel_id=1, source_target_pairs={{0,24},{1,25},{2,26},{3,27},{4,28},{5,29},{6,30},{7,31},{8,16},{9,... | collective-permute-start | bytes 221192 | tf_op jit(solution)/shard_map/ppermute | solution.py:693
  188.2 7.8 %collective-permute-start.36 = (bf16[72,512]{1,0:T(8,128)(2,1)S(1)}, bf16[72,512]{1,0:T(8,128)(2,1)S(1)}, u32[]{:S(2)}, u32[]{:S(2)}) collective-permute-start(bf16[72,512]{1,0:T(8,128)(2,1)S(1)} %get-tuple-element.250), channel_id=1, source_target_pairs={{0,16},{1,17},{2,18},{3,19},{4,20},{5,21},{6,22},{7,23},{8,24},{9,... | collective-permute-start | bytes 221192 | tf_op jit(solution)/shard_map/ppermute | solution.py:693
  199.2 12.1 %all-to-all-start = ((f32[32,8,128]{2,1,0:T(8,128)}), f32[32,8,128]{2,1,0:T(8,128)S(1)}, u32[]{:S(2)}, u32[]{:S(2)}) async-start(f32[32,8,128]{2,1,0:T(8,128)} %broadcast_in_dim.3), calls=%async_computation | async-start | bytes 262144 | tf_op jit(solution)/shard_map/all_to_all | solution.py:879
  206.2 6.4 %copy-start.26 = (f32[64,512]{1,0:T(8,128)S(1)}, f32[64,512]{1,0:T(8,128)}, u32[]{:S(2)}) copy-start(f32[64,512]{1,0:T(8,128)} %param.24) | copy-start | bytes 393220
  206.2 6.4 %copy-start.31 = (f32[64,512]{1,0:T(8,128)S(1)}, f32[64,512]{1,0:T(8,128)}, u32[]{:S(2)}) copy-start(f32[64,512]{1,0:T(8,128)} %param.31) | copy-start | bytes 393220
  206.2 6.4 %copy-start.32 = (f32[64,512]{1,0:T(8,128)S(1)}, f32[64,512]{1,0:T(8,128)}, u32[]{:S(2)}) copy-start(f32[64,512]{1,0:T(8,128)} %param.30) | copy-start | bytes 393220
  206.2 7.3 %copy-start.33 = (f32[17,16]{0,1:T(8,128)S(1)}, f32[17,16]{0,1:T(8,128)}, u32[]{:S(2)}) copy-start(f32[17,16]{0,1:T(8,128)} %param.25) | copy-start | bytes 3268
  206.2 7.3 %copy-start.34 = (f32[17,16]{0,1:T(8,128)S(1)}, f32[17,16]{0,1:T(8,128)}, u32[]{:S(2)}) copy-start(f32[17,16]{0,1:T(8,128)} %param.33) | copy-start | bytes 3268
  206.2 7.3 %copy-start.35 = (f32[17,16]{0,1:T(8,128)S(1)}, f32[17,16]{0,1:T(8,128)}, u32[]{:S(2)}) copy-start(f32[17,16]{0,1:T(8,128)} %param.32) | copy-start | bytes 3268
  210.4 4.6 %copy-start.24 = (f32[8,16,512]{2,1,0:T(8,128)S(1)}, f32[8,16,512]{2,1,0:T(8,128)}, u32[]{:S(2)}) copy-start(f32[8,16,512]{2,1,0:T(8,128)} %param.22) | copy-start | bytes 786436
  210.4 4.5 %copy-start.27 = (f32[8,16,512]{2,1,0:T(8,128)S(1)}, f32[8,16,512]{2,1,0:T(8,128)}, u32[]{:S(2)}) copy-start(f32[8,16,512]{2,1,0:T(8,128)} %param.27) | copy-start | bytes 786436
  210.4 4.5 %copy-start.28 = (f32[8,16,512]{2,1,0:T(8,128)S(1)}, f32[8,16,512]{2,1,0:T(8,128)}, u32[]{:S(2)}) copy-start(f32[8,16,512]{2,1,0:T(8,128)} %param.26) | copy-start | bytes 786436
  (11 other events, 31.4 us)

commit v5 on v4

--- a/solution.py
+++ b/solution.py
@@ -19,7 +19,6 @@
 SCALE = HEAD_DIM ** (-0.5)
 LOW = jnp.bfloat16
 F32 = jnp.float32
-LIMIT = 60 * 1024 * 1024
 
 
 def dot_nn(left, right):
@@ -427,57 +426,43 @@
 
 
 def self_back_kernel(
-    own, count_ref, place_ref, grad_ref, act_ref, query_ref, key_ref, value_ref, mixed_ref,
-    lse_ref, w_ref, *refs,
+    own, count_ref, place_ref, grad_ref, x_ref, act_ref, query_ref, key_ref, value_ref, mixed_ref,
+    lse_ref, w_ref, table_ref, two_ref, three_ref, *refs,
 ):
-    gq_ref, gk_ref, gv_ref, small_ref = refs[:4]
+    out_ref, small_ref = refs[:2]
     if own:
-        keep_ref, send_ref, bias, gq_t, gw = refs[4:]
-    else:
-        gw, bias, gq_t = refs[4:]
+        keep_ref, send_ref, parts_ref, bias, gq_t, gk_ref, gv_ref, gw, turned = refs[2:]
+    else:
+        gw, bias, gq_t, gk_ref, gv_ref = refs[2:]
     begin_sums(gw, small_ref)
     count = count_ref[pl.program_id(0)]
     bias[...] = causal_bias(bias.shape[0])
-    low = grad_ref[0].astype(LOW)
+    grad = grad_ref[0]
+    low = grad.astype(LOW)
     gw[3] += dot_tn(mixed_ref[0], low)
-    small_ref[4:5] += column_sum(low)
+    small_ref[8:9] += column_sum(low)
     grad_mixed = dot_nt(low, w_ref[3]).astype(LOW)
     attend_back(query_ref, key_ref, value_ref, mixed_ref, grad_mixed, count, bias, lse_ref, gq_t, gk_ref, gv_ref)
     gq = (gq_t[...] * SCALE).T.astype(LOW)
-    gq_ref[0] = gq
-    small_ref[2:3] += column_sum(gq)
-    small_ref[3:4] += column_sum(gv_ref[0])
+    small_ref[6:7] += column_sum(gq)
+    small_ref[7:8] += column_sum(gv_ref[0])
+    back = dot_nt(gq, w_ref[0]) + dot_nt(gk_ref[0], w_ref[1]) + dot_nt(gv_ref[0], w_ref[2])
     gw[0] += dot_tn(act_ref[0], gq)
     gw[1] += dot_tn(act_ref[0], gk_ref[0])
     gw[2] += dot_tn(act_ref[0], gv_ref[0])
-    if own:
-        end_sums(own, place_ref, gw, keep_ref, send_ref)
-
-
-def memory_kernel(gk_ref, gv_ref, w_ref, out_ref):
-    out_ref[0] = dot_nt(gk_ref[0], w_ref[1]) + dot_nt(gv_ref[0], w_ref[2])
-
-
-def input_kernel(own, place_ref, grad_ref, x_ref, gq_ref, gk_ref, gv_ref, w_ref, table_ref, *refs):
-    out_ref, small_ref = refs[-4:-2] if own else refs[-2:]
-    begin_sums(small_ref)
-    back = dot_nt(gq_ref[0], w_ref[0]) + dot_nt(gk_ref[0], w_ref[1]) + dot_nt(gv_ref[0], w_ref[2])
     hat, inverse = normalize(x_ref[0].astype(F32))
     small_ref[0:1] += column_sum(back * hat)
     small_ref[1:2] += column_sum(back)
-    out_ref[0] = grad_ref[0] + normalize_back(back, hat, inverse, table_ref[0:1])
+    out_ref[0] = grad + normalize_back(back, hat, inverse, table_ref[0:1])
 
     @pl.when(pl.program_id(0) == pl.num_programs(0) - 1)
     def _():
-        one_ref, two_ref, three_ref = refs[:3]
         small_ref[2:4] = two_ref[0:2]
         small_ref[4:6] = three_ref[0:2]
-        small_ref[6:9] = one_ref[2:5]
         small_ref[9:12] = two_ref[2:5]
         small_ref[12:13] = three_ref[2:3]
         small_ref[13:17] = three_ref[8:12]
         if own:
-            parts_ref, turned = refs[-2:]
             wide = jnp.concatenate([small_ref[...], jnp.zeros((128 - small_ref.shape[0], small_ref.shape[1]), F32)], 0)
             turned[...] = wide.T
             _, planes, depths = parts_ref.shape[:3]
@@ -490,6 +475,13 @@
                             rows = turned[pl.ds(pl.multiple_of(first + 8 * half, 8), 8)]
                             parts_ref[core, plane, depth, :, 128 * half : 128 * (half + 1)] = rows
 
+    if own:
+        end_sums(own, place_ref, gw, keep_ref, send_ref)
+
+
+def memory_kernel(gk_ref, gv_ref, w_ref, out_ref):
+    out_ref[0] = dot_nt(gk_ref[0], w_ref[1]) + dot_nt(gv_ref[0], w_ref[2])
+
 
 def by_seq(*tail):
     return pl.BlockSpec((1,) + tail, lambda seq, *_: (seq,) + (0,) * len(tail))
@@ -503,7 +495,7 @@
     return jax.ShapeDtypeStruct(shape, dtype)
 
 
-LIMITS = {'self_forward': 20, 'cross_forward': 20, 'ffn': 28, 'cross_back': 26, 'self_back': 20, 'input_grad': 16, 'memory_grad': 16}
+LIMITS = {"self_forward": 20, "cross_forward": 20, "ffn": 28, "cross_back": 26, "self_back": 22, "memory_grad": 16}
 
 
 def call(kernel, name, work, grid, scalars, args, in_specs, outs, out_specs, scratch):
@@ -632,15 +624,27 @@
     )
 
 
-def self_back(lengths, grid, grad, act, query, key, value, mixed, lse, weights):
+def self_back(lengths, grid, grad, x, act, query, key, value, mixed, lse, weights, table, smalls):
     seqs, length, width = query.shape
     block = by_seq(length, width)
-    return back_call(
-        self_back_kernel, "self_back", 22, lengths, grid,
-        (grad, act, query, key, value, mixed, lse, weights),
-        [block] * 6 + [by_seq(HEADS, length), fixed(4, width, width)],
-        [(query.shape, LOW)] * 3, [block] * 3,
-        [pltpu.VMEM((length, length), F32), pltpu.VMEM((width, length), F32)],
+    gw, small = (4, width, width), (24, width)
+    outs, out_specs = [(x.shape, F32), (small, F32)], [block, fixed(*small)]
+    scratch = [pltpu.VMEM((length, length), F32), pltpu.VMEM((width, length), F32)]
+    scratch += [pltpu.VMEM((1, length, width), LOW)] * 2
+    if grid.own:
+        sides = grid.sizes[1::-1]
+        parts, tables = sides + (4 * grid.own, width), (2,) + sides + (8, 256)
+        outs += [(parts, LOW)] * 2 + [(tables, F32)]
+        out_specs += [fixed(*parts)] * 2 + [fixed(*tables)]
+        scratch += [pltpu.VMEM(gw, F32), pltpu.VMEM((width, 128), F32)]
+    else:
+        outs, out_specs = outs + [(gw, F32)], out_specs + [fixed(*gw)]
+    return call(
+        partial(self_back_kernel, grid.own), "self_back", 22, (seqs,), (lengths, grid.spot),
+        (grad, x, act, query, key, value, mixed, lse, weights, table, *smalls),
+        [block] * 7 + [by_seq(HEADS, length), fixed(*gw), fixed(*table.shape)]
+        + [fixed(*small_part.shape) for small_part in smalls],
+        outs, out_specs, scratch,
     )
 
 
@@ -653,19 +657,8 @@
     )[0]
 
 
-def input_grad(grid, grad, x, gq, gk, gv, weights, table, smalls):
-    seqs, length, width = x.shape
-    block = by_seq(length, width)
-    outs, out_specs, scratch = [(x.shape, F32), ((24, width), F32)], [block, fixed(24, width)], []
-    if grid.own:
-        parts = (2,) + grid.sizes[1::-1] + (8, 256)
-        outs, out_specs, scratch = outs + [(parts, F32)], out_specs + [fixed(*parts)], [pltpu.VMEM((width, 128), F32)]
-    return call(
-        partial(input_kernel, grid.own), "input_grad", 5, (seqs,), (grid.spot,),
-        (grad, x, gq, gk, gv, weights, table, *smalls),
-        [block] * 5 + [fixed(4, width, width), fixed(*table.shape)] + [fixed(*small.shape) for small in smalls],
-        outs, out_specs, scratch,
-    )
+def half_add(parts, got):
+    return [part.astype(F32) + got[index].astype(F32) for index, part in enumerate(parts[0::2])]
 
 
 def tie(value, *others):
@@ -700,6 +693,9 @@
 
     def fetch(self, parts, stage):
         return [parts[0]] + [self.swap(parts[step].astype(LOW), stage, step) for step in range(1, self.sizes[stage])]
+
+    def half_send(self, parts, stage, step):
+        return self.swap(jnp.stack([part.astype(LOW) for part in parts[1::2]]), stage, step)
 
     def absolute(self, mine, other):
         depths, planes, _ = self.sizes
@@ -791,14 +787,20 @@
         return jnp.swapaxes(w_in, 1, 2).reshape(width, hidden), full[:, :out_rows].reshape(hidden, width)
 
     self_depth = grid.spread(self_chunk, 0)
-    late_depth = grid.spread(tie(jnp.concatenate([cross_chunk, ffn_chunk], 0), self_depth), 0)
+    cross_chunk, ffn_chunk, self_depth = lax.optimization_barrier((cross_chunk, ffn_chunk, self_depth))
     self_plane = grid.spread(self_depth, 1)
-    self_plane, late_depth = lax.optimization_barrier((self_plane, late_depth))
-    cross_parts = grid.send(late_depth[:, : 4 * own], 1)
+    cross_parts = grid.send(cross_chunk, 0)
+    ffn_got = grid.swap(ffn_chunk, 0, 1)
+    cross_parts, self_plane = lax.optimization_barrier((cross_parts, self_plane))
+    ffn_got = tie(ffn_got, cross_parts)
+    cross_parts = grid.send(jnp.stack(cross_parts), 1)
+    ffn_parts = jnp.stack([ffn_chunk, ffn_got])
+    ffn_got = grid.swap(ffn_parts, 0, 2)
     first = self_forward(lengths, grid, inputs, attn_whole(self_plane, grid.swap(self_plane, 2, 1)))
-    first, cross_parts = lax.optimization_barrier((first, cross_parts))
+    first, cross_parts, ffn_got = lax.optimization_barrier((first, cross_parts, ffn_got))
+    ffn_depth = jnp.concatenate([ffn_parts, ffn_got], 0)
     act_one, query_one, key_one, value_one, mixed_one, lse_one, resid_one, w_self, table = first
-    ffn_parts = grid.send(tie(late_depth[:, 4 * own :], cross_parts), 1)
+    ffn_parts = grid.send(tie(ffn_depth, cross_parts), 1)
     cross_plane = jnp.stack(cross_parts)
     second = cross_forward(
         mem_lengths, grid, resid_one, memory, table, attn_whole(cross_plane, grid.swap(cross_plane, 2, 1))
@@ -834,37 +836,44 @@
     grad_one, gk_two, gv_two, small_two, *cross_grads = cross
     cross_sum = meet(*attn_parts(cross_grads))
     ffn_sum = add_all(ffn_got)
-    grad_one, cross_sum, ffn_sum = lax.optimization_barrier((grad_one, cross_sum, ffn_sum))
+    ffn_parts = [ffn_sum[place] for place in range(grid.sizes[0])]
+    grad_one, cross_sum, ffn_parts = lax.optimization_barrier((grad_one, cross_sum, ffn_parts))
+    ffn_got = grid.half_send(ffn_parts, 0, 1)
     cross_got = grid.fetch(cross_sum, 1)
     state = self_back(
-        lengths, grid, grad_one, act_one, query_one, key_one, value_one, mixed_one, lse_one, w_self
-    )
-    state, cross_got = lax.optimization_barrier((state, cross_got))
-    gq_one, gk_one, gv_one, small_one, *self_grads = state
-    self_keep, self_send = attn_parts(self_grads)
-    late_got = grid.fetch(jnp.concatenate([add_all(cross_got), ffn_sum], 1), 0)
-    self_got = grid.swap(self_send, 2, 1)
-    grad_one_late = tie(grad_one, self_keep)
-    smalls = (small_one, small_two, small_three)
-    grad_input, grad_table, *table_parts = input_grad(
-        grid, grad_one_late, inputs, gq_one, gk_one, gv_one, w_self, table, smalls
-    )
+        lengths, grid, grad_one, inputs, act_one, query_one, key_one, value_one, mixed_one, lse_one, w_self,
+        table, (small_two, small_three),
+    )
+    state, cross_got, ffn_got = lax.optimization_barrier((state, cross_got, ffn_got))
+    ffn_parts = half_add(ffn_parts, ffn_got)
+    grad_input, grad_table, *self_grads = state
     if grid.own:
-        table_keep, table_send = table_parts[0][0], table_parts[0][1]
-    else:
+        self_keep, self_send, table_parts = self_grads
+        table_keep, table_send = table_parts[0], table_parts[1]
+    else:
+        self_keep, self_send = attn_parts(self_grads)
         parts = jnp.swapaxes(grad_table[:count].reshape(count, grid.devices, own), 0, 1)
         parts = jnp.pad(parts.reshape(grid.devices, count * own), ((0, 0), (0, -count * own % 256)))
         parts = jnp.pad(parts.reshape(grid.devices, -1, 256), ((0, 0), (0, 7), (0, 0)))[:, :8]
         table_keep, table_send = grid.relative(parts)
+    self_got = grid.swap(self_send, 2, 1)
+    late_sum = add_all(cross_got)
     table_sum = table_keep + grid.swap(table_send.astype(LOW), 2, 1).astype(F32)
     self_sum = self_keep.astype(F32) + self_got.astype(F32)
     table_sum = jnp.pad(table_sum, ((0, 0), (0, 0), (0, 0), (0, width - 256)))
     self_sum = jnp.concatenate([self_sum, table_sum], 2)
+    self_sum, late_sum, ffn_parts = lax.optimization_barrier((self_sum, late_sum, ffn_parts))
     last_got = grid.fetch(self_sum, 1)
-    last_got, late_got = lax.optimization_barrier((last_got, late_got))
-    last_share = add_all(grid.fetch(add_all(last_got), 0))
-    late_share = add_all(late_got)
-    cross_share, ffn_share = late_share[: 4 * own], late_share[4 * own :]
+    late_got = grid.fetch(late_sum, 0)
+    step = 2
+    while step < grid.sizes[0]:
+        ffn_got = grid.half_send(ffn_parts, 0, step)
+        ffn_parts = half_add(ffn_parts, ffn_got)
+        step *= 2
+    last_sum = add_all(last_got)
+    late_got, ffn_share, last_sum = lax.optimization_barrier((late_got, ffn_parts[0], last_sum))
+    last_share = add_all(grid.fetch(last_sum, 0))
+    cross_share = add_all(late_got)
     self_share = last_share[: 4 * own]
     table_share = last_share[4 * own :, :256]
     if grid.own:

time: 218 us -> 210 us (0.963)
  starting transfers between devices: 54.4 us -> 46.2 us
  waiting for transfers between devices: 51.8 us -> 55.1 us
    ppermute x38 -> x42, starting transfers between devices: 50.6 us -> 43.1 us  [swap(): return lax.ppermute(values, AXES, pairs)]
    ppermute x38 -> x42, waiting for transfers between devices: 51 us -> 54.3 us  [swap(): return lax.ppermute(values, AXES, pairs)]
    pallas_call x7 -> x6, Pallas kernels: 82.1 us -> 80.4 us  [call(): pl.pallas_call(kernel, out_shape=[shape_of(*out) for out in outs], grid_s...]
    unnamed x74 -> x70, local copies, waits for them, and re-layouts: 5.31 us -> 5.3 us
  transfers between devices with their start and end apart: 39 -> 43, of which waited for: 17 -> 22; matrix products, arithmetic and copies ran while one was open for 3% -> 3% of each run, Pallas kernels for 28% -> 28%
where the time goes in v5:
time: 210 us; the launch traced here: 209 us
  Pallas kernels  80.4 us (38%)
  waiting for transfers between devices  55.1 us (26%)
  starting transfers between devices  46.2 us (22%)
  other arithmetic  15.1 us (7%)
  local copies, waits for them, and re-layouts  6.54 us (3%)
  between operations  5.92 us (3%)
    pallas_call x6, Pallas kernels, call(): pl.pallas_call(kernel, out_shape=[shape_of(*out) for out in outs], grid_s...  80.4 us
    ppermute x42, waiting for transfers between devices, swap(): return lax.ppermute(values, AXES, pairs)  54.3 us
    ppermute x42, starting transfers between devices, swap(): return lax.ppermute(values, AXES, pairs)  43.1 us
    unnamed x70, local copies, waits for them, and re-layouts  5.3 us
  transfers between devices with their start and end apart: 43, of which 22 were waited for; matrix products, arithmetic and copies ran while one was open for 3% of the time, Pallas kernels for 28%

profile of v5, /device:TPU:0, one launch (start us, length us, event | category | flops | bytes accessed | tf_op | source)
XLA Modules:
  0.0 209.3 jit_solution(13041337930507443233)
XLA Ops:
  0.6 0.7 convert_bitcast_fusion.3
  1.4 1.0 convert.35
  2.4 4.1 %collective-permute-start.1 = (bf16[72,512]{1,0:T(8,128)(2,1)S(1)}, bf16[72,512]{1,0:T(8,128)(2,1)S(1)}, u32[]{:S(2)}, u32[]{:S(2)}) collective-permute-start(bf16[72,512]{1,0:T(8,128)(2,1)S(1)} %get-tuple-element.271), channel_id=1, source_target_pairs={{0,16},{1,17},{2,18},{3,19},{4,20},{5,21},{6,22},{7,23},{8,24},{9,... | collective-permute-start | bytes 221192 | tf_op jit(solution)/shard_map/ppermute | solution.py:686
  6.5 1.6 collective-permute-start
  8.1 0.9 convert_element_type.181
  9.0 0.9 convert_element_type.180
  10.0 0.9 collective-permute-done
  10.8 3.4 %collective-permute-done.2 = bf16[72,512]{1,0:T(8,128)(2,1)S(1)} collective-permute-done((bf16[72,512]{1,0:T(8,128)(2,1)S(1)}, bf16[72,512]{1,0:T(8,128)(2,1)S(1)}, u32[]{:S(2)}, u32[]{:S(2)}) %collective-permute-start.2) | collective-permute-done | bytes 73760 | tf_op jit(solution)/shard_map/ppermute | solution.py:686
  14.3 2.5 %collective-permute-start.8 = (bf16[4,72,512]{2,1,0:T(8,128)(2,1)S(1)}, bf16[4,72,512]{2,1,0:T(8,128)(2,1)S(1)}, u32[]{:S(2)}, u32[]{:S(2)}) collective-permute-start(bf16[4,72,512]{2,1,0:T(8,128)(2,1)S(1)} %pad_maximum_fusion.5), channel_id=1, source_target_pairs={{0,6},{1,7},{2,4},{3,5},{4,2},{5,3},{6,0},{7,1},{8,14},{9,15},{10,... | collective-permute-start | bytes 884744 | tf_op jit(solution)/shard_map/ppermute | solution.py:686
  17.8 1.6 collective-permute-start.5
  19.7 5.5 %collective-permute-done.8 = bf16[4,72,512]{2,1,0:T(8,128)(2,1)S(1)} collective-permute-done((bf16[4,72,512]{2,1,0:T(8,128)(2,1)S(1)}, bf16[4,72,512]{2,1,0:T(8,128)(2,1)S(1)}, u32[]{:S(2)}, u32[]{:S(2)}) %collective-permute-start.8) | collective-permute-done | bytes 294944 | tf_op jit(solution)/shard_map/ppermute | solution.py:686
  25.2 3.5 %collective-permute-done.7 = bf16[4,72,512]{2,1,0:T(8,128)(2,1)S(1)} collective-permute-done((bf16[4,72,512]{2,1,0:T(8,128)(2,1)S(1)}, bf16[4,72,512]{2,1,0:T(8,128)(2,1)S(1)}, u32[]{:S(2)}, u32[]{:S(2)}) %collective-permute-start.7) | collective-permute-done | bytes 294944 | tf_op jit(solution)/shard_map/ppermute | solution.py:686
  29.0 0.6 collective-permute-done.3
  29.6 1.1 collective-permute-start.13
  30.8 1.0 pad_maximum_fusion.6
  31.7 1.7 collective-permute-start.12
  33.4 1.3 collective-permute-start.11
  35.5 3.0 %collective-permute-start.14 = (bf16[2,128,512]{2,1,0:T(8,128)(2,1)S(1)}, bf16[2,128,512]{2,1,0:T(8,128)(2,1)S(1)}, u32[]{:S(2)}, u32[]{:S(2)}) collective-permute-start(bf16[2,128,512]{2,1,0:T(8,128)(2,1)S(1)} %pad_maximum_fusion.7), channel_id=1, source_target_pairs={{0,16},{1,17},{2,18},{3,19},{4,20},{5,21},{6,22},{7,23},{8,24},{9,... | collective-permute-start | bytes 786440 | tf_op jit(solution)/shard_map/ppermute | solution.py:686
  38.5 9.1 %self_forward.1 = (bf16[4,256,512]{2,1,0:T(8,128)(2,1)S(1)}, bf16[4,256,512]{2,1,0:T(8,128)(2,1)S(1)}, bf16[4,256,512]{2,1,0:T(8,128)(2,1)S(1)}, bf16[4,256,512]...) custom-call(s32[4]{0:T(128)S(1)} %copy-done.4, ...), custom_call_target="tpu_custom_call" | custom-call | flops 19800000512 | bytes 1048576 | tf_op jit(solution)/shard_map/self_forward/pallas_call | solution.py:502
  47.6 1.0 copy-done.9
  48.6 1.0 copy-done.11
  49.6 0.7 collective-permute-done.14
  50.6 2.1 collective-permute-start.18
  52.6 0.9 collective-permute-start.17
  54.1 12.2 %cross_forward.1 = (bf16[4,256,512]{2,1,0:T(8,128)(2,1)S(1)}, bf16[4,256,512]{2,1,0:T(8,128)(2,1)S(1)}, bf16[4,512,512]{2,1,0:T(8,128)(2,1)S(1)}, bf16[4,512,512...) custom-call(s32[4]{0:T(128)S(1)} %copy-done.3, ...), custom_call_target="tpu_custom_call" | custom-call | flops 26400000000 | bytes 1048576 | tf_op jit(solution)/shard_map/cross_forward/pallas_call | solution.py:502
  66.4 10.6 %collective-permute-done.17 = bf16[4,128,512]{2,1,0:T(8,128)(2,1)S(1)} collective-permute-done((bf16[4,128,512]{2,1,0:T(8,128)(2,1)S(1)}, bf16[4,128,512]{2,1,0:T(8,128)(2,1)S(1)}, u32[]{:S(2)}, u32[]{:S(2)}) %collective-permute-start.17) | collective-permute-done | bytes 524320 | tf_op jit(solution)/shard_map/ppermute | solution.py:686
  77.5 4.1 %collective-permute-done.19.refs_1_.refs_3_ = bf16[4,4,128,512]{3,2,1,0:T(8,128)(2,1)S(1)} collective-permute-done((bf16[4,4,128,512]{3,2,1,0:T(8,128)(2,1)S(1)}, bf16[4,4,128,512]{3,2,1,0:T(8,128)(2,1)S(1)}, u32[]{:S(2)}, u32[]{:S(2)}) %collective-permute-start.19) | collective-permute-done | bytes 2097184 | tf_op jit(solution)/shard_map/ppermute | solution.py:686
  81.6 21.2 %ffn.1 = (f32[4,256,512]{2,1,0:T(8,128)}, f32[4,256,512]{2,1,0:T(8,128)S(1)}, f32[16,512]{1,0:T(8,128)S(1)}, bf16[4,4,64,512]{3,2,1,0:T(8,128)(2,1)S(1)}, bf16[4...) custom-call(s32[4]{0:T(128)S(1)} %copy-done.4, ...), custom_call_target="tpu_custom_call" | custom-call | flops 26400000000 | bytes 1048576 | tf_op jit(solution)/shard_map/ffn/pallas_call | solution.py:502
  103.4 2.1 %collective-permute-done.20 = bf16[4,4,64,512]{3,2,1,0:T(8,128)(2,1)S(1)} collective-permute-done((bf16[4,4,64,512]{3,2,1,0:T(8,128)(2,1)S(1)}, bf16[4,4,64,512]{3,2,1,0:T(8,128)(2,1)S(1)}, u32[]{:S(2)}, u32[]{:S(2)}) %collective-permute-start.20) | collective-permute-done | bytes 1048608 | tf_op jit(solution)/shard_map/ppermute | solution.py:686
  105.9 1.2 collective-permute-done.21
  108.4 1.8 collective-permute-start.24
  110.2 1.2 collective-permute-start.23
  111.9 19.3 %cross_back.1 = (f32[4,256,512]{2,1,0:T(8,128)S(1)}, bf16[4,512,512]{2,1,0:T(8,128)(2,1)S(1)}, bf16[4,512,512]{2,1,0:T(8,128)(2,1)S(1)}, f32[8,512]{1,0:T(8,128)...) custom-call(s32[4]{0:T(128)S(1)} %copy-done.3, s32[3]{0:T(128)S(1)} %pad_add_fusion.place_ref, ...), custom_call_target="tpu_custom_call" | custom-call | flops 32999999488 | bytes 1048576 | tf_op jit(solution)/shard_map/cross_back/pallas_call | solution.py:502
  131.3 3.2 %collective-permute-done.23 = bf16[4,128,512]{2,1,0:T(8,128)(2,1)S(1)} collective-permute-done((bf16[4,128,512]{2,1,0:T(8,128)(2,1)S(1)}, bf16[4,128,512]{2,1,0:T(8,128)(2,1)S(1)}, u32[]{:S(2)}, u32[]{:S(2)}) %collective-permute-start.23) | collective-permute-done | bytes 524320 | tf_op jit(solution)/shard_map/ppermute | solution.py:686
  134.9 2.2 %collective-permute-done.25 = bf16[4,4,64,512]{3,2,1,0:T(8,128)(2,1)S(1)} collective-permute-done((bf16[4,4,64,512]{3,2,1,0:T(8,128)(2,1)S(1)}, bf16[4,4,64,512]{3,2,1,0:T(8,128)(2,1)S(1)}, u32[]{:S(2)}, u32[]{:S(2)}) %collective-permute-start.25) | collective-permute-done | bytes 1048608 | tf_op jit(solution)/shard_map/ppermute | solution.py:686
  138.0 1.7 collective-permute-start.28
  139.7 1.3 collective-permute-start.27
  141.6 14.4 %self_back.1 = (f32[4,256,512]{2,1,0:T(8,128)}, f32[24,512]{1,0:T(8,128)}, bf16[4,4,64,512]{3,2,1,0:T(8,128)(2,1)S(1)}, bf16[4,4,64,512]{3,2,1,0:T(8,128)(2,1)S(1)}, f32[2,4,4,8,256]{4,3,2,1,0:T(8,128)S(1)}) custom-call(s32[4]{0:T(128)S(1)} %copy-done.4, s32[3]{0:T(128)S(1)} %pad_add_fusion.place_ref, f32[4,256,512]{2,1,0:T(8,128)S(1)} %get-tuple-element.191.grad_ref, ...), custom_call_target="tpu_custom_call" | custom-call | flops 24199999488 | bytes 1048576 | tf_op jit(solution)/shard_map/self_back/pallas_call | solution.py:502
  156.9 2.0 collective-permute-done.31
  159.6 3.0 %collective-permute-start.35 = (bf16[1,128,512]{2,1,0:T(8,128)(2,1)S(1)}, bf16[1,128,512]{2,1,0:T(8,128)(2,1)S(1)}, u32[]{:S(2)}, u32[]{:S(2)}) collective-permute-start(bf16[1,128,512]{2,1,0:T(8,128)(2,1)S(1)} %bitcast.168), channel_id=1, source_target_pairs={{0,16},{1,17},{2,18},{3,19},{4,20},{5,21},{6,22},{7,23},{8,24},{9,... | collective-permute-start | bytes 393224 | tf_op jit(solution)/shard_map/ppermute | solution.py:686
  162.8 1.6 collective-permute-start.36
  164.4 1.4 collective-permute-start.38
  166.4 1.3 collective-permute-start.34
  167.7 2.0 collective-permute-done.35
  169.7 3.0 %collective-permute-done.36 = bf16[4,72,512]{2,1,0:T(8,128)(2,1)S(1)} collective-permute-done((bf16[4,72,512]{2,1,0:T(8,128)(2,1)S(1)}, bf16[4,72,512]{2,1,0:T(8,128)(2,1)S(1)}, u32[]{:S(2)}, u32[]{:S(2)}) %collective-permute-start.36) | collective-permute-done | bytes 294944 | tf_op jit(solution)/shard_map/ppermute | solution.py:686
  173.4 5.6 %collective-permute-done.38 = bf16[4,72,512]{2,1,0:T(8,128)(2,1)S(1)} collective-permute-done((bf16[4,72,512]{2,1,0:T(8,128)(2,1)S(1)}, bf16[4,72,512]{2,1,0:T(8,128)(2,1)S(1)}, u32[]{:S(2)}, u32[]{:S(2)}) %collective-permute-start.38) | collective-permute-done | bytes 294944 | tf_op jit(solution)/shard_map/ppermute | solution.py:686
  179.0 1.4 collective-permute-done.37
  180.7 1.7 collective-permute-start.41
  182.4 1.7 collective-permute-start.40
  184.1 0.6 multiply_reduce_fusion.2
  184.8 0.7 multiply_reduce_fusion
  187.0 1.8 collective-permute-done.40
  188.9 0.6 fusion.19
  191.4 0.7 broadcast_in_dim.3
  192.1 3.1 %all-to-all-start = ((f32[32,8,128]{2,1,0:T(8,128)}), f32[32,8,128]{2,1,0:T(8,128)S(1)}, u32[]{:S(2)}, u32[]{:S(2)}) async-start(f32[32,8,128]{2,1,0:T(8,128)} %broadcast_in_dim.3), calls=%async_computation | async-start | bytes 262144 | tf_op jit(solution)/shard_map/all_to_all | solution.py:888
  195.2 1.6 copy-done.6
  196.8 1.6 copy-done.8
  198.4 4.2 %memory_grad.1 = f32[4,512,512]{2,1,0:T(8,128)} custom-call(bf16[4,512,512]{2,1,0:T(8,128)(2,1)S(1)} %copy-done.6, bf16[4,512,512]{2,1,0:T(8,128)(2,1)S(1)} %copy-done.8, bf16[4,512,512]{2,1,0:T(8,128)(2,1)S(1)} %get-tuple-element.176.w_ref), custom_call_target="tpu_custom_call" | custom-call | flops 4400000000 | bytes 1048576 | tf_op jit(solution)/shard_map/memory_grad/pallas_call | solution.py:502
  202.6 0.8 all-to-all-done
  203.4 0.6 slice_reduce_fusion
  204.8 0.8 multiply_subtract_fusion.1
  205.7 0.6 multiply_subtract_fusion.3
  206.3 0.8 multiply_subtract_fusion.2
  207.1 1.0 multiply_subtract_fusion
  (160 shorter events, 12.5 us)
Async XLA Ops:
  2.3 26.6 %copy-start.26 = (bf16[4,16,512]{2,1,0:T(8,128)(2,1)}, bf16[4,16,512]{2,1,0:T(8,128)(2,1)S(1)}, u32[]{:S(2)}) copy-start(bf16[4,16,512]{2,1,0:T(8,128)(2,1)S(1)} %get-tuple-element.269) | copy-start | bytes 196612
  2.4 7.6 %collective-permute-start.1 = (bf16[72,512]{1,0:T(8,128)(2,1)S(1)}, bf16[72,512]{1,0:T(8,128)(2,1)S(1)}, u32[]{:S(2)}, u32[]{:S(2)}) collective-permute-start(bf16[72,512]{1,0:T(8,128)(2,1)S(1)} %get-tuple-element.271), channel_id=1, source_target_pairs={{0,16},{1,17},{2,18},{3,19},{4,20},{5,21},{6,22},{7,23},{8,24},{9,... | collective-permute-start | bytes 221192 | tf_op jit(solution)/shard_map/ppermute | solution.py:686
  6.5 4.4 %collective-permute-start = (bf16[72,512]{1,0:T(8,128)(2,1)S(1)}, bf16[72,512]{1,0:T(8,128)(2,1)S(1)}, u32[]{:S(2)}, u32[]{:S(2)}) collective-permute-start(bf16[72,512]{1,0:T(8,128)(2,1)S(1)} %get-tuple-element.271), channel_id=1, source_target_pairs={{0,8},{1,9},{2,10},{3,11},{4,12},{5,13},{6,14},{7,15},{8,0},{9,1},... | collective-permute-start | bytes 221192 | tf_op jit(solution)/shard_map/ppermute | solution.py:686
  8.1 6.2 %collective-permute-start.2 = (bf16[72,512]{1,0:T(8,128)(2,1)S(1)}, bf16[72,512]{1,0:T(8,128)(2,1)S(1)}, u32[]{:S(2)}, u32[]{:S(2)}) collective-permute-start(bf16[72,512]{1,0:T(8,128)(2,1)S(1)} %get-tuple-element.271), channel_id=1, source_target_pairs={{0,24},{1,25},{2,26},{3,27},{4,28},{5,29},{6,30},{7,31},{8,16},{9,... | collective-permute-start | bytes 221192 | tf_op jit(solution)/shard_map/ppermute | solution.py:686
  9.9 28.6 %copy-start.2 = (bf16[4,256,512]{2,1,0:T(8,128)(2,1)S(1)}, bf16[4,256,512]{2,1,0:T(8,128)(2,1)}, u32[]{:S(2)}) copy-start(bf16[4,256,512]{2,1,0:T(8,128)(2,1)} %x_ref.3) | copy-start | bytes 3145732
  9.9 28.6 %copy-start.4 = (s32[4]{0:T(128)S(1)}, s32[4]{0:T(128)}, u32[]{:S(2)}) copy-start(s32[4]{0:T(128)} %count_ref.9) | copy-start | bytes 52
  14.3 11.0 %collective-permute-start.8 = (bf16[4,72,512]{2,1,0:T(8,128)(2,1)S(1)}, bf16[4,72,512]{2,1,0:T(8,128)(2,1)S(1)}, u32[]{:S(2)}, u32[]{:S(2)}) collective-permute-start(bf16[4,72,512]{2,1,0:T(8,128)(2,1)S(1)} %pad_maximum_fusion.5), channel_id=1, source_target_pairs={{0,6},{1,7},{2,4},{3,5},{4,2},{5,3},{6,0},{7,1},{8,14},{9,15},{10,... | collective-permute-start | bytes 884744 | tf_op jit(solution)/shard_map/ppermute | solution.py:686
  16.8 11.9 %collective-permute-start.7 = (bf16[4,72,512]{2,1,0:T(8,128)(2,1)S(1)}, bf16[4,72,512]{2,1,0:T(8,128)(2,1)S(1)}, u32[]{:S(2)}, u32[]{:S(2)}) collective-permute-start(bf16[4,72,512]{2,1,0:T(8,128)(2,1)S(1)} %pad_maximum_fusion.5), channel_id=1, source_target_pairs={{0,4},{1,5},{2,6},{3,7},{4,0},{5,1},{6,2},{7,3},{8,12},{9,13},{10,... | collective-permute-start | bytes 884744 | tf_op jit(solution)/shard_map/ppermute | solution.py:686
  17.3 11.5 %collective-permute-start.6 = (bf16[4,72,512]{2,1,0:T(8,128)(2,1)S(1)}, bf16[4,72,512]{2,1,0:T(8,128)(2,1)S(1)}, u32[]{:S(2)}, u32[]{:S(2)}) collective-permute-start(bf16[4,72,512]{2,1,0:T(8,128)(2,1)S(1)} %pad_maximum_fusion.5), channel_id=1, source_target_pairs={{0,2},{1,3},{2,0},{3,1},{4,6},{5,7},{6,4},{7,5},{8,10},{9,11},{10,... | collective-permute-start | bytes 884744 | tf_op jit(solution)/shard_map/ppermute | solution.py:686
  17.8 11.1 %collective-permute-start.5 = (bf16[64,512]{1,0:T(8,128)(2,1)S(1)}, bf16[64,512]{1,0:T(8,128)(2,1)}, u32[]{:S(2)}, u32[]{:S(2)}) collective-permute-start(bf16[64,512]{1,0:T(8,128)(2,1)S(1)} %bitcast.161), channel_id=1, source_target_pairs={{0,24},{1,25},{2,26},{3,27},{4,28},{5,29},{6,30},{7,31},{8,16},{9,... | collective-permute-start | bytes 196616 | tf_op jit(solution)/shard_map/ppermute | solution.py:686
  19.5 9.5 %collective-permute-start.4 = (bf16[64,512]{1,0:T(8,128)(2,1)S(1)}, bf16[64,512]{1,0:T(8,128)(2,1)}, u32[]{:S(2)}, u32[]{:S(2)}) collective-permute-start(bf16[64,512]{1,0:T(8,128)(2,1)S(1)} %bitcast.162), channel_id=1, source_target_pairs={{0,16},{1,17},{2,18},{3,19},{4,20},{5,21},{6,22},{7,23},{8,24},{9,... | collective-permute-start | bytes 196616 | tf_op jit(solution)/shard_map/ppermute | solution.py:686
  25.2 4.4 %collective-permute-start.3 = (bf16[64,512]{1,0:T(8,128)(2,1)S(1)}, bf16[64,512]{1,0:T(8,128)(2,1)}, u32[]{:S(2)}, u32[]{:S(2)}) collective-permute-start(bf16[64,512]{1,0:T(8,128)(2,1)S(1)} %bitcast.163), channel_id=1, source_target_pairs={{0,8},{1,9},{2,10},{3,11},{4,12},{5,13},{6,14},{7,15},{8,0},{9,1},... | collective-permute-start | bytes 196616 | tf_op jit(solution)/shard_map/ppermute | solution.py:686
  29.6 8.9 %collective-permute-start.9 = (bf16[4,4,72,512]{3,2,1,0:T(8,128)(2,1)S(1)}, bf16[4,4,72,512]{3,2,1,0:T(8,128)(2,1)S(1)}, u32[]{:S(2)}, u32[]{:S(2)}) collective-permute-start(bf16[4,4,72,512]{3,2,1,0:T(8,128)(2,1)S(1)} %pad_maximum_fusion.2.refs_0_), channel_id=1, source_target_pairs={{0,1},{1,0},{2,3},{3,2},{4,5},{5,4},{6,7},{7,6},{8,9},{9,8},{10,11... | collective-permute-start | bytes 3538952 | tf_op jit(solution)/shard_map/ppermute | solution.py:686
  29.6 5.9 %collective-permute-start.13 = (bf16[128,512]{1,0:T(8,128)(2,1)S(1)}, bf16[128,512]{1,0:T(8,128)(2,1)S(1)}, u32[]{:S(2)}, u32[]{:S(2)}) collective-permute-start(bf16[128,512]{1,0:T(8,128)(2,1)S(1)} %pad_maximum_fusion.9), channel_id=1, source_target_pairs={{0,8},{1,9},{2,10},{3,11},{4,12},{5,13},{6,14},{7,15},{8,0},{9,1},... | collective-permute-start | bytes 393224 | tf_op jit(solution)/shard_map/ppermute | solution.py:686
  31.7 18.5 %collective-permute-start.12 = (bf16[4,64,512]{2,1,0:T(8,128)(2,1)S(1)}, bf16[4,64,512]{2,1,0:T(8,128)(2,1)S(1)}, u32[]{:S(2)}, u32[]{:S(2)}) collective-permute-start(bf16[4,64,512]{2,1,0:T(8,128)(2,1)S(1)} %pad_maximum_fusion.6), channel_id=1, source_target_pairs={{0,6},{1,7},{2,4},{3,5},{4,2},{5,3},{6,0},{7,1},{8,14},{9,15},{10,... | collective-permute-start | bytes 786440 | tf_op jit(solution)/shard_map/ppermute | solution.py:686
  33.4 16.8 %collective-permute-start.11 = (bf16[4,64,512]{2,1,0:T(8,128)(2,1)S(1)}, bf16[4,64,512]{2,1,0:T(8,128)(2,1)S(1)}, u32[]{:S(2)}, u32[]{:S(2)}) collective-permute-start(bf16[4,64,512]{2,1,0:T(8,128)(2,1)S(1)} %pad_maximum_fusion.6), channel_id=1, source_target_pairs={{0,4},{1,5},{2,6},{3,7},{4,0},{5,1},{6,2},{7,3},{8,12},{9,13},{10,... | collective-permute-start | bytes 786440 | tf_op jit(solution)/shard_map/ppermute | solution.py:686
  34.7 15.5 %collective-permute-start.10 = (bf16[4,64,512]{2,1,0:T(8,128)(2,1)S(1)}, bf16[4,64,512]{2,1,0:T(8,128)(2,1)S(1)}, u32[]{:S(2)}, u32[]{:S(2)}) collective-permute-start(bf16[4,64,512]{2,1,0:T(8,128)(2,1)S(1)} %pad_maximum_fusion.6), channel_id=1, source_target_pairs={{0,2},{1,3},{2,0},{3,1},{4,6},{5,7},{6,4},{7,5},{8,10},{9,11},{10,... | collective-permute-start | bytes 786440 | tf_op jit(solution)/shard_map/ppermute | solution.py:686
  35.5 14.7 %collective-permute-start.14 = (bf16[2,128,512]{2,1,0:T(8,128)(2,1)S(1)}, bf16[2,128,512]{2,1,0:T(8,128)(2,1)S(1)}, u32[]{:S(2)}, u32[]{:S(2)}) collective-permute-start(bf16[2,128,512]{2,1,0:T(8,128)(2,1)S(1)} %pad_maximum_fusion.7), channel_id=1, source_target_pairs={{0,16},{1,17},{2,18},{3,19},{4,20},{5,21},{6,22},{7,23},{8,24},{9,... | collective-permute-start | bytes 786440 | tf_op jit(solution)/shard_map/ppermute | solution.py:686
  49.6 16.8 %copy-start.13 = (bf16[4,256,512]{2,1,0:T(8,128)(2,1)}, bf16[4,256,512]{2,1,0:T(8,128)(2,1)S(1)}, u32[]{:S(2)}) copy-start(bf16[4,256,512]{2,1,0:T(8,128)(2,1)S(1)} %get-tuple-element.196.mixed_ref) | copy-start | bytes 3145732
  49.6 4.5 %copy-start = (bf16[4,512,512]{2,1,0:T(8,128)(2,1)S(1)}, bf16[4,512,512]{2,1,0:T(8,128)(2,1)}, u32[]{:S(2)}) copy-start(bf16[4,512,512]{2,1,0:T(8,128)(2,1)} %mem_ref.3) | copy-start | bytes 6291460
  49.6 4.5 %copy-start.3 = (s32[4]{0:T(128)S(1)}, s32[4]{0:T(128)}, u32[]{:S(2)}) copy-start(s32[4]{0:T(128)} %count_ref.8) | copy-start | bytes 52
  50.4 3.7 %collective-permute-start.15 = (bf16[4,4,64,512]{3,2,1,0:T(8,128)(2,1)S(1)}, bf16[4,4,64,512]{3,2,1,0:T(8,128)(2,1)S(1)}, u32[]{:S(2)}, u32[]{:S(2)}) collective-permute-start(bf16[4,4,64,512]{3,2,1,0:T(8,128)(2,1)S(1)} %pad_maximum_fusion.3.refs_0_), channel_id=1, source_target_pairs={{0,1},{1,0},{2,3},{3,2},{4,5},{5,4},{6,7},{7,6},{8,9},{9,8},{10,11... | collective-permute-start | bytes 3145736 | tf_op jit(solution)/shard_map/ppermute | solution.py:686
  50.6 15.9 %collective-permute-start.18 = (bf16[4,128,512]{2,1,0:T(8,128)(2,1)S(1)}, bf16[4,128,512]{2,1,0:T(8,128)(2,1)S(1)}, u32[]{:S(2)}, u32[]{:S(2)}) collective-permute-start(bf16[4,128,512]{2,1,0:T(8,128)(2,1)S(1)} %pad_maximum_fusion.4), channel_id=1, source_target_pairs={{0,6},{1,7},{2,4},{3,5},{4,2},{5,3},{6,0},{7,1},{8,14},{9,15},{10,... | collective-permute-start | bytes 1572872 | tf_op jit(solution)/shard_map/ppermute | solution.py:686
  52.6 24.4 %collective-permute-start.17 = (bf16[4,128,512]{2,1,0:T(8,128)(2,1)S(1)}, bf16[4,128,512]{2,1,0:T(8,128)(2,1)S(1)}, u32[]{:S(2)}, u32[]{:S(2)}) collective-permute-start(bf16[4,128,512]{2,1,0:T(8,128)(2,1)S(1)} %pad_maximum_fusion.4), channel_id=1, source_target_pairs={{0,4},{1,5},{2,6},{3,7},{4,0},{5,1},{6,2},{7,3},{8,12},{9,13},{10,... | collective-permute-start | bytes 1572872 | tf_op jit(solution)/shard_map/ppermute | solution.py:686
  53.6 23.5 %collective-permute-start.16 = (bf16[4,128,512]{2,1,0:T(8,128)(2,1)S(1)}, bf16[4,128,512]{2,1,0:T(8,128)(2,1)S(1)}, u32[]{:S(2)}, u32[]{:S(2)}) collective-permute-start(bf16[4,128,512]{2,1,0:T(8,128)(2,1)S(1)} %pad_maximum_fusion.4), channel_id=1, source_target_pairs={{0,2},{1,3},{2,0},{3,1},{4,6},{5,7},{6,4},{7,5},{8,10},{9,11},{10,... | collective-permute-start | bytes 1572872 | tf_op jit(solution)/shard_map/ppermute | solution.py:686
  66.4 11.0 %copy-start.15 = (bf16[4,256,512]{2,1,0:T(8,128)(2,1)}, bf16[4,256,512]{2,1,0:T(8,128)(2,1)S(1)}, u32[]{:S(2)}) copy-start(bf16[4,256,512]{2,1,0:T(8,128)(2,1)S(1)} %get-tuple-element.170.act_ref) | copy-start | bytes 3145732
  66.4 11.0 %copy-start.17 = (bf16[4,256,512]{2,1,0:T(8,128)(2,1)}, bf16[4,256,512]{2,1,0:T(8,128)(2,1)S(1)}, u32[]{:S(2)}) copy-start(bf16[4,256,512]{2,1,0:T(8,128)(2,1)S(1)} %get-tuple-element.171.query_ref) | copy-start | bytes 3145732
  66.4 11.0 %copy-start.19 = (bf16[4,256,512]{2,1,0:T(8,128)(2,1)}, bf16[4,256,512]{2,1,0:T(8,128)(2,1)S(1)}, u32[]{:S(2)}) copy-start(bf16[4,256,512]{2,1,0:T(8,128)(2,1)S(1)} %get-tuple-element.174.mixed_ref) | copy-start | bytes 3145732
  77.1 4.5 %copy-start.1 = (bf16[4,256,512]{2,1,0:T(8,128)(2,1)S(1)}, bf16[4,256,512]{2,1,0:T(8,128)(2,1)}, u32[]{:S(2)}) copy-start(bf16[4,256,512]{2,1,0:T(8,128)(2,1)} %cot_ref.1) | copy-start | bytes 3145732
  77.4 4.2 %collective-permute-start.19 = (bf16[4,4,128,512]{3,2,1,0:T(8,128)(2,1)S(1)}, bf16[4,4,128,512]{3,2,1,0:T(8,128)(2,1)S(1)}, u32[]{:S(2)}, u32[]{:S(2)}) collective-permute-start(bf16[4,4,128,512]{3,2,1,0:T(8,128)(2,1)S(1)} %pad_maximum_fusion.1.refs_0_.refs_2_), channel_id=1, source_target_pairs={{0,1},{1,0},{2,3},{3,2},{4,5},{5,4},{6,7},{7,6},{8,9},{9,8},{10,11... | collective-permute-start | bytes 6291464 | tf_op jit(solution)/shard_map/ppermute | solution.py:686
  102.8 2.7 %collective-permute-start.20 = (bf16[4,4,64,512]{3,2,1,0:T(8,128)(2,1)S(1)}, bf16[4,4,64,512]{3,2,1,0:T(8,128)(2,1)S(1)}, u32[]{:S(2)}, u32[]{:S(2)}) collective-permute-start(bf16[4,4,64,512]{3,2,1,0:T(8,128)(2,1)S(1)} %get-tuple-element.166), channel_id=1, source_target_pairs={{0,1},{1,0},{2,3},{3,2},{4,5},{5,4},{6,7},{7,6},{8,9},{9,8},{10,11... | collective-permute-start | bytes 3145736 | tf_op jit(solution)/shard_map/ppermute | solution.py:686
  103.0 4.0 %collective-permute-start.21 = (bf16[4,4,64,512]{3,2,1,0:T(8,128)(2,1)S(1)}, bf16[4,4,64,512]{3,2,1,0:T(8,128)(2,1)S(1)}, u32[]{:S(2)}, u32[]{:S(2)}) collective-permute-start(bf16[4,4,64,512]{3,2,1,0:T(8,128)(2,1)S(1)} %get-tuple-element.168), channel_id=1, source_target_pairs={{0,1},{1,0},{2,3},{3,2},{4,5},{5,4},{6,7},{7,6},{8,9},{9,8},{10,11... | collective-permute-start | bytes 3145736 | tf_op jit(solution)/shard_map/ppermute | solution.py:686
  108.4 22.9 %collective-permute-start.24 = (bf16[4,128,512]{2,1,0:T(8,128)(2,1)S(1)}, bf16[4,128,512]{2,1,0:T(8,128)(2,1)S(1)}, u32[]{:S(2)}, u32[]{:S(2)}) collective-permute-start(bf16[4,128,512]{2,1,0:T(8,128)(2,1)S(1)} %get-tuple-element.246), channel_id=1, source_target_pairs={{0,6},{1,7},{2,4},{3,5},{4,2},{5,3},{6,0},{7,1},{8,14},{9,15},{10,... | collective-permute-start | bytes 1572872 | tf_op jit(solution)/shard_map/ppermute | solution.py:686
  110.2 24.4 %collective-permute-start.23 = (bf16[4,128,512]{2,1,0:T(8,128)(2,1)S(1)}, bf16[4,128,512]{2,1,0:T(8,128)(2,1)S(1)}, u32[]{:S(2)}, u32[]{:S(2)}) collective-permute-start(bf16[4,128,512]{2,1,0:T(8,128)(2,1)S(1)} %get-tuple-element.247), channel_id=1, source_target_pairs={{0,4},{1,5},{2,6},{3,7},{4,0},{5,1},{6,2},{7,3},{8,12},{9,13},{10,... | collective-permute-start | bytes 1572872 | tf_op jit(solution)/shard_map/ppermute | solution.py:686
  111.4 23.2 %collective-permute-start.22 = (bf16[4,128,512]{2,1,0:T(8,128)(2,1)S(1)}, bf16[4,128,512]{2,1,0:T(8,128)(2,1)S(1)}, u32[]{:S(2)}, u32[]{:S(2)}) collective-permute-start(bf16[4,128,512]{2,1,0:T(8,128)(2,1)S(1)} %get-tuple-element.248), channel_id=1, source_target_pairs={{0,2},{1,3},{2,0},{3,1},{4,6},{5,7},{6,4},{7,5},{8,10},{9,11},{10,... | collective-permute-start | bytes 1572872 | tf_op jit(solution)/shard_map/ppermute | solution.py:686
  134.5 2.7 %collective-permute-start.25 = (bf16[4,4,64,512]{3,2,1,0:T(8,128)(2,1)S(1)}, bf16[4,4,64,512]{3,2,1,0:T(8,128)(2,1)S(1)}, u32[]{:S(2)}, u32[]{:S(2)}) collective-permute-start(bf16[4,4,64,512]{3,2,1,0:T(8,128)(2,1)S(1)} %get-tuple-element.186), channel_id=1, source_target_pairs={{0,1},{1,0},{2,3},{3,2},{4,5},{5,4},{6,7},{7,6},{8,9},{9,8},{10,11... | collective-permute-start | bytes 3145736 | tf_op jit(solution)/shard_map/ppermute | solution.py:686
  137.5 4.0 %copy-start.10 = (bf16[4,256,512]{2,1,0:T(8,128)(2,1)S(1)}, bf16[4,256,512]{2,1,0:T(8,128)(2,1)}, u32[]{:S(2)}) copy-start(bf16[4,256,512]{2,1,0:T(8,128)(2,1)} %copy-done.9) | copy-start | bytes 3145732
  137.5 4.0 %copy-start.12 = (bf16[4,256,512]{2,1,0:T(8,128)(2,1)S(1)}, bf16[4,256,512]{2,1,0:T(8,128)(2,1)}, u32[]{:S(2)}) copy-start(bf16[4,256,512]{2,1,0:T(8,128)(2,1)} %copy-done.11) | copy-start | bytes 3145732
  137.6 18.4 %collective-permute-start.29 = (bf16[2,128,512]{2,1,0:T(8,128)(2,1)S(1)}, bf16[2,128,512]{2,1,0:T(8,128)(2,1)S(1)}, u32[]{:S(2)}, u32[]{:S(2)}) collective-permute-start(bf16[2,128,512]{2,1,0:T(8,128)(2,1)S(1)} %pad_maximum_fusion.8), channel_id=1, source_target_pairs={{0,8},{1,9},{2,10},{3,11},{4,12},{5,13},{6,14},{7,15},{8,0},{9,1},... | collective-permute-start | bytes 786440 | tf_op jit(solution)/shard_map/ppermute | solution.py:686
  138.0 18.0 %collective-permute-start.28 = (bf16[4,64,512]{2,1,0:T(8,128)(2,1)S(1)}, bf16[4,64,512]{2,1,0:T(8,128)(2,1)S(1)}, u32[]{:S(2)}, u32[]{:S(2)}) collective-permute-start(bf16[4,64,512]{2,1,0:T(8,128)(2,1)S(1)} %get-tuple-element.252), channel_id=1, source_target_pairs={{0,6},{1,7},{2,4},{3,5},{4,2},{5,3},{6,0},{7,1},{8,14},{9,15},{10,... | collective-permute-start | bytes 786440 | tf_op jit(solution)/shard_map/ppermute | solution.py:686
  139.7 16.3 %collective-permute-start.27 = (bf16[4,64,512]{2,1,0:T(8,128)(2,1)S(1)}, bf16[4,64,512]{2,1,0:T(8,128)(2,1)S(1)}, u32[]{:S(2)}, u32[]{:S(2)}) collective-permute-start(bf16[4,64,512]{2,1,0:T(8,128)(2,1)S(1)} %get-tuple-element.253), channel_id=1, source_target_pairs={{0,4},{1,5},{2,6},{3,7},{4,0},{5,1},{6,2},{7,3},{8,12},{9,13},{10,... | collective-permute-start | bytes 786440 | tf_op jit(solution)/shard_map/ppermute | solution.py:686
  141.0 15.0 %collective-permute-start.26 = (bf16[4,64,512]{2,1,0:T(8,128)(2,1)S(1)}, bf16[4,64,512]{2,1,0:T(8,128)(2,1)S(1)}, u32[]{:S(2)}, u32[]{:S(2)}) collective-permute-start(bf16[4,64,512]{2,1,0:T(8,128)(2,1)S(1)} %get-tuple-element.254), channel_id=1, source_target_pairs={{0,2},{1,3},{2,0},{3,1},{4,6},{5,7},{6,4},{7,5},{8,10},{9,11},{10,... | collective-permute-start | bytes 786440 | tf_op jit(solution)/shard_map/ppermute | solution.py:686
  156.0 2.8 %collective-permute-start.30 = (bf16[4,4,64,512]{3,2,1,0:T(8,128)(2,1)S(1)}, bf16[4,4,64,512]{3,2,1,0:T(8,128)(2,1)S(1)}, u32[]{:S(2)}, u32[]{:S(2)}) collective-permute-start(bf16[4,4,64,512]{3,2,1,0:T(8,128)(2,1)S(1)} %get-tuple-element.211), channel_id=1, source_target_pairs={{0,1},{1,0},{2,3},{3,2},{4,5},{5,4},{6,7},{7,6},{8,9},{9,8},{10,11... | collective-permute-start | bytes 3145736 | tf_op jit(solution)/shard_map/ppermute | solution.py:686
  156.1 2.7 %collective-permute-start.31 = (bf16[4,4,8,256]{3,2,1,0:T(8,128)(2,1)S(1)}, bf16[4,4,8,256]{3,2,1,0:T(8,128)(2,1)S(1)}, u32[]{:S(2)}, u32[]{:S(2)}) collective-permute-start(bf16[4,4,8,256]{3,2,1,0:T(8,128)(2,1)S(1)} %fusion.7), channel_id=1, source_target_pairs={{0,1},{1,0},{2,3},{3,2},{4,5},{5,4},{6,7},{7,6},{8,9},{9,8},{10,11... | collective-permute-start | bytes 196616 | tf_op jit(solution)/shard_map/ppermute | solution.py:686
  159.6 10.1 %collective-permute-start.35 = (bf16[1,128,512]{2,1,0:T(8,128)(2,1)S(1)}, bf16[1,128,512]{2,1,0:T(8,128)(2,1)S(1)}, u32[]{:S(2)}, u32[]{:S(2)}) collective-permute-start(bf16[1,128,512]{2,1,0:T(8,128)(2,1)S(1)} %bitcast.168), channel_id=1, source_target_pairs={{0,16},{1,17},{2,18},{3,19},{4,20},{5,21},{6,22},{7,23},{8,24},{9,... | collective-permute-start | bytes 393224 | tf_op jit(solution)/shard_map/ppermute | solution.py:686
  162.8 10.0 %collective-permute-start.36 = (bf16[4,72,512]{2,1,0:T(8,128)(2,1)S(1)}, bf16[4,72,512]{2,1,0:T(8,128)(2,1)S(1)}, u32[]{:S(2)}, u32[]{:S(2)}) collective-permute-start(bf16[4,72,512]{2,1,0:T(8,128)(2,1)S(1)} %get-tuple-element.249), channel_id=1, source_target_pairs={{0,2},{1,3},{2,0},{3,1},{4,6},{5,7},{6,4},{7,5},{8,10},{9,11},{10,... | collective-permute-start | bytes 884744 | tf_op jit(solution)/shard_map/ppermute | solution.py:686
  164.4 14.6 %collective-permute-start.38 = (bf16[4,72,512]{2,1,0:T(8,128)(2,1)S(1)}, bf16[4,72,512]{2,1,0:T(8,128)(2,1)S(1)}, u32[]{:S(2)}, u32[]{:S(2)}) collective-permute-start(bf16[4,72,512]{2,1,0:T(8,128)(2,1)S(1)} %get-tuple-element.250), channel_id=1, source_target_pairs={{0,6},{1,7},{2,4},{3,5},{4,2},{5,3},{6,0},{7,1},{8,14},{9,15},{10,... | collective-permute-start | bytes 884744 | tf_op jit(solution)/shard_map/ppermute | solution.py:686
  165.8 14.5 %collective-permute-start.37 = (bf16[4,72,512]{2,1,0:T(8,128)(2,1)S(1)}, bf16[4,72,512]{2,1,0:T(8,128)(2,1)S(1)}, u32[]{:S(2)}, u32[]{:S(2)}) collective-permute-start(bf16[4,72,512]{2,1,0:T(8,128)(2,1)S(1)} %get-tuple-element.251), channel_id=1, source_target_pairs={{0,4},{1,5},{2,6},{3,7},{4,0},{5,1},{6,2},{7,3},{8,12},{9,13},{10,... | collective-permute-start | bytes 884744 | tf_op jit(solution)/shard_map/ppermute | solution.py:686
  166.4 14.1 %collective-permute-start.34 = (bf16[64,512]{1,0:T(8,128)(2,1)S(1)}, bf16[64,512]{1,0:T(8,128)(2,1)S(1)}, u32[]{:S(2)}, u32[]{:S(2)}) collective-permute-start(bf16[64,512]{1,0:T(8,128)(2,1)S(1)} %get-tuple-element.263), channel_id=1, source_target_pairs={{0,24},{1,25},{2,26},{3,27},{4,28},{5,29},{6,30},{7,31},{8,16},{9,... | collective-permute-start | bytes 196616 | tf_op jit(solution)/shard_map/ppermute | solution.py:686
  169.7 10.8 %collective-permute-start.33 = (bf16[64,512]{1,0:T(8,128)(2,1)S(1)}, bf16[64,512]{1,0:T(8,128)(2,1)S(1)}, u32[]{:S(2)}, u32[]{:S(2)}) collective-permute-start(bf16[64,512]{1,0:T(8,128)(2,1)S(1)} %get-tuple-element.264), channel_id=1, source_target_pairs={{0,16},{1,17},{2,18},{3,19},{4,20},{5,21},{6,22},{7,23},{8,24},{9,... | collective-permute-start | bytes 196616 | tf_op jit(solution)/shard_map/ppermute | solution.py:686
  172.8 7.7 %collective-permute-start.32 = (bf16[64,512]{1,0:T(8,128)(2,1)S(1)}, bf16[64,512]{1,0:T(8,128)(2,1)S(1)}, u32[]{:S(2)}, u32[]{:S(2)}) collective-permute-start(bf16[64,512]{1,0:T(8,128)(2,1)S(1)} %get-tuple-element.265), channel_id=1, source_target_pairs={{0,8},{1,9},{2,10},{3,11},{4,12},{5,13},{6,14},{7,15},{8,0},{9,1},... | collective-permute-start | bytes 196616 | tf_op jit(solution)/shard_map/ppermute | solution.py:686
  180.6 6.2 %collective-permute-start.39 = (bf16[72,512]{1,0:T(8,128)(2,1)S(1)}, bf16[72,512]{1,0:T(8,128)(2,1)S(1)}, u32[]{:S(2)}, u32[]{:S(2)}) collective-permute-start(bf16[72,512]{1,0:T(8,128)(2,1)S(1)} %get-tuple-element.259), channel_id=1, source_target_pairs={{0,8},{1,9},{2,10},{3,11},{4,12},{5,13},{6,14},{7,15},{8,0},{9,1},... | collective-permute-start | bytes 221192 | tf_op jit(solution)/shard_map/ppermute | solution.py:686
  180.7 6.3 %collective-permute-start.41 = (bf16[72,512]{1,0:T(8,128)(2,1)S(1)}, bf16[72,512]{1,0:T(8,128)(2,1)S(1)}, u32[]{:S(2)}, u32[]{:S(2)}) collective-permute-start(bf16[72,512]{1,0:T(8,128)(2,1)S(1)} %get-tuple-element.260), channel_id=1, source_target_pairs={{0,24},{1,25},{2,26},{3,27},{4,28},{5,29},{6,30},{7,31},{8,16},{9,... | collective-permute-start | bytes 221192 | tf_op jit(solution)/shard_map/ppermute | solution.py:686
  182.4 6.4 %collective-permute-start.40 = (bf16[72,512]{1,0:T(8,128)(2,1)S(1)}, bf16[72,512]{1,0:T(8,128)(2,1)S(1)}, u32[]{:S(2)}, u32[]{:S(2)}) collective-permute-start(bf16[72,512]{1,0:T(8,128)(2,1)S(1)} %get-tuple-element.261), channel_id=1, source_target_pairs={{0,16},{1,17},{2,18},{3,19},{4,20},{5,21},{6,22},{7,23},{8,24},{9,... | collective-permute-start | bytes 221192 | tf_op jit(solution)/shard_map/ppermute | solution.py:686
  192.1 11.3 %all-to-all-start = ((f32[32,8,128]{2,1,0:T(8,128)}), f32[32,8,128]{2,1,0:T(8,128)S(1)}, u32[]{:S(2)}, u32[]{:S(2)}) async-start(f32[32,8,128]{2,1,0:T(8,128)} %broadcast_in_dim.3), calls=%async_computation | async-start | bytes 262144 | tf_op jit(solution)/shard_map/all_to_all | solution.py:888
  198.4 6.4 %copy-start.22 = (f32[64,512]{1,0:T(8,128)S(1)}, f32[64,512]{1,0:T(8,128)}, u32[]{:S(2)}) copy-start(f32[64,512]{1,0:T(8,128)} %param.24) | copy-start | bytes 393220
  198.4 6.4 %copy-start.27 = (f32[64,512]{1,0:T(8,128)S(1)}, f32[64,512]{1,0:T(8,128)}, u32[]{:S(2)}) copy-start(f32[64,512]{1,0:T(8,128)} %param.31) | copy-start | bytes 393220
  198.4 6.4 %copy-start.28 = (f32[64,512]{1,0:T(8,128)S(1)}, f32[64,512]{1,0:T(8,128)}, u32[]{:S(2)}) copy-start(f32[64,512]{1,0:T(8,128)} %param.30) | copy-start | bytes 393220
  198.4 7.3 %copy-start.31 = (f32[17,16]{0,1:T(8,128)S(1)}, f32[17,16]{0,1:T(8,128)}, u32[]{:S(2)}) copy-start(f32[17,16]{0,1:T(8,128)} %param.25) | copy-start | bytes 3268
  198.4 7.3 %copy-start.32 = (f32[17,16]{0,1:T(8,128)S(1)}, f32[17,16]{0,1:T(8,128)}, u32[]{:S(2)}) copy-start(f32[17,16]{0,1:T(8,128)} %param.33) | copy-start | bytes 3268
  198.4 7.3 %copy-start.33 = (f32[17,16]{0,1:T(8,128)S(1)}, f32[17,16]{0,1:T(8,128)}, u32[]{:S(2)}) copy-start(f32[17,16]{0,1:T(8,128)} %param.32) | copy-start | bytes 3268
  202.6 4.5 %copy-start.21 = (f32[8,16,512]{2,1,0:T(8,128)S(1)}, f32[8,16,512]{2,1,0:T(8,128)}, u32[]{:S(2)}) copy-start(f32[8,16,512]{2,1,0:T(8,128)} %param.22) | copy-start | bytes 786436
  202.6 4.5 %copy-start.24 = (f32[8,16,512]{2,1,0:T(8,128)S(1)}, f32[8,16,512]{2,1,0:T(8,128)}, u32[]{:S(2)}) copy-start(f32[8,16,512]{2,1,0:T(8,128)} %param.27) | copy-start | bytes 786436
  202.6 4.5 %copy-start.25 = (f32[8,16,512]{2,1,0:T(8,128)S(1)}, f32[8,16,512]{2,1,0:T(8,128)}, u32[]{:S(2)}) copy-start(f32[8,16,512]{2,1,0:T(8,128)} %param.26) | copy-start | bytes 786436
  (13 other events, 39.0 us)
